TPU v7x, 256 devices: a whole 4x4x8 slice. The times are simulated.
256 devices in a mesh: pole: 4 (over y), node: 64 (over z, x, core).
Axes of the slice: x: 4, y: 4, z: 8, core: 2. Of those that a mesh axis runs over, the one named last changes fastest.
Arguments:
- dens_part: bfloat16 [4, 262144, 338], P('pole', 'node'), may hold values from -1.5 to 1.5
- dest_node: int32 [262144], P('node'), may hold values from 0 to 63, as said below
- pair_slot: int32 [262144], P('node'), may hold values from 0 to 1023, as said below
- deriv: bfloat16 [262144, 1014], P(('pole', 'node')), may hold values from -0.119628906 to 0.119628906
- pair_atoms: int32 [2, 262144], P(None, ('pole', 'node')), may hold values from 0 to 32767
Outputs:
- forces: float32 [3, 32768], P(None, ('pole', 'node'))
Inputs may be any that keep to these rules, and one draw needn't show every extreme that they name: The share of block s is (s // 1024) % 4. Of the 1024 blocks of one share at most 32 have the same dest_node, and in every share exactly 32 do for some node index. Within one pole index, the number of blocks that a share on node n sends to node (n + k) % 64 depends on k alone. Every pair of pole index p and node index m receives exactly 1024 blocks of share p. `pair_slot`: the blocks of share p with dest_node m take each position of 0 to 1023 exactly once.
All inputs are finite; a program needn't handle non-finite values.
Results may differ from a plain program's by a relative error of at most 0.009.
Values may be sent and summed in bfloat16 or wider, within the bound.
No kernel may reach another device: no remote copies, remote signals or barrier semaphores. Data moves between devices by JAX's collectives and lax.ppermute only.
A program may use at most 64 MiB of HBM per device.

v0:
```python
import jax
import jax.numpy as jnp
from jax import lax
from jax.sharding import PartitionSpec as P

ATOM_DEV = 128


def body(dens_part, dest_node, pair_slot, deriv, pair_atoms):
    blocks_here = deriv.shape[0]
    width = dens_part.shape[2]
    half_width = width // 2
    nodes = lax.axis_size("node")
    poles = lax.axis_size("pole")
    pole_here = lax.axis_index("pole")
    capacity = 2 * blocks_here // nodes
    partials = dens_part[0]
    summed_all = lax.psum(partials, "pole").astype(jnp.float32)
    share_sum = lax.dynamic_slice_in_dim(summed_all, pole_here * blocks_here, blocks_here, 0)
    density = share_sum.astype(jnp.bfloat16)
    target_node = lax.dynamic_slice_in_dim(dest_node, pole_here * blocks_here, blocks_here, 0)
    target_slot = lax.dynamic_slice_in_dim(pair_slot, pole_here * blocks_here, blocks_here, 0)
    onehot = (target_node[:, None] == jnp.arange(nodes, dtype=jnp.int32)[None, :]).astype(jnp.int32)
    slot_rank = jnp.sum((jnp.cumsum(onehot, axis=0) - onehot) * onehot, axis=1)
    placement_row = target_node * capacity + slot_rank
    outgoing = jnp.zeros((nodes * capacity, width), jnp.bfloat16).at[placement_row].set(density)
    sent_slot = (
        jnp.full((nodes * capacity,), blocks_here, jnp.int32).at[placement_row].set(target_slot)
    )
    arrived, recv_slot = (
        lax.all_to_all(
            outgoing.reshape(nodes, capacity, width),
            "node",
            split_axis=0,
            concat_axis=0,
            tiled=True,
        ),
        lax.all_to_all(
            sent_slot.reshape(nodes, capacity), "node", split_axis=0, concat_axis=0, tiled=True
        ),
    )
    pair_dens = (
        jnp.zeros((blocks_here, width), jnp.bfloat16)
        .at[recv_slot.reshape(-1)]
        .set(arrived.reshape(-1, width), mode="drop")
    )
    grad_h = deriv[:, : 3 * half_width].reshape(blocks_here, 3, half_width)
    grad_s = deriv[:, 3 * half_width :].reshape(blocks_here, 3, half_width)
    first = jnp.einsum(
        "bk,bck->bc", pair_dens[:, :half_width], grad_h, preferred_element_type=jnp.float32
    )
    second = jnp.einsum(
        "bk,bck->bc", pair_dens[:, half_width:], grad_s, preferred_element_type=jnp.float32
    )
    pair_term = first - second
    atoms_total = ATOM_DEV * poles * nodes
    partial_forces = jnp.zeros((3, atoms_total), jnp.float32)
    partial_forces = partial_forces.at[:, pair_atoms[0]].add(-2.0 * pair_term.T)
    partial_forces = partial_forces.at[:, pair_atoms[1]].add(2.0 * pair_term.T)
    return lax.psum_scatter(partial_forces, ("pole", "node"), scatter_dimension=1, tiled=True)


def solution(mesh):
    return jax.shard_map(
        body,
        mesh=mesh,
        in_specs=(
            P("pole", "node", None),
            P("node"),
            P("node"),
            P(("pole", "node"), None),
            P(None, ("pole", "node")),
        ),
        out_specs=P(None, ("pole", "node")),
        check_vma=False,
    )
```

profile of v0, /device:TPU:1, one launch (start us, length us, event | category | flops | bytes accessed | tf_op | source)
XLA Modules:
  0.0 1484.8 jit_solution(2434604027894393543)
XLA Ops:
  6.5 0.0 copy-start.2
  6.5 0.0 all-reduce.2.cloned.1.call-start
  6.5 0.7 all-reduce.2.cloned.1.call-update
  7.3 0.0 dynamic-slice-start.1
  7.3 0.0 dynamic-slice-start
  7.3 0.0 copy-done.2
  7.3 18.0 %reduce-window.6 = s32[64,8,128]{2,1,0:T(8,128)S(1)} reduce-window(s32[64,8,128]{2,1,0:T(8,128)S(1)} %fusion.18, s32[]{:T(128)} %constant.13.clone.1), window={size=1x1x128 pad=0_0x0_0x127_0}, to_apply=%region_0.0 | reduce-window | flops 8323072 | bytes 524292 | tf_op jit(solution)/shard_map/reduce-window
  25.4 0.1 slice.32
  25.5 0.1 copy.11
  25.7 0.1 copy.12
  25.8 0.1 broadcast_add_fusion
  25.9 0.0 dynamic-slice-done.1
  25.9 0.1 fusion.15
  26.0 0.0 dynamic-slice-done
  26.0 4.3 scatter_custom_fusion
  30.3 0.7 all_to_all.9
  31.0 13.0 all-to-all-start
  44.0 45.1 %all-reduce.2.cloned.1.call-done = bf16[4096,338]{0,1:T(8,128)(2,1)} async-done(((bf16[4096,338]{0,1:T(8,128)(2,1)}), bf16[4096,338]{0,1:T(8,128)(2,1)}) %all-reduce.2.cloned.1.call-update) | async-done | bytes 2768912 | tf_op jit(solution)/shard_map/psum | solution.py:18
  89.2 1.1 convert_convert_fusion
  90.3 0.4 copy.14
  90.7 6.4 scatter_custom_fusion.1
  97.0 0.0 all-to-all-done
  97.0 10.8 all-to-all-start.1
  107.9 0.0 reduce-scatter.2.cloned.1.call-start
  107.9 1.9 fusion.23
  109.9 0.3 reshape.125
  110.1 2.5 copy.20
  112.7 0.3 reshape.124
  112.9 0.0 copy-start.3
  113.0 2.5 copy.17
  115.5 0.0 copy-done.3
  115.5 0.0 copy-start.1
  115.5 0.5 broadcast.99
  116.0 0.8 reduce.3
  116.9 0.1 reshape.121
  117.0 29.8 %all-to-all-done.1 = bf16[64,32,338]{2,1,0:T(8,128)(2,1)} async-done(((bf16[64,32,338]{2,1,0:T(8,128)(2,1)}), bf16[64,32,338]{2,1,0:T(8,128)(2,1)}, u32[]{:S(2)}, u32[]{:S(2)}) %all-to-all-start.1) | async-done | bytes 1384480 | tf_op jit(solution)/shard_map/all_to_all | solution.py:31
  146.8 10.1 scatter_custom_fusion.2
  156.9 0.3 slice_bitcast_fusion
  157.2 0.0 copy-done.1
  157.2 0.0 copy-start
  157.2 1.2 fusion.4
  158.5 0.4 copy-done
  158.8 1.2 fusion.2
  160.0 12.8 scatter_custom_fusion.3
  172.9 17.5 %scatter_custom_fusion.4 = f32[3,32768]{0,1:T(8,128)} fusion(f32[3,32768]{0,1:T(8,128)} %scatter_custom_fusion.3, s32[1024]{0:T(1024)S(1)} %bitcast.56, f32[]{:T(128)} %constant.11.clone.1, f32[1024,3]{1,0:T(8,128)S(1)} %bitcast.50, f32[1024,3]{1,0:T(8,128)S(1)} %bitcast.52), kind=kCustom, calls=%fused_computation.16 | custom fusion | flops 9216 | bytes 1442304 | tf_op jit(solution)/shard_map/scatter-add | solution.py:59
  190.4 0.0 reduce-scatter.2.cloned.1.call-update
  190.4 1286.1 %reduce-scatter.2.cloned.1.call-done = f32[3,128]{0,1:T(8,128)} async-done(((f32[3,32768]{0,1:T(8,128)}), f32[3,128]{0,1:T(8,128)}) %reduce-scatter.2.cloned.1.call-update) | async-done | bytes 1552 | tf_op jit(solution)/shard_map/reduce_scatter | solution.py:60
  1476.5 1.5 copy.15
  (7 shorter events, 0.1 us)
Async XLA Ops:
  6.5 0.8 copy-start.2
  6.5 82.6 %all-reduce.2.cloned.1.call-start = ((), (), s32[]{:S(2)}) async-start(), calls=%async_computation.3 | async-start | bytes 5636096 | tf_op jit(solution)/shard_map/psum | solution.py:18
  7.3 18.6 %dynamic-slice-start.1 = ((s32[4096]{0:T(1024)}, s32[]{:T(128)}), s32[1024]{0:T(1024)S(1)}, s32[]{:S(2)}) async-start(s32[4096]{0:T(1024)} %param.6, s32[]{:T(128)} %select_n.40), calls=%async_computation.6 | async-start | bytes 8704 | tf_op jit(solution)/shard_map/dynamic_slice | solution.py:21
  7.3 18.7 %dynamic-slice-start = ((s32[4096]{0:T(1024)}, s32[]{:T(128)}), s32[1024]{0:T(1024)S(1)}, s32[]{:S(2)}) async-start(s32[4096]{0:T(1024)} %param.7, s32[]{:T(128)} %select_n.40), calls=%async_computation.5 | async-start | bytes 8704 | tf_op jit(solution)/shard_map/dynamic_slice | solution.py:22
  31.0 66.0 %all-to-all-start = ((s32[64,1,32]{2,1,0:T(1,128)}), s32[64,1,32]{2,1,0:T(1,128)S(1)}, u32[]{:S(2)}, u32[]{:S(2)}) async-start(s32[64,1,32]{2,1,0:T(1,128)} %bitcast.5), calls=%async_computation | async-start | bytes 65536 | tf_op jit(solution)/shard_map/all_to_all | solution.py:38
  97.0 49.8 %all-to-all-start.1 = ((bf16[64,32,338]{2,1,0:T(8,128)(2,1)}), bf16[64,32,338]{2,1,0:T(8,128)(2,1)}, u32[]{:S(2)}, u32[]{:S(2)}) async-start(bf16[64,32,338]{2,1,0:T(8,128)(2,1)} %bitcast.8), calls=%async_computation.1 | async-start | bytes 3145728 | tf_op jit(solution)/shard_map/all_to_all | solution.py:31
  107.9 1368.6 %reduce-scatter.2.cloned.1.call-start = ((), (), s32[]{:S(2)}) async-start(), calls=%async_computation.4 | async-start | bytes 16842752 | tf_op jit(solution)/shard_map/reduce_scatter | solution.py:60
  112.9 2.6 copy-start.3
  115.5 41.7 %copy-start.1 = (bf16[1024,3,169]{2,1,0:T(4,128)(2,1)S(1)}, bf16[1024,3,169]{2,1,0:T(4,128)(2,1)}, u32[]{:S(2)}) copy-start(bf16[1024,3,169]{2,1,0:T(4,128)(2,1)} %copy.17) | copy-start | bytes 3115012
  157.2 1.6 copy-start
Sparse Core Ops, SparseCore 0:
  9.7 79.3 all-reduce.1
  190.5 1285.9 reduce-scatter.1
where the time goes:
time: 1490 us; the launch traced here: 1480 us
  waiting for transfers between devices  1360 us (91%)
  other arithmetic  50.6 us (3%)
  local copies, waits for them, and re-layouts  32.5 us (2%)
  starting transfers between devices  23.8 us (2%)
    reduce_scatter x1, waiting for transfers between devices, body(): lax.psum_scatter(partial_forces, ('pole', 'node'), scatter_dimension=1, t...  1290 us
    psum x1, waiting for transfers between devices, body(): summed_all = lax.psum(partials, 'pole').astype(jnp.float32)  45.1 us
    all_to_all x1, waiting for transfers between devices, body(): lax.all_to_all(outgoing.reshape(nodes, capacity, width), 'node', split_ax...  29.8 us
  transfers between devices with their start and end apart: 4, of which 3 were waited for; matrix products, arithmetic and copies ran while one was open for 3% of the time, Pallas kernels for 0%

commit v1 on v0

v1 whole, which is shorter than its diff:
```python
import functools

import jax
import jax.numpy as jnp
from jax import lax
from jax.experimental import pallas as pl
from jax.experimental.pallas import tpu as pltpu
from jax.sharding import PartitionSpec as P

ATOM_DEV = 128
LANES = 128
BASE = 32
F32 = jnp.float32
BF16 = jnp.bfloat16


def iota(shape, dim):
    return lax.broadcasted_iota(jnp.int32, shape, dim)


def params(mib=48):
    return pltpu.CompilerParams(vmem_limit_bytes=mib * 1024 * 1024)


def cost(flops, nbytes):
    return pl.CostEstimate(flops=flops, bytes_accessed=nbytes, transcendentals=0)


def plan_kernel(capacity, node_row, node_col, place):
    blocks = node_row.shape[1]
    tile = min(256, blocks)
    row = node_row[...]
    rank = jnp.zeros((1, blocks), F32)
    for start in range(0, blocks, tile):
        col = node_col[start : start + tile, :]
        earlier = iota((tile, blocks), 0) + start < iota((tile, blocks), 1)
        same = jnp.where((col == row) & earlier, 1.0, 0.0)
        rank = rank + jnp.sum(same, axis=0, keepdims=True)
    place[...] = row * capacity + rank.astype(jnp.int32)


def deriv_kernel(half, deriv, out):
    rows = deriv.shape[0]
    wide = out.shape[2]
    values = deriv[...].astype(F32)
    for c in range(3):
        first = values[:, c * half : (c + 1) * half]
        second = -values[:, (3 + c) * half : (4 + c) * half]
        rest = jnp.zeros((rows, wide - 2 * half), F32)
        out[c] = jnp.concatenate([first, second, rest], axis=1).astype(BF16)


def pack_kernel(width, place, slot_col, own, low, high, out, dens):
    blocks = own.shape[0]
    wide = out.shape[1]
    half = blocks // 2
    extra = jnp.zeros((half, wide - width), F32)
    for part, arrived in ((0, low), (1, high)):
        rows = pl.ds(part * half, half)
        total = own[rows, :].astype(F32) + arrived[...].astype(F32)
        total = jnp.concatenate([total, extra], axis=1)
        slot = slot_col[rows, :]
        lane = iota((half, wide), 1)
        total = jnp.where(lane == width, (slot // BASE + 1).astype(F32), total)
        total = jnp.where(lane == width + 1, (slot % BASE).astype(F32), total)
        dens[rows, :] = total.astype(BF16)
    tile = min(256, out.shape[0])
    where = place[...]
    for start in range(0, out.shape[0], tile):
        pick = jnp.where(iota((tile, blocks), 0) + start == where, 1.0, 0.0)
        moved = jnp.dot(pick.astype(BF16), dens[...], preferred_element_type=F32)
        out[start : start + tile, :] = moved.astype(BF16)


def force_kernel(width, arrived, deriv, atoms_row, atoms_col, out, total):
    blocks = deriv.shape[1]
    slots, wide = arrived.shape
    owners = out.shape[0]
    pick_cols = (iota((8, wide), 1) == iota((8, wide), 0) + width) & (iota((8, wide), 0) < 2)
    picker = jnp.where(pick_cols, 1.0, 0.0).astype(BF16)
    coded = lax.dot_general(
        picker, arrived[...], (((1,), (1,)), ((), ())), preferred_element_type=F32
    )
    slot_row = ((coded[0:1, :] - 1.0) * BASE + coded[1:2, :]).astype(jnp.int32)
    tile = min(256, blocks)
    for start in range(0, blocks, tile):
        pick = jnp.where(iota((tile, slots), 0) + start == slot_row, 1.0, 0.0)
        dens = jnp.dot(pick.astype(BF16), arrived[...], preferred_element_type=F32)
        hi = atoms_row[:, start : start + tile] // ATOM_DEV
        lo = atoms_col[start : start + tile, :] % ATOM_DEV
        place_lo = [iota((tile, ATOM_DEV), 1) == lo[:, e : e + 1] for e in range(2)]
        weighted = [[], []]
        for c in range(3):
            prod = dens * deriv[c, start : start + tile, :].astype(F32)
            term = jnp.sum(prod, axis=1, keepdims=True)
            for e, sign in ((0, -2.0), (1, 2.0)):
                weighted[e].append(jnp.where(place_lo[e], sign * term, 0.0).astype(BF16))
        added = jnp.zeros((owners, 3 * ATOM_DEV), F32)
        for e in range(2):
            rows = jnp.where(iota((owners, tile), 0) == hi[e : e + 1, :], 1.0, 0.0)
            added = added + jnp.dot(
                rows.astype(BF16), jnp.concatenate(weighted[e], axis=1), preferred_element_type=F32
            )
        if start == 0:
            total[...] = added
        else:
            total[...] += added
    out[...] = total[...].astype(BF16)


def body(dens_part, dest_node, pair_slot, deriv, pair_atoms):
    blocks = deriv.shape[0]
    width = dens_part.shape[2]
    half_width = width // 2
    wide = (width + 2 + LANES - 1) // LANES * LANES
    nodes = lax.axis_size("node")
    poles = lax.axis_size("pole")
    pole = lax.axis_index("pole")
    capacity = 2 * blocks // nodes
    slots = nodes * capacity
    owners = poles * nodes
    half = blocks // 2
    partials = dens_part[0]

    def part(share, which):
        first = lax.rem(share, poles) * blocks + which * half
        return lax.dynamic_slice(partials, (first, 0), (half, width))

    up = [(k, (k + 1) % poles) for k in range(poles)]
    down = [(k, (k - 1) % poles) for k in range(poles)]
    with jax.named_scope("pole_sum"):
        low = lax.ppermute(part(pole + poles - 1, 0), "pole", up)
        high = lax.ppermute(part(pole + 1, 1), "pole", down)
        for step in range(2, poles):
            low = (low.astype(F32) + part(pole + poles - step, 0).astype(F32)).astype(BF16)
            high = (high.astype(F32) + part(pole + step, 1).astype(F32)).astype(BF16)
            low = lax.ppermute(low, "pole", up)
            high = lax.ppermute(high, "pole", down)
        own = lax.dynamic_slice(partials, (pole * blocks, 0), (blocks, width))

    target_node = lax.dynamic_slice_in_dim(dest_node, pole * blocks, blocks, 0)
    target_slot = lax.dynamic_slice_in_dim(pair_slot, pole * blocks, blocks, 0)
    place = pl.pallas_call(
        functools.partial(plan_kernel, capacity),
        out_shape=jax.ShapeDtypeStruct((1, blocks), jnp.int32),
        compiler_params=params(),
        cost_estimate=cost(6 * blocks * blocks, 8 * blocks),
        name="placement",
    )(target_node.reshape(1, blocks), target_node.reshape(blocks, 1))

    tile = min(256, blocks)
    aligned = pl.pallas_call(
        functools.partial(deriv_kernel, half_width),
        grid=(blocks // tile,),
        in_specs=[pl.BlockSpec((tile, deriv.shape[1]), lambda i: (i, 0))],
        out_specs=pl.BlockSpec((3, tile, wide), lambda i: (0, i, 0)),
        out_shape=jax.ShapeDtypeStruct((3, blocks, wide), BF16),
        compiler_params=params(),
        cost_estimate=cost(6 * blocks * wide, 4 * blocks * deriv.shape[1]),
        name="align_derivatives",
    )(deriv)

    outgoing = pl.pallas_call(
        functools.partial(pack_kernel, width),
        out_shape=jax.ShapeDtypeStruct((slots, wide), BF16),
        scratch_shapes=[pltpu.VMEM((blocks, wide), BF16)],
        compiler_params=params(),
        cost_estimate=cost(2 * slots * blocks * wide, 2 * (slots + 2 * blocks) * wide),
        name="pack_density",
    )(place, target_slot.reshape(blocks, 1), own, low, high)

    with jax.named_scope("route_density"):
        arrived = lax.all_to_all(
            outgoing.reshape(nodes, capacity, wide), "node", 0, 0, tiled=True
        ).reshape(slots, wide)

    partial_forces = pl.pallas_call(
        functools.partial(force_kernel, width),
        out_shape=jax.ShapeDtypeStruct((owners, 3 * ATOM_DEV), BF16),
        scratch_shapes=[pltpu.VMEM((owners, 3 * ATOM_DEV), F32)],
        compiler_params=params(),
        cost_estimate=cost(2 * slots * blocks * wide, 2 * (slots + 3 * blocks) * wide),
        name="contract_and_scatter",
    )(arrived, aligned, pair_atoms, pair_atoms.T)

    with jax.named_scope("force_exchange"):
        gathered = lax.all_to_all(
            partial_forces.reshape(owners, 3, ATOM_DEV), ("pole", "node"), 0, 0, tiled=True
        )
        return jnp.sum(gathered.astype(F32), axis=0)


def solution(mesh):
    return jax.shard_map(
        body,
        mesh=mesh,
        in_specs=(
            P("pole", "node", None),
            P("node"),
            P("node"),
            P(("pole", "node"), None),
            P(None, ("pole", "node")),
        ),
        out_specs=P(None, ("pole", "node")),
        check_vma=False,
    )
```

time: 1490 us -> 129 us (0.09)
  waiting for transfers between devices: 1360 us -> 52.4 us
  other arithmetic: 50.6 us -> 3.98 us
  blocking collectives: 0 us -> 21.9 us
  local copies, waits for them, and re-layouts: 32.5 us -> 12.1 us
    reduce_scatter x1 -> x0, waiting for transfers between devices: 1290 us -> none  [body(): lax.psum_scatter(partial_forces, ('pole', 'node'), scatter_dimension=1, t...]
    psum x1 -> x0, waiting for transfers between devices: 45.1 us -> none  [body(): summed_all = lax.psum(partials, 'pole').astype(jnp.float32)]
    scatter-add x2 -> x0, other arithmetic: 30.3 us -> none  [the longest x1 17.5 us: body(): partial_forces = partial_forces.at[:, pair_atoms[1]].add(2.0 * pair_term.T)]
    all_to_all x0 -> x1, blocking collectives: none -> 21.9 us  [body(): lax.all_to_all(partial_forces.reshape(owners, 3, ATOM_DEV), ('pole', 'nod...]
    scatter x3 -> x0, local copies, waits for them, and re-layouts: 20.8 us -> none  [the longest x1 10.1 us: body(): pair_dens = jnp.zeros((blocks_here, width), jnp.bfloat16).at[recv_slot.re...]
    ppermute x0 -> x6, waiting for transfers between devices: none -> 19.5 us  [the longest x2 7.23 us: body(): high = lax.ppermute(high, 'pole', down)]
    another operation x3 -> x0, other arithmetic: 18.2 us -> none
    all_to_all x2 -> x1, waiting for transfers between devices: 29.8 us -> 33 us  [body(): lax.all_to_all(outgoing.reshape(nodes, capacity, wide), 'node', 0, 0, til...]
  transfers between devices with their start and end apart: 4 -> 7, of which waited for: 3 -> 5; matrix products, arithmetic and copies ran while one was open for 3% -> 8% of each run, Pallas kernels for 0% -> 1%
where the time goes in v1:
time: 129 us
  waiting for transfers between devices  52.4 us (41%)
  starting transfers between devices  26.2 us (20%)
  blocking collectives  21.9 us (17%)
  local copies, waits for them, and re-layouts  12.1 us (9%)
  Pallas kernels  11.9 us (9%)
  other arithmetic  3.98 us (3%)
    all_to_all x1, waiting for transfers between devices, body(): lax.all_to_all(outgoing.reshape(nodes, capacity, wide), 'node', 0, 0, til...  33 us
    all_to_all x1, blocking collectives, body(): lax.all_to_all(partial_forces.reshape(owners, 3, ATOM_DEV), ('pole', 'nod...  21.9 us
    all_to_all x1, starting transfers between devices, body(): lax.all_to_all(outgoing.reshape(nodes, capacity, wide), 'node', 0, 0, til...  15.3 us
    ppermute x2, waiting for transfers between devices, body(): high = lax.ppermute(high, 'pole', down)  7.23 us
    ppermute x2, starting transfers between devices, body(): high = lax.ppermute(high, 'pole', down)  7.08 us
    ppermute x1, waiting for transfers between devices, body(): high = lax.ppermute(part(pole + 1, 1), 'pole', down)  7.04 us
    unnamed x12, local copies, waits for them, and re-layouts  7 us
    pallas_call x1, Pallas kernels, body(): pl.pallas_call(functools.partial(force_kernel, width), out_shape=jax.Shap...  5.9 us
  transfers between devices with their start and end apart: 7, of which 5 were waited for; matrix products, arithmetic and copies ran while one was open for 8% of the time, Pallas kernels for 1%

profile of v1, /device:TPU:1, one launch (start us, length us, event | category | flops | bytes accessed | tf_op | source)
XLA Modules:
  0.0 128.8 jit_solution(5616344140305759970)
XLA Ops:
  0.0 1.7 %constant_dynamic-slice_fusion = (bf16[1,512,338]{1,2,0:T(8,128)(2,1)S(1)}, bf16[1,512,338]{1,2,0:T(8,128)(2,1)S(1)}, bf16[1,512,338]{1,2,0:T(8,128)(2,1)S(1)}, ...) fusion(bf16[1,4096,338]{1,2,0:T(8,128)(2,1)} %param.5, ...), kind=kLoop, calls=%fused_computation.9 | loop fusion | bytes 4153368 | tf_op jit(solution)/shard_map/pole_sum/dynamic_slice | solution.py:127
  1.7 0.2 copy.32
  2.0 3.6 %collective-permute-start.3 = (bf16[512,338]{1,0:T(8,128)(2,1)S(1)}, bf16[512,338]{1,0:T(8,128)(2,1)S(1)}, u32[]{:S(2)}, u32[]{:S(2)}) collective-permute-start(bf16[512,338]{1,0:T(8,128)(2,1)S(1)} %bitcast.28), channel_id=1, source_target_pairs={{0,192},{64,0},{128,64},{192,128},{1,193},{65,1},{129,65},{193,129... | collective-permute-start | bytes 1038344 | tf_op jit(solution)/shard_map/pole_sum/ppermute | solution.py:133
  5.6 0.2 copy.29
  5.8 0.1 collective-permute-start
  5.9 0.2 copy.42
  6.1 0.2 copy.40
  6.4 7.0 %collective-permute-done.3 = bf16[512,338]{1,0:T(8,128)(2,1)S(1)} collective-permute-done((bf16[512,338]{1,0:T(8,128)(2,1)S(1)}, bf16[512,338]{1,0:T(8,128)(2,1)S(1)}, u32[]{:S(2)}, u32[]{:S(2)}) %collective-permute-start.3) | collective-permute-done | bytes 346144 | tf_op jit(solution)/shard_map/pole_sum/ppermute | solution.py:133
  13.4 0.1 fusion.1
  13.5 3.5 %collective-permute-start.4 = (bf16[512,338]{1,0:T(8,128)(2,1)S(1)}, bf16[512,338]{1,0:T(8,128)(2,1)}, u32[]{:S(2)}, u32[]{:S(2)}) collective-permute-start(bf16[512,338]{1,0:T(8,128)(2,1)S(1)} %fusion.1), channel_id=1, source_target_pairs={{0,192},{64,0},{128,64},{192,128},{1,193},{65,1},{129,65},{193,129... | collective-permute-start | bytes 1038344 | tf_op jit(solution)/shard_map/pole_sum/ppermute | solution.py:138
  17.0 0.0 collective-permute-done
  17.0 0.1 fusion.3
  17.1 0.1 collective-permute-start.1
  17.2 0.2 copy.43
  17.4 0.2 copy.41
  17.6 6.2 %collective-permute-done.4 = bf16[512,338]{1,0:T(8,128)(2,1)} collective-permute-done((bf16[512,338]{1,0:T(8,128)(2,1)S(1)}, bf16[512,338]{1,0:T(8,128)(2,1)}, u32[]{:S(2)}, u32[]{:S(2)}) %collective-permute-start.4) | collective-permute-done | bytes 346144 | tf_op jit(solution)/shard_map/pole_sum/ppermute | solution.py:138
  23.8 1.1 fusion
  24.9 3.6 %collective-permute-start.5 = (bf16[512,338]{1,0:T(8,128)(2,1)S(1)}, bf16[512,338]{1,0:T(8,128)(2,1)S(1)}, u32[]{:S(2)}, u32[]{:S(2)}) collective-permute-start(bf16[512,338]{1,0:T(8,128)(2,1)S(1)} %fusion), channel_id=1, source_target_pairs={{0,192},{64,0},{128,64},{192,128},{1,193},{65,1},{129,65},{193,129... | collective-permute-start | bytes 1038344 | tf_op jit(solution)/shard_map/pole_sum/ppermute | solution.py:138
  28.5 0.0 collective-permute-done.1
  28.5 1.8 %fusion.2 = bf16[512,338]{1,0:T(8,128)(2,1)} fusion(bf16[512,338]{1,0:T(8,128)(2,1)} %collective-permute-done.1, bf16[1,512,338]{2,1,0:T(8,128)(2,1)S(1)} %copy.41), kind=kLoop, calls=%fused_computation.5 | loop fusion | flops 692224 | bytes 1038336 | tf_op jit(solution)/shard_map/pole_sum/convert_element_type | solution.py:135
  30.4 0.0 collective-permute-start.2
  30.4 0.0 dynamic-slice-start
  30.4 0.7 dynamic_slice.33
  31.1 0.2 copy.27.node_col
  31.3 1.2 constant_dynamic-slice_fusion.6
  32.5 0.4 copy.28
  32.8 0.0 dynamic-slice-done
  32.8 0.2 copy.35.slot_col
  33.1 0.4 placement.1.place
  33.5 1.0 collective-permute-done.5.high
  34.5 5.2 %collective-permute-done.2.low = bf16[512,338]{1,0:T(8,128)(2,1)S(1)} collective-permute-done((bf16[512,338]{1,0:T(8,128)(2,1)}, bf16[512,338]{1,0:T(8,128)(2,1)S(1)}, u32[]{:S(2)}, u32[]{:S(2)}) %collective-permute-start.2) | collective-permute-done | bytes 346144 | tf_op jit(solution)/shard_map/pole_sum/ppermute | solution.py:137
  39.7 4.2 %pack_density.1 = bf16[2048,384]{1,0:T(8,128)(2,1)} custom-call(s32[1,1024]{1,0:T(1,128)S(1)} %placement.1.place, s32[1024,1]{1,0:T(8,128)S(1)} %copy.35.slot_col, bf16[1024,338]{1,0:T(8,128)(2,1)S(1)} %bitcast.22, bf16[512,338]{1,0:T(8,128)(2,1)S(1)} %collective-permute-done.2.low, bf16[512,338]{1,0:T(8,128)(2,1)S(1)} %collective-permute-done.5.high), custom_call_target="tpu_custom_call" | custom-call | flops 1610612736 | bytes 3145728 | tf_op jit(solution)/shard_map/pack_density/pallas_call | solution.py:163
  43.8 15.3 %all-to-all-start = ((bf16[64,32,384]{2,1,0:T(8,128)(2,1)}), bf16[64,32,384]{2,1,0:T(8,128)(2,1)}, u32[]{:S(2)}, u32[]{:S(2)}) async-start(bf16[64,32,384]{2,1,0:T(8,128)(2,1)} %bitcast.10), calls=%async_computation | async-start | bytes 3145728 | tf_op jit(solution)/shard_map/route_density/all_to_all | solution.py:173
  59.2 0.0 copy-start.2
  59.2 2.9 %copy.36.deriv = bf16[1024,1014]{1,0:T(8,128)(2,1)S(1)} copy(bf16[1024,1014]{0,1:T(8,128)(2,1)} %param.8) | data formatting | bytes 4153344 | tf_op args[3]
  62.1 0.0 copy-done.2
  62.1 0.2 copy.37
  62.3 1.4 %align_derivatives.1.deriv = bf16[3,1024,384]{2,1,0:T(8,128)(2,1)S(1)} custom-call(bf16[1024,1014]{1,0:T(8,128)(2,1)S(1)} %copy.36.deriv), custom_call_target="tpu_custom_call" | custom-call | flops 2359296 | bytes 4153344 | tf_op jit(solution)/shard_map/align_derivatives/pallas_call | solution.py:152
  63.7 0.0 copy-start
  63.7 1.4 %copy-done = bf16[3,1024,384]{2,1,0:T(8,128)(2,1)} copy-done((bf16[3,1024,384]{2,1,0:T(8,128)(2,1)}, bf16[3,1024,384]{2,1,0:T(8,128)(2,1)S(1)}, u32[]{:S(2)}) %copy-start) | copy-done | bytes 2359320
  65.1 33.0 %all-to-all-done = bf16[64,32,384]{2,1,0:T(8,128)(2,1)} async-done(((bf16[64,32,384]{2,1,0:T(8,128)(2,1)}), bf16[64,32,384]{2,1,0:T(8,128)(2,1)}, u32[]{:S(2)}, u32[]{:S(2)}) %all-to-all-start) | async-done | bytes 1572896 | tf_op jit(solution)/shard_map/route_density/all_to_all | solution.py:173
  98.1 0.0 copy-start.1
  98.1 1.7 %copy-done.1 = bf16[3,1024,384]{2,1,0:T(8,128)(2,1)S(1)} copy-done((bf16[3,1024,384]{2,1,0:T(8,128)(2,1)S(1)}, bf16[3,1024,384]{2,1,0:T(8,128)(2,1)}, u32[]{:S(2)}) %copy-start.1) | copy-done | bytes 2359320
  99.8 5.9 %contract_and_scatter.1 = bf16[256,384]{1,0:T(8,128)(2,1)S(1)} custom-call(bf16[2048,384]{1,0:T(8,128)(2,1)} %bitcast.11.arrived, bf16[3,1024,384]{2,1,0:T(8,128)(2,1)S(1)} %copy-done.1, s32[2,1024]{1,0:T(2,128)S(1)} %copy-done.2, s32[1024,2]{1,0:T(8,128)S(1)} %bitcast.23), custom_call_target="tpu_custom_call" | custom-call | flops 1610612736 | bytes 3932160 | tf_op jit(solution)/shard_map/contract_and_scatter/pallas_call | solution.py:177
  105.7 0.1 copy.38
  105.8 0.2 copy.39
  106.0 21.9 %all_to_all.10 = bf16[256,3,128]{2,1,0:T(4,128)(2,1)S(1)} all-to-all(bf16[256,3,128]{2,1,0:T(4,128)(2,1)S(1)} %copy.39), channel_id=1, replica_groups=mesh['pole'=4,'node'=64] {'pole','node'}, dimensions={0} | all-to-all | bytes 393216 | tf_op jit(solution)/shard_map/force_exchange/all_to_all | solution.py:187
  127.9 0.9 convert_reduce_fusion
Async XLA Ops:
  2.0 11.4 %collective-permute-start.3 = (bf16[512,338]{1,0:T(8,128)(2,1)S(1)}, bf16[512,338]{1,0:T(8,128)(2,1)S(1)}, u32[]{:S(2)}, u32[]{:S(2)}) collective-permute-start(bf16[512,338]{1,0:T(8,128)(2,1)S(1)} %bitcast.28), channel_id=1, source_target_pairs={{0,192},{64,0},{128,64},{192,128},{1,193},{65,1},{129,65},{193,129... | collective-permute-start | bytes 1038344 | tf_op jit(solution)/shard_map/pole_sum/ppermute | solution.py:133
  5.8 11.2 %collective-permute-start = (bf16[512,338]{1,0:T(8,128)(2,1)S(1)}, bf16[512,338]{1,0:T(8,128)(2,1)S(1)}, u32[]{:S(2)}, u32[]{:S(2)}) collective-permute-start(bf16[512,338]{1,0:T(8,128)(2,1)S(1)} %bitcast.27), channel_id=1, source_target_pairs={{0,64},{64,128},{128,192},{192,0},{1,65},{65,129},{129,193},{193,1... | collective-permute-start | bytes 1038344 | tf_op jit(solution)/shard_map/pole_sum/ppermute | solution.py:132
  13.5 10.3 %collective-permute-start.4 = (bf16[512,338]{1,0:T(8,128)(2,1)S(1)}, bf16[512,338]{1,0:T(8,128)(2,1)}, u32[]{:S(2)}, u32[]{:S(2)}) collective-permute-start(bf16[512,338]{1,0:T(8,128)(2,1)S(1)} %fusion.1), channel_id=1, source_target_pairs={{0,192},{64,0},{128,64},{192,128},{1,193},{65,1},{129,65},{193,129... | collective-permute-start | bytes 1038344 | tf_op jit(solution)/shard_map/pole_sum/ppermute | solution.py:138
  17.1 11.4 %collective-permute-start.1 = (bf16[512,338]{1,0:T(8,128)(2,1)S(1)}, bf16[512,338]{1,0:T(8,128)(2,1)}, u32[]{:S(2)}, u32[]{:S(2)}) collective-permute-start(bf16[512,338]{1,0:T(8,128)(2,1)S(1)} %fusion.3), channel_id=1, source_target_pairs={{0,64},{64,128},{128,192},{192,0},{1,65},{65,129},{129,193},{193,1... | collective-permute-start | bytes 1038344 | tf_op jit(solution)/shard_map/pole_sum/ppermute | solution.py:137
  24.9 9.5 %collective-permute-start.5 = (bf16[512,338]{1,0:T(8,128)(2,1)S(1)}, bf16[512,338]{1,0:T(8,128)(2,1)S(1)}, u32[]{:S(2)}, u32[]{:S(2)}) collective-permute-start(bf16[512,338]{1,0:T(8,128)(2,1)S(1)} %fusion), channel_id=1, source_target_pairs={{0,192},{64,0},{128,64},{192,128},{1,193},{65,1},{129,65},{193,129... | collective-permute-start | bytes 1038344 | tf_op jit(solution)/shard_map/pole_sum/ppermute | solution.py:138
  30.4 9.3 %collective-permute-start.2 = (bf16[512,338]{1,0:T(8,128)(2,1)}, bf16[512,338]{1,0:T(8,128)(2,1)S(1)}, u32[]{:S(2)}, u32[]{:S(2)}) collective-permute-start(bf16[512,338]{1,0:T(8,128)(2,1)} %fusion.2), channel_id=1, source_target_pairs={{0,64},{64,128},{128,192},{192,0},{1,65},{65,129},{129,193},{193,1... | collective-permute-start | bytes 1038344 | tf_op jit(solution)/shard_map/pole_sum/ppermute | solution.py:137
  30.4 2.5 %dynamic-slice-start = ((s32[4096]{0:T(1024)}, s32[]{:T(128)}), s32[1024]{0:T(1024)S(1)}, s32[]{:S(2)}) async-start(s32[4096]{0:T(1024)} %param.7, s32[]{:T(128)} %select_n.23), calls=%async_computation.2 | async-start | bytes 8704 | tf_op jit(solution)/shard_map/dynamic_slice | solution.py:142
  43.8 54.3 %all-to-all-start = ((bf16[64,32,384]{2,1,0:T(8,128)(2,1)}), bf16[64,32,384]{2,1,0:T(8,128)(2,1)}, u32[]{:S(2)}, u32[]{:S(2)}) async-start(bf16[64,32,384]{2,1,0:T(8,128)(2,1)} %bitcast.10), calls=%async_computation | async-start | bytes 3145728 | tf_op jit(solution)/shard_map/route_density/all_to_all | solution.py:173
  59.2 2.9 %copy-start.2 = (s32[2,1024]{1,0:T(2,128)S(1)}, s32[2,1024]{1,0:T(2,128)}, u32[]{:S(2)}) copy-start(s32[2,1024]{1,0:T(2,128)} %atoms_row.1) | copy-start | bytes 24580
  63.7 1.4 %copy-start = (bf16[3,1024,384]{2,1,0:T(8,128)(2,1)}, bf16[3,1024,384]{2,1,0:T(8,128)(2,1)S(1)}, u32[]{:S(2)}) copy-start(bf16[3,1024,384]{2,1,0:T(8,128)(2,1)S(1)} %align_derivatives.1.deriv) | copy-start | bytes 7077892
  98.1 1.7 %copy-start.1 = (bf16[3,1024,384]{2,1,0:T(8,128)(2,1)S(1)}, bf16[3,1024,384]{2,1,0:T(8,128)(2,1)}, u32[]{:S(2)}) copy-start(bf16[3,1024,384]{2,1,0:T(8,128)(2,1)} %copy-done) | copy-start | bytes 7077892

commit v2 on v1

v2 whole, which is shorter than its diff:
```python
import functools

import jax
import jax.numpy as jnp
from jax import lax
from jax.experimental import pallas as pl
from jax.experimental.pallas import tpu as pltpu
from jax.sharding import PartitionSpec as P

ATOM_DEV = 128
LANES = 128
BASE = 32
F32 = jnp.float32
BF16 = jnp.bfloat16


def iota(shape, dim):
    return lax.broadcasted_iota(jnp.int32, shape, dim)


def params(mib=16):
    return pltpu.CompilerParams(vmem_limit_bytes=mib * 1024 * 1024)


def cost(flops, nbytes):
    return pl.CostEstimate(flops=flops, bytes_accessed=nbytes, transcendentals=0)


def one_hot(row, start, rows):
    found = iota((rows, row.shape[1]), 0) + start == row
    return jnp.where(found, 1.0, 0.0).astype(BF16)


def rows_times(a, b):
    return lax.dot_general(a, b, (((1,), (1,)), ((), ())), preferred_element_type=F32)


def plan_kernel(capacity, node_row, node_col, pick, where):
    slots, blocks = pick.shape
    tile = min(256, blocks)
    row = node_row[...]
    rank = jnp.zeros((1, blocks), F32)
    for start in range(0, blocks, tile):
        col = node_col[start : start + tile, :]
        earlier = iota((tile, blocks), 0) + start < iota((tile, blocks), 1)
        same = jnp.where((col == row) & earlier, 1.0, 0.0)
        rank = rank + jnp.sum(same, axis=0, keepdims=True)
    place = row * capacity + rank.astype(jnp.int32)
    where[...] = place
    for start in range(0, slots, tile):
        pick[start : start + tile, :] = one_hot(place, start, tile)


def deriv_kernel(half, deriv, out_second, out_first):
    rows = deriv.shape[0]
    split = out_second.shape[2]
    wide = split + out_first.shape[2]
    values = deriv[...].astype(F32)
    for c in range(3):
        first = values[:, c * half : (c + 1) * half]
        second = -values[:, (3 + c) * half : (4 + c) * half]
        rest = jnp.zeros((rows, wide - 2 * half), F32)
        line = jnp.concatenate([first, second, rest], axis=1).astype(BF16)
        out_second[c] = line[:, :split]
        out_first[c] = line[:, split:]


def pole_total(parts):
    total = parts[0][...].astype(F32)
    for other in parts[1:]:
        total = total + other[...].astype(F32)
    return total


def pack_first_kernel(pick, slot_row, *refs):
    *parts, out, dens = refs
    columns = parts[0].shape[0]
    wide = dens.shape[0]
    slot = slot_row[...]
    dens[columns:, :] = jnp.zeros((wide - columns, dens.shape[1]), F32)
    dens[:columns, :] = pole_total(parts)
    dens[columns : columns + 1, :] = (slot // BASE + 1).astype(F32)
    dens[columns + 1 : columns + 2, :] = (slot % BASE).astype(F32)
    total = dens[...].astype(BF16)
    tile = min(256, out.shape[0])
    for start in range(0, out.shape[0], tile):
        rows = pick[start : start + tile, :]
        out[start : start + tile, :] = rows_times(rows, total).astype(BF16)


def pack_second_kernel(where, *refs):
    *parts, out = refs
    total = pole_total(parts).astype(BF16)
    place = where[...]
    tile = min(256, out.shape[0])
    for start in range(0, out.shape[0], tile):
        rows = one_hot(place, start, tile)
        out[start : start + tile, :] = rows_times(rows, total).astype(BF16)


def row_terms(dens, deriv, start):
    rows, wide = dens.shape
    ones = jnp.ones((8, LANES), BF16)
    terms = []
    for c in range(3):
        prod = dens * deriv[c, start : start + rows, :].astype(F32)
        folded = prod[:, :LANES]
        for first in range(LANES, wide, LANES):
            folded = folded + prod[:, first : first + LANES]
        large = folded.astype(BF16)
        small = (folded - large.astype(F32)).astype(BF16)
        terms.append((rows_times(ones, large) + rows_times(ones, small))[0:1, :])
    return terms


def contract_first_kernel(columns, arrived, deriv, atoms, info):
    blocks = atoms.shape[1]
    slots, wide = arrived.shape
    line = iota((8, wide), 0)
    picker = jnp.where((iota((8, wide), 1) == line + columns) & (line < 2), 1.0, 0.0)
    coded = rows_times(picker.astype(BF16), arrived[...])
    slot_row = (coded[0:1, :] - 1.0) * BASE + coded[1:2, :]
    info[...] = jnp.zeros_like(info)
    info[3:4, :] = slot_row
    info[4:6, :blocks] = atoms[...].astype(F32)
    slot_row = slot_row.astype(jnp.int32)
    tile = min(256, blocks)
    for start in range(0, blocks, tile):
        dens = jnp.dot(
            one_hot(slot_row, start, tile), arrived[...], preferred_element_type=F32
        )
        for c, term in enumerate(row_terms(dens, deriv, start)):
            info[c : c + 1, start : start + tile] = term


def force_kernel(arrived, deriv, info, out, total):
    blocks = deriv.shape[1]
    owners = out.shape[0]
    slot_row = info[3:4, :].astype(jnp.int32)
    tile = min(256, blocks)
    for start in range(0, blocks, tile):
        dens = jnp.dot(
            one_hot(slot_row, start, tile), arrived[...], preferred_element_type=F32
        )
        terms = row_terms(dens, deriv, start)
        added = None
        for e, sign in ((0, -2.0), (1, 2.0)):
            atom = info[4 + e : 5 + e, start : start + tile].astype(jnp.int32)
            found = iota((ATOM_DEV, tile), 0) == atom % ATOM_DEV
            weighted = []
            for c in range(3):
                term = sign * (terms[c] + info[c : c + 1, start : start + tile])
                weighted.append(jnp.where(found, term, 0.0).astype(BF16))
            owner = one_hot(atom // ATOM_DEV, 0, owners)
            moved = rows_times(owner, jnp.concatenate(weighted, axis=0))
            added = moved if added is None else added + moved
        if start == 0:
            total[...] = added
        else:
            total[...] += added
    out[...] = total[...].astype(BF16)


def body(dens_part, dest_node, pair_slot, deriv, pair_atoms):
    blocks = deriv.shape[0]
    width = dens_part.shape[2]
    half_width = width // 2
    split = width // LANES * LANES
    last = width - split
    wide = (last + 2 + LANES - 1) // LANES * LANES
    nodes = lax.axis_size("node")
    poles = lax.axis_size("pole")
    pole = lax.axis_index("pole")
    capacity = 2 * blocks // nodes
    slots = nodes * capacity
    owners = poles * nodes
    partials = dens_part[0].T

    def exchange(first_column, columns):
        def share(which):
            start = lax.rem(pole + which, poles) * blocks
            return lax.dynamic_slice(partials, (first_column, start), (columns, blocks))

        parts = []
        for step in (1, 3, 2):
            pairs = [(k, (k + step) % poles) for k in range(poles)]
            parts.append(lax.ppermute(share(step), "pole", pairs))
        return [share(0)] + parts

    with jax.named_scope("pole_exchange_first"):
        parts_first = exchange(split, last)
    with jax.named_scope("pole_exchange_second"):
        parts_second = exchange(0, split)

    target_node = lax.dynamic_slice_in_dim(dest_node, pole * blocks, blocks, 0)
    target_slot = lax.dynamic_slice_in_dim(pair_slot, pole * blocks, blocks, 0)
    pick_out, place = pl.pallas_call(
        functools.partial(plan_kernel, capacity),
        out_shape=[
            jax.ShapeDtypeStruct((slots, blocks), BF16),
            jax.ShapeDtypeStruct((1, blocks), jnp.int32),
        ],
        compiler_params=params(),
        cost_estimate=cost(6 * blocks * blocks, 2 * slots * blocks),
        name="placement",
    )(target_node.reshape(1, blocks), target_node.reshape(blocks, 1))

    tile = min(256, blocks)
    deriv_second, deriv_first = pl.pallas_call(
        functools.partial(deriv_kernel, half_width),
        grid=(blocks // tile,),
        in_specs=[pl.BlockSpec((tile, deriv.shape[1]), lambda i: (i, 0))],
        out_specs=[
            pl.BlockSpec((3, tile, split), lambda i: (0, i, 0)),
            pl.BlockSpec((3, tile, wide), lambda i: (0, i, 0)),
        ],
        out_shape=[
            jax.ShapeDtypeStruct((3, blocks, split), BF16),
            jax.ShapeDtypeStruct((3, blocks, wide), BF16),
        ],
        compiler_params=params(),
        cost_estimate=cost(6 * blocks * width, 4 * blocks * deriv.shape[1]),
        name="align_derivatives",
    )(deriv)

    def route(packed):
        columns = packed.shape[1]
        moved = lax.all_to_all(
            packed.reshape(nodes, capacity, columns), "node", 0, 0, tiled=True
        )
        return moved.reshape(slots, columns)

    packed_first = pl.pallas_call(
        pack_first_kernel,
        out_shape=jax.ShapeDtypeStruct((slots, wide), BF16),
        scratch_shapes=[pltpu.VMEM((wide, blocks), F32)],
        compiler_params=params(),
        cost_estimate=cost(16 * slots * blocks * wide, 16 * slots * blocks),
        name="pack_first",
    )(pick_out, target_slot.reshape(1, blocks), *parts_first)
    with jax.named_scope("route_first"):
        arrived_first = route(packed_first)

    packed_second = pl.pallas_call(
        pack_second_kernel,
        out_shape=jax.ShapeDtypeStruct((slots, split), BF16),
        compiler_params=params(),
        cost_estimate=cost(200 * slots * blocks * split, 200 * slots * blocks),
        name="pack_second",
    )(place, *parts_second)
    with jax.named_scope("route_second"):
        arrived_second = route(packed_second)

    info = pl.pallas_call(
        functools.partial(contract_first_kernel, last),
        out_shape=jax.ShapeDtypeStruct((8, slots), F32),
        compiler_params=params(),
        cost_estimate=cost(2 * slots * blocks * wide, 2 * slots * blocks),
        name="contract_first",
    )(arrived_first, deriv_first, pair_atoms)

    partial_forces = pl.pallas_call(
        force_kernel,
        out_shape=jax.ShapeDtypeStruct((owners, 3 * ATOM_DEV), BF16),
        scratch_shapes=[pltpu.VMEM((owners, 3 * ATOM_DEV), F32)],
        compiler_params=params(),
        cost_estimate=cost(2 * slots * blocks * split, 2 * slots * blocks),
        name="contract_and_scatter",
    )(arrived_second, deriv_second, info)

    with jax.named_scope("force_exchange"):
        gathered = lax.all_to_all(
            partial_forces.reshape(owners, 3, ATOM_DEV), ("pole", "node"), 0, 0, tiled=True
        )
        return jnp.sum(gathered.astype(F32), axis=0)


def solution(mesh):
    return jax.shard_map(
        body,
        mesh=mesh,
        in_specs=(
            P("pole", "node", None),
            P("node"),
            P("node"),
            P(("pole", "node"), None),
            P(None, ("pole", "node")),
        ),
        out_specs=P(None, ("pole", "node")),
        check_vma=False,
    )
```

time: 129 us -> 116 us (0.90)
  waiting for transfers between devices: 52.4 us -> 34.6 us
  other arithmetic: 3.98 us -> 0.85 us
  starting transfers between devices: 26.2 us -> 28.4 us
  Pallas kernels: 11.9 us -> 13.8 us
  local copies, waits for them, and re-layouts: 12.1 us -> 13.9 us
  blocking collectives: 21.9 us -> 23.6 us
    ppermute x6, waiting for transfers between devices: 19.5 us -> 4.26 us  [exchange(): parts.append(lax.ppermute(share(step), 'pole', pairs))]
    all_to_all x1 -> x2, starting transfers between devices: 15.3 us -> 20.4 us  [route(): lax.all_to_all(packed.reshape(nodes, capacity, columns), 'node', 0, 0, ti...]
    convert_element_type x4 -> x0, other arithmetic: 3.13 us -> none  [the longest x2 1.94 us: body(): (low.astype(F32) + part(pole + poles - step, 0).astype(F32)).astype(BF16)]
    ppermute x6, starting transfers between devices: 10.9 us -> 8 us  [exchange(): parts.append(lax.ppermute(share(step), 'pole', pairs))]
    all_to_all x1 -> x2, waiting for transfers between devices: 33 us -> 30.3 us  [route(): lax.all_to_all(packed.reshape(nodes, capacity, columns), 'node', 0, 0, ti...]
    pallas_call x3 -> x5, Pallas kernels: 10.5 us -> 12.5 us  [the longest x1 4.26 us: body(): pl.pallas_call(force_kernel, out_shape=jax.ShapeDtypeStruct((owners, 3 *...]
    all_to_all x1, blocking collectives: 21.9 us -> 23.6 us  [body(): lax.all_to_all(partial_forces.reshape(owners, 3, ATOM_DEV), ('pole', 'nod...]
    dynamic_slice x5 -> x2, local copies, waits for them, and re-layouts: 3.67 us -> 4.63 us  [share(): return lax.dynamic_slice(partials, (first_column, start), (columns, blocks))]
  transfers between devices with their start and end apart: 7 -> 8, of which waited for: 5 -> 3; matrix products, arithmetic and copies ran while one was open for 8% -> 6% of each run, Pallas kernels for 1% -> 8%
where the time goes in v2:
time: 116 us; the launch traced here: 115 us
  waiting for transfers between devices  34.6 us (30%)
  starting transfers between devices  28.4 us (24%)
  blocking collectives  23.6 us (20%)
  local copies, waits for them, and re-layouts  13.9 us (12%)
  Pallas kernels  13.8 us (12%)
    all_to_all x2, waiting for transfers between devices, route(): lax.all_to_all(packed.reshape(nodes, capacity, columns), 'node', 0, 0, ti...  30.3 us
    all_to_all x1, blocking collectives, body(): lax.all_to_all(partial_forces.reshape(owners, 3, ATOM_DEV), ('pole', 'nod...  23.6 us
    all_to_all x2, starting transfers between devices, route(): lax.all_to_all(packed.reshape(nodes, capacity, columns), 'node', 0, 0, ti...  20.4 us
    ppermute x6, starting transfers between devices, exchange(): parts.append(lax.ppermute(share(step), 'pole', pairs))  8 us
    unnamed x11, local copies, waits for them, and re-layouts  7.3 us
    dynamic_slice x2, local copies, waits for them, and re-layouts, share(): return lax.dynamic_slice(partials, (first_column, start), (columns, blocks))  4.63 us
    pallas_call x1, Pallas kernels, body(): pl.pallas_call(force_kernel, out_shape=jax.ShapeDtypeStruct((owners, 3 *...  4.26 us
    ppermute x6, waiting for transfers between devices, exchange(): parts.append(lax.ppermute(share(step), 'pole', pairs))  4.26 us
  transfers between devices with their start and end apart: 8, of which 3 were waited for; matrix products, arithmetic and copies ran while one was open for 6% of the time, Pallas kernels for 8%

profile of v2, /device:TPU:1, one launch (start us, length us, event | category | flops | bytes accessed | tf_op | source)
XLA Modules:
  0.0 115.1 jit_solution(13112769095826982903)
XLA Ops:
  0.0 1.9 %dynamic-slice_bitcast_fusion.4 = (bf16[82,1024]{1,0:T(8,128)(2,1)S(1)}, bf16[82,1024]{1,0:T(8,128)(2,1)S(1)}, bf16[82,1024]{1,0:T(8,128)(2,1)S(1)}, bf16[82,1024]{1,0:T(8,128)(2,1)}) fusion(bf16[1,4096,338]{1,2,0:T(8,128)(2,1)} %param.5, s32[]{:T(128)S(6)} %select_n.24, s32[]{:T(128)S(6)} %select_n.22, s32[]{:T(128)S(6)} %select_n.21, s32[]{:T(128)S(6)} %select_n.23), kind=kLoop, calls=%fused_computation.5 | loop fusion | bytes 1343504 | tf_op jit(solution)/shard_map/pole_exchange_first/dynamic_slice | solution.py:182
  1.9 2.1 %collective-permute-start.3 = (bf16[82,1024]{1,0:T(8,128)(2,1)S(1)}, bf16[82,1024]{1,0:T(8,128)(2,1)S(1)}, u32[]{:S(2)}, u32[]{:S(2)}) collective-permute-start(bf16[82,1024]{1,0:T(8,128)(2,1)S(1)} %get-tuple-element.14), channel_id=1, source_target_pairs={{0,64},{64,128},{128,192},{192,0},{1,65},{65,129},{129,193},{193,1... | collective-permute-start | bytes 503816 | tf_op jit(solution)/shard_map/pole_exchange_first/ppermute | solution.py:187
  4.0 1.4 %collective-permute-start.4 = (bf16[82,1024]{1,0:T(8,128)(2,1)}, bf16[82,1024]{1,0:T(8,128)(2,1)S(1)}, u32[]{:S(2)}, u32[]{:S(2)}) collective-permute-start(bf16[82,1024]{1,0:T(8,128)(2,1)} %get-tuple-element.16), channel_id=1, source_target_pairs={{0,192},{64,0},{128,64},{192,128},{1,193},{65,1},{129,65},{193,129... | collective-permute-start | bytes 503816 | tf_op jit(solution)/shard_map/pole_exchange_first/ppermute | solution.py:187
  5.5 1.6 %collective-permute-start.5 = (bf16[82,1024]{1,0:T(8,128)(2,1)S(1)}, bf16[82,1024]{1,0:T(8,128)(2,1)S(1)}, u32[]{:S(2)}, u32[]{:S(2)}) collective-permute-start(bf16[82,1024]{1,0:T(8,128)(2,1)S(1)} %get-tuple-element.13), channel_id=1, source_target_pairs={{0,128},{64,192},{128,0},{192,64},{1,129},{65,193},{129,1},{193,65... | collective-permute-start | bytes 503816 | tf_op jit(solution)/shard_map/pole_exchange_first/ppermute | solution.py:187
  7.1 2.7 %dynamic-slice_bitcast_fusion = (bf16[256,1024]{1,0:T(8,128)(2,1)}, bf16[256,1024]{1,0:T(8,128)(2,1)}, bf16[256,1024]{1,0:T(8,128)(2,1)}, bf16[256,1024]{1,0:T(8,128)(2,1)S(1)}) fusion(bf16[1,4096,338]{1,2,0:T(8,128)(2,1)} %param.5, s32[]{:T(128)S(6)} %select_n.24, s32[]{:T(128)S(6)} %select_n.23, s32[]{:T(128)S(6)} %select_n.22, s32[]{:T(128)S(6)} %select_n.21), kind=kLoop, calls=%fused_computation.1 | loop fusion | bytes 4194320 | tf_op jit(solution)/shard_map/pole_exchange_second/dynamic_slice | solution.py:182
  9.8 0.4 collective-permute-start
  10.2 2.3 %collective-permute-start.1 = (bf16[256,1024]{1,0:T(8,128)(2,1)}, bf16[256,1024]{1,0:T(8,128)(2,1)S(1)}, u32[]{:S(2)}, u32[]{:S(2)}) collective-permute-start(bf16[256,1024]{1,0:T(8,128)(2,1)} %get-tuple-element.18), channel_id=1, source_target_pairs={{0,192},{64,0},{128,64},{192,128},{1,193},{65,1},{129,65},{193,129... | collective-permute-start | bytes 1572872 | tf_op jit(solution)/shard_map/pole_exchange_second/ppermute | solution.py:187
  12.5 0.0 collective-permute-done.3.refs_1_
  12.5 0.1 collective-permute-start.2
  12.6 0.7 dynamic_slice.30
  13.3 0.2 copy.10.node_col
  13.6 0.7 dynamic_slice.35
  14.3 1.4 %placement.1 = (bf16[2048,1024]{1,0:T(8,128)(2,1)S(1)}, s32[1,1024]{1,0:T(1,128)S(1)}) custom-call(s32[1,1024]{1,0:T(1,128)S(1)} %bitcast.43, s32[1024,1]{1,0:T(8,128)S(1)} %copy.10.node_col), custom_call_target="tpu_custom_call" | custom-call | flops 6291456 | bytes 4194304 | tf_op jit(solution)/shard_map/placement/pallas_call | solution.py:197
  15.7 0.0 collective-permute-done.4.refs_2_
  15.7 0.0 collective-permute-done.5.refs_3_
  15.7 2.1 %pack_first.1 = bf16[2048,128]{1,0:T(8,128)(2,1)} custom-call(bf16[2048,1024]{1,0:T(8,128)(2,1)S(1)} %get-tuple-element.11.pick, s32[1,1024]{1,0:T(1,128)S(1)} %bitcast.44, bf16[82,1024]{1,0:T(8,128)(2,1)S(1)} %get-tuple-element.15.refs_0_, bf16[82,1024]{1,0:T(8,128)(2,1)S(1)} %collective-permute-done.3.refs_1_, ...), custom_call_target="tpu_custom_call" | custom-call | flops 4294967296 | bytes 33554432 | tf_op jit(solution)/shard_map/pack_first/pallas_call | solution.py:233
  17.8 14.7 %all-to-all-start.1 = ((bf16[64,32,128]{2,1,0:T(8,128)(2,1)}), bf16[64,32,128]{2,1,0:T(8,128)(2,1)S(1)}, u32[]{:S(2)}, u32[]{:S(2)}) async-start(bf16[64,32,128]{2,1,0:T(8,128)(2,1)} %bitcast.21), calls=%async_computation.1 | async-start | bytes 1048576 | tf_op jit(solution)/shard_map/route_first/all_to_all | solution.py:228
  32.5 0.0 collective-permute-done.refs_1_
  32.5 0.0 collective-permute-done.1.refs_2_
  32.5 4.2 %collective-permute-done.2.refs_3_ = bf16[256,1024]{1,0:T(8,128)(2,1)S(1)} collective-permute-done((bf16[256,1024]{1,0:T(8,128)(2,1)}, bf16[256,1024]{1,0:T(8,128)(2,1)S(1)}, u32[]{:S(2)}, u32[]{:S(2)}) %collective-permute-start.2) | collective-permute-done | bytes 524320 | tf_op jit(solution)/shard_map/pole_exchange_second/ppermute | solution.py:187
  36.7 2.4 %pack_second.1 = bf16[2048,256]{1,0:T(8,128)(2,1)} custom-call(s32[1,1024]{1,0:T(1,128)S(1)} %get-tuple-element.9.where, bf16[256,1024]{1,0:T(8,128)(2,1)S(1)} %get-tuple-element.20.refs_0_, bf16[256,1024]{1,0:T(8,128)(2,1)S(1)} %collective-permute-done.refs_1_, bf16[256,1024]{1,0:T(8,128)(2,1)S(1)} %collective-permute-done.1.refs_2_, ...), custom_call_target="tpu_custom_call" | custom-call | flops 107374182400 | bytes 419430400 | tf_op jit(solution)/shard_map/pack_second/pallas_call | solution.py:244
  39.1 11.1 %all-to-all-done.1 = bf16[64,32,128]{2,1,0:T(8,128)(2,1)S(1)} async-done(((bf16[64,32,128]{2,1,0:T(8,128)(2,1)}), bf16[64,32,128]{2,1,0:T(8,128)(2,1)S(1)}, u32[]{:S(2)}, u32[]{:S(2)}) %all-to-all-start.1) | async-done | bytes 524320 | tf_op jit(solution)/shard_map/route_first/all_to_all | solution.py:228
  50.2 0.0 copy-start
  50.2 0.8 copy-done
  51.0 5.7 %all-to-all-start = ((bf16[64,32,256]{2,1,0:T(8,128)(2,1)}), bf16[64,32,256]{2,1,0:T(8,128)(2,1)S(1)}, u32[]{:S(2)}, u32[]{:S(2)}) async-start(bf16[64,32,256]{2,1,0:T(8,128)(2,1)} %bitcast.10), calls=%async_computation | async-start | bytes 2097152 | tf_op jit(solution)/shard_map/route_second/all_to_all | solution.py:228
  56.7 0.0 copy-start.4
  56.7 2.9 %copy.11.deriv = bf16[1024,1014]{1,0:T(8,128)(2,1)S(1)} copy(bf16[1024,1014]{0,1:T(8,128)(2,1)} %param.8) | data formatting | bytes 4153344 | tf_op args[3]
  59.6 1.3 %align_derivatives.1 = (bf16[3,1024,256]{2,1,0:T(8,128)(2,1)S(1)}, bf16[3,1024,128]{2,1,0:T(8,128)(2,1)S(1)}) custom-call(bf16[1024,1014]{1,0:T(8,128)(2,1)S(1)} %copy.11.deriv), custom_call_target="tpu_custom_call" | custom-call | flops 2076672 | bytes 4153344 | tf_op jit(solution)/shard_map/align_derivatives/pallas_call | solution.py:209
  60.9 0.0 copy-start.2
  60.9 1.2 %copy-done.2 = bf16[3,1024,256]{2,1,0:T(8,128)(2,1)} copy-done((bf16[3,1024,256]{2,1,0:T(8,128)(2,1)}, bf16[3,1024,256]{2,1,0:T(8,128)(2,1)S(1)}, u32[]{:S(2)}) %copy-start.2) | copy-done | bytes 1572888
  62.1 0.0 copy-done.4
  62.1 0.0 copy-start.1
  62.1 1.0 copy-done.1
  63.2 2.3 %contract_first.1.info = f32[8,2048]{1,0:T(8,128)S(1)} custom-call(bf16[2048,128]{1,0:T(8,128)(2,1)S(1)} %bitcast.41, bf16[3,1024,128]{2,1,0:T(8,128)(2,1)S(1)} %get-tuple-element.12.deriv, s32[2,1024]{1,0:T(2,128)S(1)} %copy-done.4), custom_call_target="tpu_custom_call" | custom-call | flops 536870912 | bytes 4194304 | tf_op jit(solution)/shard_map/contract_first/pallas_call | solution.py:254
  65.5 19.2 %all-to-all-done = bf16[64,32,256]{2,1,0:T(8,128)(2,1)S(1)} async-done(((bf16[64,32,256]{2,1,0:T(8,128)(2,1)}), bf16[64,32,256]{2,1,0:T(8,128)(2,1)S(1)}, u32[]{:S(2)}, u32[]{:S(2)}) %all-to-all-start) | async-done | bytes 1048608 | tf_op jit(solution)/shard_map/route_second/all_to_all | solution.py:228
  84.7 0.0 copy-start.3
  84.7 1.4 %copy-done.3 = bf16[3,1024,256]{2,1,0:T(8,128)(2,1)S(1)} copy-done((bf16[3,1024,256]{2,1,0:T(8,128)(2,1)S(1)}, bf16[3,1024,256]{2,1,0:T(8,128)(2,1)}, u32[]{:S(2)}) %copy-start.3) | copy-done | bytes 1572888
  86.1 4.3 %contract_and_scatter.1 = bf16[256,384]{1,0:T(8,128)(2,1)S(1)} custom-call(bf16[2048,256]{1,0:T(8,128)(2,1)S(1)} %bitcast.40, bf16[3,1024,256]{2,1,0:T(8,128)(2,1)S(1)} %copy-done.3, f32[8,2048]{1,0:T(8,128)S(1)} %contract_first.1.info), custom_call_target="tpu_custom_call" | custom-call | flops 1073741824 | bytes 4194304 | tf_op jit(solution)/shard_map/contract_and_scatter/pallas_call | solution.py:262
  90.4 0.1 copy.12
  90.5 0.2 copy.13
  90.7 23.6 %all_to_all.15 = bf16[256,3,128]{2,1,0:T(4,128)(2,1)S(1)} all-to-all(bf16[256,3,128]{2,1,0:T(4,128)(2,1)S(1)} %copy.13), channel_id=1, replica_groups=mesh['pole'=4,'node'=64] {'pole','node'}, dimensions={0} | all-to-all | bytes 393216 | tf_op jit(solution)/shard_map/force_exchange/all_to_all | solution.py:272
  114.3 0.9 convert_reduce_fusion
Async XLA Ops:
  1.9 10.6 %collective-permute-start.3 = (bf16[82,1024]{1,0:T(8,128)(2,1)S(1)}, bf16[82,1024]{1,0:T(8,128)(2,1)S(1)}, u32[]{:S(2)}, u32[]{:S(2)}) collective-permute-start(bf16[82,1024]{1,0:T(8,128)(2,1)S(1)} %get-tuple-element.14), channel_id=1, source_target_pairs={{0,64},{64,128},{128,192},{192,0},{1,65},{65,129},{129,193},{193,1... | collective-permute-start | bytes 503816 | tf_op jit(solution)/shard_map/pole_exchange_first/ppermute | solution.py:187
  4.0 11.6 %collective-permute-start.4 = (bf16[82,1024]{1,0:T(8,128)(2,1)}, bf16[82,1024]{1,0:T(8,128)(2,1)S(1)}, u32[]{:S(2)}, u32[]{:S(2)}) collective-permute-start(bf16[82,1024]{1,0:T(8,128)(2,1)} %get-tuple-element.16), channel_id=1, source_target_pairs={{0,192},{64,0},{128,64},{192,128},{1,193},{65,1},{129,65},{193,129... | collective-permute-start | bytes 503816 | tf_op jit(solution)/shard_map/pole_exchange_first/ppermute | solution.py:187
  5.5 10.2 %collective-permute-start.5 = (bf16[82,1024]{1,0:T(8,128)(2,1)S(1)}, bf16[82,1024]{1,0:T(8,128)(2,1)S(1)}, u32[]{:S(2)}, u32[]{:S(2)}) collective-permute-start(bf16[82,1024]{1,0:T(8,128)(2,1)S(1)} %get-tuple-element.13), channel_id=1, source_target_pairs={{0,128},{64,192},{128,0},{192,64},{1,129},{65,193},{129,1},{193,65... | collective-permute-start | bytes 503816 | tf_op jit(solution)/shard_map/pole_exchange_first/ppermute | solution.py:187
  9.8 22.6 %collective-permute-start = (bf16[256,1024]{1,0:T(8,128)(2,1)}, bf16[256,1024]{1,0:T(8,128)(2,1)S(1)}, u32[]{:S(2)}, u32[]{:S(2)}) collective-permute-start(bf16[256,1024]{1,0:T(8,128)(2,1)} %get-tuple-element.19), channel_id=1, source_target_pairs={{0,64},{64,128},{128,192},{192,0},{1,65},{65,129},{129,193},{193,1... | collective-permute-start | bytes 1572872 | tf_op jit(solution)/shard_map/pole_exchange_second/ppermute | solution.py:187
  10.2 22.2 %collective-permute-start.1 = (bf16[256,1024]{1,0:T(8,128)(2,1)}, bf16[256,1024]{1,0:T(8,128)(2,1)S(1)}, u32[]{:S(2)}, u32[]{:S(2)}) collective-permute-start(bf16[256,1024]{1,0:T(8,128)(2,1)} %get-tuple-element.18), channel_id=1, source_target_pairs={{0,192},{64,0},{128,64},{192,128},{1,193},{65,1},{129,65},{193,129... | collective-permute-start | bytes 1572872 | tf_op jit(solution)/shard_map/pole_exchange_second/ppermute | solution.py:187
  12.5 24.2 %collective-permute-start.2 = (bf16[256,1024]{1,0:T(8,128)(2,1)}, bf16[256,1024]{1,0:T(8,128)(2,1)S(1)}, u32[]{:S(2)}, u32[]{:S(2)}) collective-permute-start(bf16[256,1024]{1,0:T(8,128)(2,1)} %get-tuple-element.17), channel_id=1, source_target_pairs={{0,128},{64,192},{128,0},{192,64},{1,129},{65,193},{129,1},{193,65... | collective-permute-start | bytes 1572872 | tf_op jit(solution)/shard_map/pole_exchange_second/ppermute | solution.py:187
  17.8 32.4 %all-to-all-start.1 = ((bf16[64,32,128]{2,1,0:T(8,128)(2,1)}), bf16[64,32,128]{2,1,0:T(8,128)(2,1)S(1)}, u32[]{:S(2)}, u32[]{:S(2)}) async-start(bf16[64,32,128]{2,1,0:T(8,128)(2,1)} %bitcast.21), calls=%async_computation.1 | async-start | bytes 1048576 | tf_op jit(solution)/shard_map/route_first/all_to_all | solution.py:228
  50.2 0.8 copy-start
  51.0 33.7 %all-to-all-start = ((bf16[64,32,256]{2,1,0:T(8,128)(2,1)}), bf16[64,32,256]{2,1,0:T(8,128)(2,1)S(1)}, u32[]{:S(2)}, u32[]{:S(2)}) async-start(bf16[64,32,256]{2,1,0:T(8,128)(2,1)} %bitcast.10), calls=%async_computation | async-start | bytes 2097152 | tf_op jit(solution)/shard_map/route_second/all_to_all | solution.py:228
  56.7 5.4 %copy-start.4 = (s32[2,1024]{1,0:T(2,128)S(1)}, s32[2,1024]{1,0:T(2,128)}, u32[]{:S(2)}) copy-start(s32[2,1024]{1,0:T(2,128)} %atoms.1) | copy-start | bytes 24580
  60.9 1.2 %copy-start.2 = (bf16[3,1024,256]{2,1,0:T(8,128)(2,1)}, bf16[3,1024,256]{2,1,0:T(8,128)(2,1)S(1)}, u32[]{:S(2)}) copy-start(bf16[3,1024,256]{2,1,0:T(8,128)(2,1)S(1)} %get-tuple-element.10.deriv) | copy-start | bytes 4718596
  62.1 1.0 copy-start.1
  84.7 1.4 %copy-start.3 = (bf16[3,1024,256]{2,1,0:T(8,128)(2,1)S(1)}, bf16[3,1024,256]{2,1,0:T(8,128)(2,1)}, u32[]{:S(2)}) copy-start(bf16[3,1024,256]{2,1,0:T(8,128)(2,1)} %copy-done.2) | copy-start | bytes 4718596

commit v3 on v2

--- a/solution.py
+++ b/solution.py
@@ -27,26 +27,31 @@
 
 
 def one_hot(row, start, rows):
-    found = iota((rows, row.shape[1]), 0) + start == row
-    return jnp.where(found, 1.0, 0.0).astype(BF16)
+    line = lax.broadcasted_iota(jnp.int16, (rows, row.shape[1]), 0)
+    found = line == (row - start).astype(jnp.int16)
+    return jnp.where(found, jnp.ones((), BF16), jnp.zeros((), BF16))
 
 
 def rows_times(a, b):
     return lax.dot_general(a, b, (((1,), (1,)), ((), ())), preferred_element_type=F32)
 
 
-def plan_kernel(capacity, node_row, node_col, pick, where):
+def plan_kernel(capacity, nodes, pole, node, slot, pick, where, slot_row):
     slots, blocks = pick.shape
+    here = pole[0]
+    slot_row[...] = slot[pl.ds(here, 1), :]
+    row = node[pl.ds(here, 1), :]
     tile = min(256, blocks)
-    row = node_row[...]
-    rank = jnp.zeros((1, blocks), F32)
+    earlier = jnp.where(iota((tile, tile), 0) < iota((tile, tile), 1), 1.0, 0.0).astype(BF16)
+    seen = jnp.zeros((nodes, 1), F32)
     for start in range(0, blocks, tile):
-        col = node_col[start : start + tile, :]
-        earlier = iota((tile, blocks), 0) + start < iota((tile, blocks), 1)
-        same = jnp.where((col == row) & earlier, 1.0, 0.0)
-        rank = rank + jnp.sum(same, axis=0, keepdims=True)
-    place = row * capacity + rank.astype(jnp.int32)
-    where[...] = place
+        part = row[:, start : start + tile]
+        same = jnp.where(iota((nodes, tile), 0) == part, 1.0, 0.0)
+        before = jnp.dot(same.astype(BF16), earlier, preferred_element_type=F32) + seen
+        rank = jnp.sum(same * before, axis=0, keepdims=True).astype(jnp.int32)
+        where[:, start : start + tile] = part * capacity + rank
+        seen = seen + jnp.sum(same, axis=1, keepdims=True)
+    place = where[...]
     for start in range(0, slots, tile):
         pick[start : start + tile, :] = one_hot(place, start, tile)
 
@@ -73,7 +78,7 @@
 
 
 def pack_first_kernel(pick, slot_row, *refs):
-    *parts, out, dens = refs
+    *parts, out, dens, rows, sem = refs
     columns = parts[0].shape[0]
     wide = dens.shape[0]
     slot = slot_row[...]
@@ -82,20 +87,31 @@
     dens[columns : columns + 1, :] = (slot // BASE + 1).astype(F32)
     dens[columns + 1 : columns + 2, :] = (slot % BASE).astype(F32)
     total = dens[...].astype(BF16)
-    tile = min(256, out.shape[0])
-    for start in range(0, out.shape[0], tile):
-        rows = pick[start : start + tile, :]
-        out[start : start + tile, :] = rows_times(rows, total).astype(BF16)
-
-
-def pack_second_kernel(where, *refs):
-    *parts, out = refs
+    tile = min(512, rows.shape[0])
+    copies = []
+    for start in range(0, rows.shape[0], tile):
+        part = pl.ds(start, tile)
+        rows[part, :] = rows_times(pick[part, :], total).astype(BF16)
+        copies.append(
+            pltpu.make_async_copy(rows.at[part, :], out.at[part, :], sem.at[start // tile])
+        )
+        copies[-1].start()
+    for copy in copies:
+        copy.wait()
+
+
+def pack_second_kernel(capacity, core, where, *refs):
+    *parts, same, other = refs
     total = pole_total(parts).astype(BF16)
     place = where[...]
-    tile = min(256, out.shape[0])
-    for start in range(0, out.shape[0], tile):
-        rows = one_hot(place, start, tile)
-        out[start : start + tile, :] = rows_times(rows, total).astype(BF16)
+    block, rank = place // capacity, place % capacity
+    row = block // 2 * capacity + rank
+    tile = min(512, same.shape[0])
+    for out, whose in ((other, 1 - core[0]), (same, core[0])):
+        wanted = jnp.where(block % 2 == whose, row, -1)
+        for start in range(0, out.shape[0], tile):
+            rows = one_hot(wanted, start, tile)
+            out[start : start + tile, :] = rows_times(rows, total).astype(BF16)
 
 
 def row_terms(dens, deriv, start):
@@ -113,7 +129,7 @@
     return terms
 
 
-def contract_first_kernel(columns, arrived, deriv, atoms, info):
+def contract_first_kernel(columns, capacity, core, arrived, deriv, atoms, info):
     blocks = atoms.shape[1]
     slots, wide = arrived.shape
     line = iota((8, wide), 0)
@@ -121,7 +137,11 @@
     coded = rows_times(picker.astype(BF16), arrived[...])
     slot_row = (coded[0:1, :] - 1.0) * BASE + coded[1:2, :]
     info[...] = jnp.zeros_like(info)
-    info[3:4, :] = slot_row
+    line = jnp.broadcast_to(slot_row, info.shape)
+    ahead = pltpu.roll(line, slots - capacity, 1)
+    behind = pltpu.roll(line, capacity, 1)
+    swapped = jnp.where(iota(info.shape, 1) % (2 * capacity) < capacity, ahead, behind)
+    info[3:4, :] = jnp.where(core[0] == 0, line, swapped)[0:1, :]
     info[4:6, :blocks] = atoms[...].astype(F32)
     slot_row = slot_row.astype(jnp.int32)
     tile = min(256, blocks)
@@ -133,15 +153,23 @@
             info[c : c + 1, start : start + tile] = term
 
 
-def force_kernel(arrived, deriv, info, out, total):
+def force_kernel(arrived, source, info, out, total, deriv, sem):
     blocks = deriv.shape[1]
-    owners = out.shape[0]
+    owners = out.shape[1]
     slot_row = info[3:4, :].astype(jnp.int32)
-    tile = min(256, blocks)
+    tile = min(512, blocks)
+    copies = []
+    for i in range(blocks // tile):
+        rows = pl.ds(i * tile, tile)
+        copies.append(
+            pltpu.make_async_copy(source.at[:, rows, :], deriv.at[:, rows, :], sem.at[i])
+        )
+        copies[i].start()
     for start in range(0, blocks, tile):
         dens = jnp.dot(
             one_hot(slot_row, start, tile), arrived[...], preferred_element_type=F32
         )
+        copies[start // tile].wait()
         terms = row_terms(dens, deriv, start)
         added = None
         for e, sign in ((0, -2.0), (1, 2.0)):
@@ -158,7 +186,8 @@
             total[...] = added
         else:
             total[...] += added
-    out[...] = total[...].astype(BF16)
+    for c in range(3):
+        out[c] = total[:, c * ATOM_DEV : (c + 1) * ATOM_DEV].astype(BF16)
 
 
 def body(dens_part, dest_node, pair_slot, deriv, pair_atoms):
@@ -185,25 +214,30 @@
         for step in (1, 3, 2):
             pairs = [(k, (k + step) % poles) for k in range(poles)]
             parts.append(lax.ppermute(share(step), "pole", pairs))
-        return [share(0)] + parts
+        return parts
 
     with jax.named_scope("pole_exchange_first"):
         parts_first = exchange(split, last)
+        parts_first.append(
+            lax.dynamic_slice(partials, (split, pole * blocks), (last, blocks))
+        )
     with jax.named_scope("pole_exchange_second"):
         parts_second = exchange(0, split)
 
-    target_node = lax.dynamic_slice_in_dim(dest_node, pole * blocks, blocks, 0)
-    target_slot = lax.dynamic_slice_in_dim(pair_slot, pole * blocks, blocks, 0)
-    pick_out, place = pl.pallas_call(
-        functools.partial(plan_kernel, capacity),
+    whole = pl.BlockSpec(memory_space=pltpu.VMEM)
+    scalar = pl.BlockSpec(memory_space=pltpu.SMEM)
+    pick_out, place, slot_row = pl.pallas_call(
+        functools.partial(plan_kernel, capacity, nodes),
+        in_specs=[scalar, whole, whole],
         out_shape=[
             jax.ShapeDtypeStruct((slots, blocks), BF16),
             jax.ShapeDtypeStruct((1, blocks), jnp.int32),
+            jax.ShapeDtypeStruct((1, blocks), jnp.int32),
         ],
         compiler_params=params(),
         cost_estimate=cost(6 * blocks * blocks, 2 * slots * blocks),
         name="placement",
-    )(target_node.reshape(1, blocks), target_node.reshape(blocks, 1))
+    )(pole.reshape(1), dest_node.reshape(poles, blocks), pair_slot.reshape(poles, blocks))
 
     tile = min(256, blocks)
     deriv_second, deriv_first = pl.pallas_call(
@@ -215,7 +249,7 @@
             pl.BlockSpec((3, tile, wide), lambda i: (0, i, 0)),
         ],
         out_shape=[
-            jax.ShapeDtypeStruct((3, blocks, split), BF16),
+            pltpu.HBM((3, blocks, split), BF16),
             jax.ShapeDtypeStruct((3, blocks, wide), BF16),
         ],
         compiler_params=params(),
@@ -233,44 +267,71 @@
     packed_first = pl.pallas_call(
         pack_first_kernel,
         out_shape=jax.ShapeDtypeStruct((slots, wide), BF16),
-        scratch_shapes=[pltpu.VMEM((wide, blocks), F32)],
+        out_specs=pl.BlockSpec(memory_space=pltpu.HBM),
+        scratch_shapes=[
+            pltpu.VMEM((wide, blocks), F32),
+            pltpu.VMEM((slots, wide), BF16),
+            pltpu.SemaphoreType.DMA((max(1, slots // 512),)),
+        ],
         compiler_params=params(),
         cost_estimate=cost(16 * slots * blocks * wide, 16 * slots * blocks),
         name="pack_first",
-    )(pick_out, target_slot.reshape(1, blocks), *parts_first)
+    )(pick_out, slot_row, *parts_first)
+    with jax.named_scope("pole_exchange_second"):
+        later, packed_first = lax.optimization_barrier((partials, packed_first))
+        parts_second.append(
+            lax.dynamic_slice(later, (0, pole * blocks), (split, blocks))
+        )
     with jax.named_scope("route_first"):
         arrived_first = route(packed_first)
 
-    packed_second = pl.pallas_call(
-        pack_second_kernel,
-        out_shape=jax.ShapeDtypeStruct((slots, split), BF16),
+    core = lax.rem(lax.axis_index("node"), 2)
+    half = jax.ShapeDtypeStruct((slots // 2, split), BF16)
+    same_core, other_core = pl.pallas_call(
+        functools.partial(pack_second_kernel, capacity),
+        in_specs=[scalar] + [whole] * (1 + len(parts_second)),
+        out_shape=[half, half],
         compiler_params=params(),
         cost_estimate=cost(200 * slots * blocks * split, 200 * slots * blocks),
         name="pack_second",
-    )(place, *parts_second)
+    )(core.reshape(1), place, *parts_second)
     with jax.named_scope("route_second"):
-        arrived_second = route(packed_second)
+        sibling = lax.ppermute(other_core, "node", [(k, k ^ 1) for k in range(nodes)])
+        chips = nodes // 2
+        both = jnp.concatenate(
+            [x.reshape(chips, capacity, split) for x in (same_core, sibling)], axis=1
+        )
+        groups = [list(range(c, nodes, 2)) for c in range(2)]
+        arrived_second = lax.all_to_all(
+            both, "node", 0, 0, axis_index_groups=groups, tiled=True
+        ).reshape(slots, split)
 
     info = pl.pallas_call(
-        functools.partial(contract_first_kernel, last),
+        functools.partial(contract_first_kernel, last, capacity),
+        in_specs=[scalar, whole, whole, whole],
         out_shape=jax.ShapeDtypeStruct((8, slots), F32),
         compiler_params=params(),
         cost_estimate=cost(2 * slots * blocks * wide, 2 * slots * blocks),
         name="contract_first",
-    )(arrived_first, deriv_first, pair_atoms)
+    )(core.reshape(1), arrived_first, deriv_first, pair_atoms)
 
     partial_forces = pl.pallas_call(
         force_kernel,
-        out_shape=jax.ShapeDtypeStruct((owners, 3 * ATOM_DEV), BF16),
-        scratch_shapes=[pltpu.VMEM((owners, 3 * ATOM_DEV), F32)],
+        in_specs=[whole, pl.BlockSpec(memory_space=pltpu.HBM), whole],
+        out_shape=jax.ShapeDtypeStruct((3, owners, ATOM_DEV), BF16),
+        scratch_shapes=[
+            pltpu.VMEM((owners, 3 * ATOM_DEV), F32),
+            pltpu.VMEM((3, blocks, split), BF16),
+            pltpu.SemaphoreType.DMA((max(1, blocks // 512),)),
+        ],
         compiler_params=params(),
         cost_estimate=cost(2 * slots * blocks * split, 2 * slots * blocks),
         name="contract_and_scatter",
-    )(arrived_second, deriv_second, info)
+    )(arrived_second, pltpu.with_memory_space_constraint(deriv_second, pltpu.HBM), info)
 
     with jax.named_scope("force_exchange"):
         gathered = lax.all_to_all(
-            partial_forces.reshape(owners, 3, ATOM_DEV), ("pole", "node"), 0, 0, tiled=True
+            jnp.transpose(partial_forces, (1, 0, 2)), ("pole", "node"), 0, 0, tiled=True
         )
         return jnp.sum(gathered.astype(F32), axis=0)
 

time: 116 us -> 111 us (0.957)
  local copies, waits for them, and re-layouts: 13.9 us -> 9.19 us
  waiting for transfers between devices: 34.6 us -> 32.1 us
  blocking collectives: 23.6 us -> 25.2 us
  starting transfers between devices: 28.4 us -> 29.7 us
    all_to_all x2 -> x1, waiting for transfers between devices: 30.3 us -> 5.89 us  [route(): lax.all_to_all(packed.reshape(nodes, capacity, columns), 'node', 0, 0, ti...]
    all_to_all x0 -> x1, waiting for transfers between devices: none -> 18.5 us  [body(): lax.all_to_all(both, 'node', 0, 0, axis_index_groups=groups, tiled=True)]
    all_to_all x2 -> x1, starting transfers between devices: 20.4 us -> 14.4 us  [route(): lax.all_to_all(packed.reshape(nodes, capacity, columns), 'node', 0, 0, ti...]
    all_to_all x0 -> x1, starting transfers between devices: none -> 5.32 us  [body(): lax.all_to_all(both, 'node', 0, 0, axis_index_groups=groups, tiled=True)]
    unnamed x11, local copies, waits for them, and re-layouts: 7.3 us -> 3.68 us
    dynamic_slice x2 -> x1, local copies, waits for them, and re-layouts: 4.63 us -> 2.29 us  [share(): return lax.dynamic_slice(partials, (first_column, start), (columns, blocks))]
    pallas_call x4, Pallas kernels: 10.4 us -> 8.33 us  [the longest x1 3.96 us: body(): pl.pallas_call(force_kernel, in_specs=[whole, pl.BlockSpec(memory_space=p...]
    ppermute x6, waiting for transfers between devices: 4.26 us -> 6.13 us  [exchange(): parts.append(lax.ppermute(share(step), 'pole', pairs))]
  transfers between devices with their start and end apart: 8 -> 9, of which waited for: 3 -> 5; matrix products, arithmetic and copies ran while one was open for 6% -> 7% of each run, Pallas kernels for 8% -> 8%
where the time goes in v3:
time: 111 us
  waiting for transfers between devices  32.1 us (29%)
  starting transfers between devices  29.7 us (27%)
  blocking collectives  25.2 us (23%)
  Pallas kernels  12.8 us (12%)
  local copies, waits for them, and re-layouts  9.19 us (8%)
  other arithmetic  1.93 us (2%)
    all_to_all x1, blocking collectives, body(): lax.all_to_all(jnp.transpose(partial_forces, (1, 0, 2)), ('pole', 'node')...  25.2 us
    all_to_all x1, waiting for transfers between devices, body(): lax.all_to_all(both, 'node', 0, 0, axis_index_groups=groups, tiled=True)  18.5 us
    all_to_all x1, starting transfers between devices, route(): lax.all_to_all(packed.reshape(nodes, capacity, columns), 'node', 0, 0, ti...  14.4 us
    ppermute x6, starting transfers between devices, exchange(): parts.append(lax.ppermute(share(step), 'pole', pairs))  8.09 us
    ppermute x6, waiting for transfers between devices, exchange(): parts.append(lax.ppermute(share(step), 'pole', pairs))  6.13 us
    all_to_all x1, waiting for transfers between devices, route(): lax.all_to_all(packed.reshape(nodes, capacity, columns), 'node', 0, 0, ti...  5.89 us
    all_to_all x1, starting transfers between devices, body(): lax.all_to_all(both, 'node', 0, 0, axis_index_groups=groups, tiled=True)  5.32 us
    pallas_call x1, Pallas kernels, body(): pl.pallas_call(force_kernel, in_specs=[whole, pl.BlockSpec(memory_space=p...  3.96 us
  transfers between devices with their start and end apart: 9, of which 5 were waited for; matrix products, arithmetic and copies ran while one was open for 7% of the time, Pallas kernels for 8%

profile of v3, /device:TPU:1, one launch (start us, length us, event | category | flops | bytes accessed | tf_op | source)
XLA Modules:
  0.0 110.9 jit_solution(9744527752301541107)
XLA Ops:
  0.0 0.0 copy-start.3
  0.0 0.0 copy-start.4
  0.0 1.9 %dynamic-slice_bitcast_fusion.3 = (bf16[82,1024]{1,0:T(8,128)(2,1)S(1)}, bf16[82,1024]{1,0:T(8,128)(2,1)}, bf16[82,1024]{1,0:T(8,128)(2,1)S(1)}, bf16[82,1024]{1,0:T(8,128)(2,1)S(1)}) fusion(bf16[1,4096,338]{1,2,0:T(8,128)(2,1)} %param.5, s32[]{:T(128)S(6)} %select_n.19, s32[]{:T(128)S(6)} %select_n.17, s32[]{:T(128)S(6)} %select_n.16, s32[]{:T(128)S(6)} %select_n.18), kind=kLoop, calls=%fused_computation.5 | loop fusion | bytes 1343504 | tf_op jit(solution)/shard_map/pole_exchange_first/dynamic_slice | solution.py:222
  2.0 2.1 %collective-permute-start.3 = (bf16[82,1024]{1,0:T(8,128)(2,1)S(1)}, bf16[82,1024]{1,0:T(8,128)(2,1)S(1)}, u32[]{:S(2)}, u32[]{:S(2)}) collective-permute-start(bf16[82,1024]{1,0:T(8,128)(2,1)S(1)} %get-tuple-element.25), channel_id=1, source_target_pairs={{0,64},{64,128},{128,192},{192,0},{1,65},{65,129},{129,193},{193,1... | collective-permute-start | bytes 503816 | tf_op jit(solution)/shard_map/pole_exchange_first/ppermute | solution.py:216
  4.1 1.4 %collective-permute-start.4 = (bf16[82,1024]{1,0:T(8,128)(2,1)}, bf16[82,1024]{1,0:T(8,128)(2,1)S(1)}, u32[]{:S(2)}, u32[]{:S(2)}) collective-permute-start(bf16[82,1024]{1,0:T(8,128)(2,1)} %get-tuple-element.24), channel_id=1, source_target_pairs={{0,192},{64,0},{128,64},{192,128},{1,193},{65,1},{129,65},{193,129... | collective-permute-start | bytes 503816 | tf_op jit(solution)/shard_map/pole_exchange_first/ppermute | solution.py:216
  5.5 1.6 %collective-permute-start.5 = (bf16[82,1024]{1,0:T(8,128)(2,1)S(1)}, bf16[82,1024]{1,0:T(8,128)(2,1)S(1)}, u32[]{:S(2)}, u32[]{:S(2)}) collective-permute-start(bf16[82,1024]{1,0:T(8,128)(2,1)S(1)} %get-tuple-element.26), channel_id=1, source_target_pairs={{0,128},{64,192},{128,0},{192,64},{1,129},{65,193},{129,1},{193,65... | collective-permute-start | bytes 503816 | tf_op jit(solution)/shard_map/pole_exchange_first/ppermute | solution.py:216
  7.2 2.3 %dynamic-slice_bitcast_fusion = (bf16[256,1024]{1,0:T(8,128)(2,1)S(1)}, bf16[256,1024]{1,0:T(8,128)(2,1)S(1)}, bf16[256,1024]{1,0:T(8,128)(2,1)}) fusion(bf16[1,4096,338]{1,2,0:T(8,128)(2,1)} %param.5, s32[]{:T(128)S(6)} %select_n.18, s32[]{:T(128)S(6)} %select_n.17, s32[]{:T(128)S(6)} %select_n.16), kind=kLoop, calls=%fused_computation.2 | loop fusion | bytes 3145740 | tf_op jit(solution)/shard_map/pole_exchange_second/dynamic_slice | solution.py:211
  9.4 0.4 collective-permute-start
  9.8 2.3 %collective-permute-start.1 = (bf16[256,1024]{1,0:T(8,128)(2,1)S(1)}, bf16[256,1024]{1,0:T(8,128)(2,1)S(1)}, u32[]{:S(2)}, u32[]{:S(2)}) collective-permute-start(bf16[256,1024]{1,0:T(8,128)(2,1)S(1)} %get-tuple-element.28), channel_id=1, source_target_pairs={{0,192},{64,0},{128,64},{192,128},{1,193},{65,1},{129,65},{193,129... | collective-permute-start | bytes 1572872 | tf_op jit(solution)/shard_map/pole_exchange_second/ppermute | solution.py:216
  12.1 0.0 copy-done.3
  12.1 0.0 copy-done.4
  12.2 0.7 placement.1
  12.9 0.0 collective-permute-done.3.refs_0_
  12.9 0.2 collective-permute-start.2
  13.1 0.0 collective-permute-done.4.refs_1_
  13.1 1.2 %collective-permute-done.5.refs_2_ = bf16[82,1024]{1,0:T(8,128)(2,1)S(1)} collective-permute-done((bf16[82,1024]{1,0:T(8,128)(2,1)S(1)}, bf16[82,1024]{1,0:T(8,128)(2,1)S(1)}, u32[]{:S(2)}, u32[]{:S(2)}) %collective-permute-start.5) | collective-permute-done | bytes 167968 | tf_op jit(solution)/shard_map/pole_exchange_first/ppermute | solution.py:216
  14.3 2.0 %pack_first.1 = bf16[2048,128]{1,0:T(8,128)(2,1)} custom-call(bf16[2048,1024]{1,0:T(8,128)(2,1)S(1)} %get-tuple-element.15.pick, s32[1,1024]{1,0:T(1,128)S(1)} %get-tuple-element.16.slot_row, bf16[82,1024]{1,0:T(8,128)(2,1)S(1)} %collective-permute-done.3.refs_0_, bf16[82,1024]{1,0:T(8,128)(2,1)S(1)} %collective-permute-done.4.refs_1_, ...), custom_call_target="tpu_custom_call" | custom-call | flops 4294967296 | bytes 33554432 | tf_op jit(solution)/shard_map/pack_first/pallas_call | solution.py:267
  16.3 14.4 %all-to-all-start.1 = ((bf16[64,32,128]{2,1,0:T(8,128)(2,1)}), bf16[64,32,128]{2,1,0:T(8,128)(2,1)S(1)}, u32[]{:S(2)}, u32[]{:S(2)}) async-start(bf16[64,32,128]{2,1,0:T(8,128)(2,1)} %bitcast.21), calls=%async_computation.1 | async-start | bytes 1048576 | tf_op jit(solution)/shard_map/route_first/all_to_all | solution.py:262
  30.7 1.1 constant_dynamic-slice_fusion.refs_3_
  31.8 0.0 collective-permute-done.refs_0_
  31.8 0.0 collective-permute-done.1.refs_1_
  31.8 4.9 %collective-permute-done.2.refs_2_ = bf16[256,1024]{1,0:T(8,128)(2,1)S(1)} collective-permute-done((bf16[256,1024]{1,0:T(8,128)(2,1)S(1)}, bf16[256,1024]{1,0:T(8,128)(2,1)S(1)}, u32[]{:S(2)}, u32[]{:S(2)}) %collective-permute-start.2) | collective-permute-done | bytes 524320 | tf_op jit(solution)/shard_map/pole_exchange_second/ppermute | solution.py:216
  36.8 1.3 %pack_second.1 = (bf16[1024,256]{1,0:T(8,128)(2,1)S(1)}, bf16[1024,256]{1,0:T(8,128)(2,1)S(1)}) custom-call(s32[1]{0:T(128)} %bitcast.core, s32[1,1024]{1,0:T(1,128)S(1)} %get-tuple-element.14.where, bf16[256,1024]{1,0:T(8,128)(2,1)S(1)} %collective-permute-done.refs_0_, bf16[256,1024]{1,0:T(8,128)(2,1)S(1)} %collective-permute-done.1.refs_1_, ...), custom_call_target="tpu_custom_call" | custom-call | flops 107374182400 | bytes 419430400 | tf_op jit(solution)/shard_map/pack_second/pallas_call | solution.py:290
  38.1 1.8 %collective-permute-start.6 = (bf16[1024,256]{1,0:T(8,128)(2,1)S(1)}, bf16[1024,256]{1,0:T(8,128)(2,1)S(1)}, u32[]{:S(2)}, u32[]{:S(2)}) collective-permute-start(bf16[1024,256]{1,0:T(8,128)(2,1)S(1)} %get-tuple-element.19), channel_id=1, source_target_pairs={{0,1},{1,0},{2,3},{3,2},{4,5},{5,4},{6,7},{7,6},{8,9},{9,8},{10,11... | collective-permute-start | bytes 1572872 | tf_op jit(solution)/shard_map/route_second/ppermute | solution.py:299
  39.9 1.5 %collective-permute-done.6 = bf16[1024,256]{1,0:T(8,128)(2,1)S(1)} collective-permute-done((bf16[1024,256]{1,0:T(8,128)(2,1)S(1)}, bf16[1024,256]{1,0:T(8,128)(2,1)S(1)}, u32[]{:S(2)}, u32[]{:S(2)}) %collective-permute-start.6) | collective-permute-done | bytes 524320 | tf_op jit(solution)/shard_map/route_second/ppermute | solution.py:299
  41.5 1.1 pad_maximum_fusion
  42.5 5.9 %all-to-all-done.1 = bf16[64,32,128]{2,1,0:T(8,128)(2,1)S(1)} async-done(((bf16[64,32,128]{2,1,0:T(8,128)(2,1)}), bf16[64,32,128]{2,1,0:T(8,128)(2,1)S(1)}, u32[]{:S(2)}, u32[]{:S(2)}) %all-to-all-start.1) | async-done | bytes 524320 | tf_op jit(solution)/shard_map/route_first/all_to_all | solution.py:262
  48.4 0.0 copy-start
  48.4 0.8 copy-done
  49.2 5.3 %all-to-all-start = ((bf16[32,64,256]{2,1,0:T(8,128)(2,1)}), bf16[32,64,256]{2,1,0:T(8,128)(2,1)S(1)}, u32[]{:S(2)}, u32[]{:S(2)}) async-start(bf16[32,64,256]{2,1,0:T(8,128)(2,1)} %pad_maximum_fusion), calls=%async_computation | async-start | bytes 2097152 | tf_op jit(solution)/shard_map/route_second/all_to_all | solution.py:305
  54.6 0.0 copy-start.2
  54.6 2.9 %copy.7.deriv = bf16[1024,1014]{1,0:T(8,128)(2,1)S(1)} copy(bf16[1024,1014]{0,1:T(8,128)(2,1)} %param.8) | data formatting | bytes 4153344 | tf_op args[3]
  57.5 0.0 copy-start.1
  57.5 2.4 %align_derivatives.1 = (bf16[3,1024,256]{2,1,0:T(8,128)(2,1)}, bf16[3,1024,128]{2,1,0:T(8,128)(2,1)S(1)}) custom-call(bf16[1024,1014]{1,0:T(8,128)(2,1)S(1)} %copy.7.deriv), custom_call_target="tpu_custom_call" | custom-call | flops 2076672 | bytes 4153344 | tf_op jit(solution)/shard_map/align_derivatives/pallas_call | solution.py:243
  59.9 0.0 copy-done.2
  59.9 0.0 copy-done.1
  59.9 2.3 %contract_first.1.info = f32[8,2048]{1,0:T(8,128)S(1)} custom-call(s32[1]{0:T(128)} %bitcast.core, bf16[2048,128]{1,0:T(8,128)(2,1)S(1)} %bitcast.40, bf16[3,1024,128]{2,1,0:T(8,128)(2,1)S(1)} %get-tuple-element.22.deriv, s32[2,1024]{1,0:T(2,128)S(1)} %copy-done.2), custom_call_target="tpu_custom_call" | custom-call | flops 536870912 | bytes 4194304 | tf_op jit(solution)/shard_map/contract_first/pallas_call | solution.py:309
  62.2 18.5 %all-to-all-done = bf16[32,64,256]{2,1,0:T(8,128)(2,1)S(1)} async-done(((bf16[32,64,256]{2,1,0:T(8,128)(2,1)}), bf16[32,64,256]{2,1,0:T(8,128)(2,1)S(1)}, u32[]{:S(2)}, u32[]{:S(2)}) %all-to-all-start) | async-done | bytes 1048608 | tf_op jit(solution)/shard_map/route_second/all_to_all | solution.py:305
  80.8 4.0 %contract_and_scatter.1 = bf16[3,256,128]{2,1,0:T(8,128)(2,1)S(1)} custom-call(bf16[2048,256]{1,0:T(8,128)(2,1)S(1)} %bitcast.39, bf16[3,1024,256]{2,1,0:T(8,128)(2,1)} %get-tuple-element.20.source, f32[8,2048]{1,0:T(8,128)S(1)} %contract_first.1.info), custom_call_target="tpu_custom_call" | custom-call | flops 1073741824 | bytes 4194304 | tf_op jit(solution)/shard_map/contract_and_scatter/pallas_call | solution.py:318
  84.7 0.2 copy.8
  84.9 25.2 %all_to_all.15 = bf16[256,3,128]{2,1,0:T(4,128)(2,1)S(1)} all-to-all(bf16[256,3,128]{2,1,0:T(4,128)(2,1)S(1)} %copy.8), channel_id=1, replica_groups=mesh['pole'=4,'node'=64] {'pole','node'}, dimensions={0} | all-to-all | bytes 393216 | tf_op jit(solution)/shard_map/force_exchange/all_to_all | solution.py:333
  110.1 0.9 convert_reduce_fusion
  (2 shorter events, 0.0 us)
Async XLA Ops:
  0.0 12.1 %copy-start.3 = (s32[4096]{0:T(1024)S(1)}, s32[4096]{0:T(1024)}, u32[]{:S(2)}) copy-start(s32[4096]{0:T(1024)} %param.6) | copy-start | bytes 49156
  0.0 12.1 %copy-start.4 = (s32[4096]{0:T(1024)S(1)}, s32[4096]{0:T(1024)}, u32[]{:S(2)}) copy-start(s32[4096]{0:T(1024)} %param.7) | copy-start | bytes 49156
  2.0 11.0 %collective-permute-start.3 = (bf16[82,1024]{1,0:T(8,128)(2,1)S(1)}, bf16[82,1024]{1,0:T(8,128)(2,1)S(1)}, u32[]{:S(2)}, u32[]{:S(2)}) collective-permute-start(bf16[82,1024]{1,0:T(8,128)(2,1)S(1)} %get-tuple-element.25), channel_id=1, source_target_pairs={{0,64},{64,128},{128,192},{192,0},{1,65},{65,129},{129,193},{193,1... | collective-permute-start | bytes 503816 | tf_op jit(solution)/shard_map/pole_exchange_first/ppermute | solution.py:216
  4.1 9.0 %collective-permute-start.4 = (bf16[82,1024]{1,0:T(8,128)(2,1)}, bf16[82,1024]{1,0:T(8,128)(2,1)S(1)}, u32[]{:S(2)}, u32[]{:S(2)}) collective-permute-start(bf16[82,1024]{1,0:T(8,128)(2,1)} %get-tuple-element.24), channel_id=1, source_target_pairs={{0,192},{64,0},{128,64},{192,128},{1,193},{65,1},{129,65},{193,129... | collective-permute-start | bytes 503816 | tf_op jit(solution)/shard_map/pole_exchange_first/ppermute | solution.py:216
  5.5 8.8 %collective-permute-start.5 = (bf16[82,1024]{1,0:T(8,128)(2,1)S(1)}, bf16[82,1024]{1,0:T(8,128)(2,1)S(1)}, u32[]{:S(2)}, u32[]{:S(2)}) collective-permute-start(bf16[82,1024]{1,0:T(8,128)(2,1)S(1)} %get-tuple-element.26), channel_id=1, source_target_pairs={{0,128},{64,192},{128,0},{192,64},{1,129},{65,193},{129,1},{193,65... | collective-permute-start | bytes 503816 | tf_op jit(solution)/shard_map/pole_exchange_first/ppermute | solution.py:216
  9.4 22.4 %collective-permute-start = (bf16[256,1024]{1,0:T(8,128)(2,1)}, bf16[256,1024]{1,0:T(8,128)(2,1)S(1)}, u32[]{:S(2)}, u32[]{:S(2)}) collective-permute-start(bf16[256,1024]{1,0:T(8,128)(2,1)} %get-tuple-element.29), channel_id=1, source_target_pairs={{0,64},{64,128},{128,192},{192,0},{1,65},{65,129},{129,193},{193,1... | collective-permute-start | bytes 1572872 | tf_op jit(solution)/shard_map/pole_exchange_second/ppermute | solution.py:216
  9.8 22.0 %collective-permute-start.1 = (bf16[256,1024]{1,0:T(8,128)(2,1)S(1)}, bf16[256,1024]{1,0:T(8,128)(2,1)S(1)}, u32[]{:S(2)}, u32[]{:S(2)}) collective-permute-start(bf16[256,1024]{1,0:T(8,128)(2,1)S(1)} %get-tuple-element.28), channel_id=1, source_target_pairs={{0,192},{64,0},{128,64},{192,128},{1,193},{65,1},{129,65},{193,129... | collective-permute-start | bytes 1572872 | tf_op jit(solution)/shard_map/pole_exchange_second/ppermute | solution.py:216
  12.9 23.9 %collective-permute-start.2 = (bf16[256,1024]{1,0:T(8,128)(2,1)S(1)}, bf16[256,1024]{1,0:T(8,128)(2,1)S(1)}, u32[]{:S(2)}, u32[]{:S(2)}) collective-permute-start(bf16[256,1024]{1,0:T(8,128)(2,1)S(1)} %get-tuple-element.27), channel_id=1, source_target_pairs={{0,128},{64,192},{128,0},{192,64},{1,129},{65,193},{129,1},{193,65... | collective-permute-start | bytes 1572872 | tf_op jit(solution)/shard_map/pole_exchange_second/ppermute | solution.py:216
  16.3 32.1 %all-to-all-start.1 = ((bf16[64,32,128]{2,1,0:T(8,128)(2,1)}), bf16[64,32,128]{2,1,0:T(8,128)(2,1)S(1)}, u32[]{:S(2)}, u32[]{:S(2)}) async-start(bf16[64,32,128]{2,1,0:T(8,128)(2,1)} %bitcast.21), calls=%async_computation.1 | async-start | bytes 1048576 | tf_op jit(solution)/shard_map/route_first/all_to_all | solution.py:262
  38.1 3.4 %collective-permute-start.6 = (bf16[1024,256]{1,0:T(8,128)(2,1)S(1)}, bf16[1024,256]{1,0:T(8,128)(2,1)S(1)}, u32[]{:S(2)}, u32[]{:S(2)}) collective-permute-start(bf16[1024,256]{1,0:T(8,128)(2,1)S(1)} %get-tuple-element.19), channel_id=1, source_target_pairs={{0,1},{1,0},{2,3},{3,2},{4,5},{5,4},{6,7},{7,6},{8,9},{9,8},{10,11... | collective-permute-start | bytes 1572872 | tf_op jit(solution)/shard_map/route_second/ppermute | solution.py:299
  48.4 0.8 copy-start
  49.2 31.5 %all-to-all-start = ((bf16[32,64,256]{2,1,0:T(8,128)(2,1)}), bf16[32,64,256]{2,1,0:T(8,128)(2,1)S(1)}, u32[]{:S(2)}, u32[]{:S(2)}) async-start(bf16[32,64,256]{2,1,0:T(8,128)(2,1)} %pad_maximum_fusion), calls=%async_computation | async-start | bytes 2097152 | tf_op jit(solution)/shard_map/route_second/all_to_all | solution.py:305
  54.6 5.3 %copy-start.2 = (s32[2,1024]{1,0:T(2,128)S(1)}, s32[2,1024]{1,0:T(2,128)}, u32[]{:S(2)}) copy-start(s32[2,1024]{1,0:T(2,128)} %atoms.1) | copy-start | bytes 24580
  57.5 2.5 %copy-start.1 = (bf16[64,32,128]{2,1,0:T(8,128)(2,1)S(1)}, bf16[64,32,128]{2,1,0:T(8,128)(2,1)}, u32[]{:S(2)}) copy-start(bf16[64,32,128]{2,1,0:T(8,128)(2,1)} %copy-done) | copy-start | bytes 1572868

commit v4 on v3

--- a/solution.py
+++ b/solution.py
@@ -123,9 +123,7 @@
         folded = prod[:, :LANES]
         for first in range(LANES, wide, LANES):
             folded = folded + prod[:, first : first + LANES]
-        large = folded.astype(BF16)
-        small = (folded - large.astype(F32)).astype(BF16)
-        terms.append((rows_times(ones, large) + rows_times(ones, small))[0:1, :])
+        terms.append(rows_times(ones, folded.astype(BF16))[0:1, :])
     return terms
 
 
@@ -252,7 +250,7 @@
             pltpu.HBM((3, blocks, split), BF16),
             jax.ShapeDtypeStruct((3, blocks, wide), BF16),
         ],
-        compiler_params=params(),
+        compiler_params=params(60),
         cost_estimate=cost(6 * blocks * width, 4 * blocks * deriv.shape[1]),
         name="align_derivatives",
     )(deriv)

time: 111 us -> 110 us (level)
  waiting for transfers between devices: 32.1 us -> 28.3 us
  local copies, waits for them, and re-layouts: 9.19 us -> 10.6 us
  Pallas kernels: 12.8 us -> 14.1 us
    all_to_all x1, waiting for transfers between devices: 18.5 us -> 14.7 us  [body(): lax.all_to_all(both, 'node', 0, 0, axis_index_groups=groups, tiled=True)]
    pallas_call x1, Pallas kernels: 2.44 us -> 4.37 us  [body(): pl.pallas_call(functools.partial(deriv_kernel, half_width), grid=(blocks...]
    unnamed x11 -> x9, local copies, waits for them, and re-layouts: 3.68 us -> 5.11 us
  transfers between devices with their start and end apart: 9 -> 9, of which waited for: 5 -> 5; matrix products, arithmetic and copies ran while one was open for 7% -> 8% of each run, Pallas kernels for 8% -> 10%
where the time goes in v4:
time: 110 us
  starting transfers between devices  29.6 us (27%)
  waiting for transfers between devices  28.3 us (26%)
  blocking collectives  25.2 us (23%)
  Pallas kernels  14.1 us (13%)
  local copies, waits for them, and re-layouts  10.6 us (10%)
  other arithmetic  1.91 us (2%)
    all_to_all x1, blocking collectives, body(): lax.all_to_all(jnp.transpose(partial_forces, (1, 0, 2)), ('pole', 'node')...  25.2 us
    all_to_all x1, waiting for transfers between devices, body(): lax.all_to_all(both, 'node', 0, 0, axis_index_groups=groups, tiled=True)  14.7 us
    all_to_all x1, starting transfers between devices, route(): lax.all_to_all(packed.reshape(nodes, capacity, columns), 'node', 0, 0, ti...  14.4 us
    ppermute x6, starting transfers between devices, exchange(): parts.append(lax.ppermute(share(step), 'pole', pairs))  8.09 us
    ppermute x6, waiting for transfers between devices, exchange(): parts.append(lax.ppermute(share(step), 'pole', pairs))  6.13 us
    all_to_all x1, waiting for transfers between devices, route(): lax.all_to_all(packed.reshape(nodes, capacity, columns), 'node', 0, 0, ti...  5.92 us
    all_to_all x1, starting transfers between devices, body(): lax.all_to_all(both, 'node', 0, 0, axis_index_groups=groups, tiled=True)  5.29 us
    unnamed x9, local copies, waits for them, and re-layouts  5.11 us
  transfers between devices with their start and end apart: 9, of which 5 were waited for; matrix products, arithmetic and copies ran while one was open for 8% of the time, Pallas kernels for 10%

profile of v4, /device:TPU:1, one launch (start us, length us, event | category | flops | bytes accessed | tf_op | source)
XLA Modules:
  0.0 109.7 jit_solution(15759223492768936581)
XLA Ops:
  0.0 0.0 copy-start.2
  0.0 0.0 copy-start.3
  0.0 1.9 %dynamic-slice_bitcast_fusion.3 = (bf16[82,1024]{1,0:T(8,128)(2,1)S(1)}, bf16[82,1024]{1,0:T(8,128)(2,1)}, bf16[82,1024]{1,0:T(8,128)(2,1)S(1)}, bf16[82,1024]{1,0:T(8,128)(2,1)S(1)}) fusion(bf16[1,4096,338]{1,2,0:T(8,128)(2,1)} %param.5, s32[]{:T(128)S(6)} %select_n.19, s32[]{:T(128)S(6)} %select_n.17, s32[]{:T(128)S(6)} %select_n.16, s32[]{:T(128)S(6)} %select_n.18), kind=kLoop, calls=%fused_computation.5 | loop fusion | bytes 1343504 | tf_op jit(solution)/shard_map/pole_exchange_first/dynamic_slice | solution.py:220
  1.9 2.1 %collective-permute-start.3 = (bf16[82,1024]{1,0:T(8,128)(2,1)S(1)}, bf16[82,1024]{1,0:T(8,128)(2,1)S(1)}, u32[]{:S(2)}, u32[]{:S(2)}) collective-permute-start(bf16[82,1024]{1,0:T(8,128)(2,1)S(1)} %get-tuple-element.25), channel_id=1, source_target_pairs={{0,64},{64,128},{128,192},{192,0},{1,65},{65,129},{129,193},{193,1... | collective-permute-start | bytes 503816 | tf_op jit(solution)/shard_map/pole_exchange_first/ppermute | solution.py:214
  4.1 1.4 %collective-permute-start.4 = (bf16[82,1024]{1,0:T(8,128)(2,1)}, bf16[82,1024]{1,0:T(8,128)(2,1)S(1)}, u32[]{:S(2)}, u32[]{:S(2)}) collective-permute-start(bf16[82,1024]{1,0:T(8,128)(2,1)} %get-tuple-element.24), channel_id=1, source_target_pairs={{0,192},{64,0},{128,64},{192,128},{1,193},{65,1},{129,65},{193,129... | collective-permute-start | bytes 503816 | tf_op jit(solution)/shard_map/pole_exchange_first/ppermute | solution.py:214
  5.5 1.6 %collective-permute-start.5 = (bf16[82,1024]{1,0:T(8,128)(2,1)S(1)}, bf16[82,1024]{1,0:T(8,128)(2,1)S(1)}, u32[]{:S(2)}, u32[]{:S(2)}) collective-permute-start(bf16[82,1024]{1,0:T(8,128)(2,1)S(1)} %get-tuple-element.26), channel_id=1, source_target_pairs={{0,128},{64,192},{128,0},{192,64},{1,129},{65,193},{129,1},{193,65... | collective-permute-start | bytes 503816 | tf_op jit(solution)/shard_map/pole_exchange_first/ppermute | solution.py:214
  7.1 2.3 %dynamic-slice_bitcast_fusion = (bf16[256,1024]{1,0:T(8,128)(2,1)S(1)}, bf16[256,1024]{1,0:T(8,128)(2,1)S(1)}, bf16[256,1024]{1,0:T(8,128)(2,1)}) fusion(bf16[1,4096,338]{1,2,0:T(8,128)(2,1)} %param.5, s32[]{:T(128)S(6)} %select_n.18, s32[]{:T(128)S(6)} %select_n.17, s32[]{:T(128)S(6)} %select_n.16), kind=kLoop, calls=%fused_computation.2 | loop fusion | bytes 3145740 | tf_op jit(solution)/shard_map/pole_exchange_second/dynamic_slice | solution.py:209
  9.4 0.4 collective-permute-start
  9.8 2.3 %collective-permute-start.1 = (bf16[256,1024]{1,0:T(8,128)(2,1)S(1)}, bf16[256,1024]{1,0:T(8,128)(2,1)S(1)}, u32[]{:S(2)}, u32[]{:S(2)}) collective-permute-start(bf16[256,1024]{1,0:T(8,128)(2,1)S(1)} %get-tuple-element.28), channel_id=1, source_target_pairs={{0,192},{64,0},{128,64},{192,128},{1,193},{65,1},{129,65},{193,129... | collective-permute-start | bytes 1572872 | tf_op jit(solution)/shard_map/pole_exchange_second/ppermute | solution.py:214
  12.1 0.0 copy-done.2
  12.1 0.0 copy-done.3
  12.1 0.7 placement.1
  12.9 0.0 collective-permute-done.3.refs_0_
  12.9 0.2 collective-permute-start.2
  13.1 0.0 collective-permute-done.4.refs_1_
  13.1 1.2 %collective-permute-done.5.refs_2_ = bf16[82,1024]{1,0:T(8,128)(2,1)S(1)} collective-permute-done((bf16[82,1024]{1,0:T(8,128)(2,1)S(1)}, bf16[82,1024]{1,0:T(8,128)(2,1)S(1)}, u32[]{:S(2)}, u32[]{:S(2)}) %collective-permute-start.5) | collective-permute-done | bytes 167968 | tf_op jit(solution)/shard_map/pole_exchange_first/ppermute | solution.py:214
  14.3 2.0 %pack_first.1 = bf16[2048,128]{1,0:T(8,128)(2,1)} custom-call(bf16[2048,1024]{1,0:T(8,128)(2,1)S(1)} %get-tuple-element.15.pick, s32[1,1024]{1,0:T(1,128)S(1)} %get-tuple-element.16.slot_row, bf16[82,1024]{1,0:T(8,128)(2,1)S(1)} %collective-permute-done.3.refs_0_, bf16[82,1024]{1,0:T(8,128)(2,1)S(1)} %collective-permute-done.4.refs_1_, ...), custom_call_target="tpu_custom_call" | custom-call | flops 4294967296 | bytes 33554432 | tf_op jit(solution)/shard_map/pack_first/pallas_call | solution.py:265
  16.3 14.4 %all-to-all-start.1 = ((bf16[64,32,128]{2,1,0:T(8,128)(2,1)}), bf16[64,32,128]{2,1,0:T(8,128)(2,1)S(1)}, u32[]{:S(2)}, u32[]{:S(2)}) async-start(bf16[64,32,128]{2,1,0:T(8,128)(2,1)} %bitcast.21), calls=%async_computation.1 | async-start | bytes 1048576 | tf_op jit(solution)/shard_map/route_first/all_to_all | solution.py:260
  30.7 1.1 constant_dynamic-slice_fusion.refs_3_
  31.8 0.0 collective-permute-done.refs_0_
  31.8 0.0 collective-permute-done.1.refs_1_
  31.8 4.9 %collective-permute-done.2.refs_2_ = bf16[256,1024]{1,0:T(8,128)(2,1)S(1)} collective-permute-done((bf16[256,1024]{1,0:T(8,128)(2,1)S(1)}, bf16[256,1024]{1,0:T(8,128)(2,1)S(1)}, u32[]{:S(2)}, u32[]{:S(2)}) %collective-permute-start.2) | collective-permute-done | bytes 524320 | tf_op jit(solution)/shard_map/pole_exchange_second/ppermute | solution.py:214
  36.8 1.3 %pack_second.1 = (bf16[1024,256]{1,0:T(8,128)(2,1)S(1)}, bf16[1024,256]{1,0:T(8,128)(2,1)S(1)}) custom-call(s32[1]{0:T(128)} %bitcast.core, s32[1,1024]{1,0:T(1,128)S(1)} %get-tuple-element.14.where, bf16[256,1024]{1,0:T(8,128)(2,1)S(1)} %collective-permute-done.refs_0_, bf16[256,1024]{1,0:T(8,128)(2,1)S(1)} %collective-permute-done.1.refs_1_, ...), custom_call_target="tpu_custom_call" | custom-call | flops 107374182400 | bytes 419430400 | tf_op jit(solution)/shard_map/pack_second/pallas_call | solution.py:288
  38.1 1.9 %collective-permute-start.6 = (bf16[1024,256]{1,0:T(8,128)(2,1)S(1)}, bf16[1024,256]{1,0:T(8,128)(2,1)S(1)}, u32[]{:S(2)}, u32[]{:S(2)}) collective-permute-start(bf16[1024,256]{1,0:T(8,128)(2,1)S(1)} %get-tuple-element.19), channel_id=1, source_target_pairs={{0,1},{1,0},{2,3},{3,2},{4,5},{5,4},{6,7},{7,6},{8,9},{9,8},{10,11... | collective-permute-start | bytes 1572872 | tf_op jit(solution)/shard_map/route_second/ppermute | solution.py:297
  39.9 1.5 %collective-permute-done.6 = bf16[1024,256]{1,0:T(8,128)(2,1)S(1)} collective-permute-done((bf16[1024,256]{1,0:T(8,128)(2,1)S(1)}, bf16[1024,256]{1,0:T(8,128)(2,1)S(1)}, u32[]{:S(2)}, u32[]{:S(2)}) %collective-permute-start.6) | collective-permute-done | bytes 524320 | tf_op jit(solution)/shard_map/route_second/ppermute | solution.py:297
  41.5 1.1 pad_maximum_fusion
  42.5 5.9 %all-to-all-done.1 = bf16[64,32,128]{2,1,0:T(8,128)(2,1)S(1)} async-done(((bf16[64,32,128]{2,1,0:T(8,128)(2,1)}), bf16[64,32,128]{2,1,0:T(8,128)(2,1)S(1)}, u32[]{:S(2)}, u32[]{:S(2)}) %all-to-all-start.1) | async-done | bytes 524320 | tf_op jit(solution)/shard_map/route_first/all_to_all | solution.py:260
  48.4 5.3 %all-to-all-start = ((bf16[32,64,256]{2,1,0:T(8,128)(2,1)}), bf16[32,64,256]{2,1,0:T(8,128)(2,1)S(1)}, u32[]{:S(2)}, u32[]{:S(2)}) async-start(bf16[32,64,256]{2,1,0:T(8,128)(2,1)} %pad_maximum_fusion), calls=%async_computation | async-start | bytes 2097152 | tf_op jit(solution)/shard_map/route_second/all_to_all | solution.py:303
  53.7 0.0 copy-start.1
  53.7 4.0 %copy.7.deriv = bf16[1024,1014]{1,0:T(8,128)(2,1)} copy(bf16[1024,1014]{0,1:T(8,128)(2,1)} %param.8) | data formatting | bytes 4153344 | tf_op args[3]
  57.7 4.4 %align_derivatives.1 = (bf16[3,1024,256]{2,1,0:T(8,128)(2,1)}, bf16[3,1024,128]{2,1,0:T(8,128)(2,1)}) custom-call(bf16[1024,1014]{1,0:T(8,128)(2,1)} %copy.7.deriv), custom_call_target="tpu_custom_call" | custom-call | flops 2076672 | bytes 4153344 | tf_op jit(solution)/shard_map/align_derivatives/pallas_call | solution.py:241
  62.1 0.0 copy-done.1
  62.1 0.0 copy-start
  62.1 1.1 %copy-done = bf16[3,1024,128]{2,1,0:T(8,128)(2,1)S(1)} copy-done((bf16[3,1024,128]{2,1,0:T(8,128)(2,1)S(1)}, bf16[3,1024,128]{2,1,0:T(8,128)(2,1)}, u32[]{:S(2)}) %copy-start) | copy-done | bytes 786456
  63.2 2.0 %contract_first.1.info = f32[8,2048]{1,0:T(8,128)S(1)} custom-call(s32[1]{0:T(128)} %bitcast.core, bf16[2048,128]{1,0:T(8,128)(2,1)S(1)} %bitcast.40, bf16[3,1024,128]{2,1,0:T(8,128)(2,1)S(1)} %copy-done, s32[2,1024]{1,0:T(2,128)S(1)} %copy-done.1), custom_call_target="tpu_custom_call" | custom-call | flops 536870912 | bytes 4194304 | tf_op jit(solution)/shard_map/contract_first/pallas_call | solution.py:307
  65.3 14.7 %all-to-all-done = bf16[32,64,256]{2,1,0:T(8,128)(2,1)S(1)} async-done(((bf16[32,64,256]{2,1,0:T(8,128)(2,1)}), bf16[32,64,256]{2,1,0:T(8,128)(2,1)S(1)}, u32[]{:S(2)}, u32[]{:S(2)}) %all-to-all-start) | async-done | bytes 1048608 | tf_op jit(solution)/shard_map/route_second/all_to_all | solution.py:303
  79.9 3.6 %contract_and_scatter.1 = bf16[3,256,128]{2,1,0:T(8,128)(2,1)S(1)} custom-call(bf16[2048,256]{1,0:T(8,128)(2,1)S(1)} %bitcast.39, bf16[3,1024,256]{2,1,0:T(8,128)(2,1)} %get-tuple-element.20.source, f32[8,2048]{1,0:T(8,128)S(1)} %contract_first.1.info), custom_call_target="tpu_custom_call" | custom-call | flops 1073741824 | bytes 4194304 | tf_op jit(solution)/shard_map/contract_and_scatter/pallas_call | solution.py:316
  83.5 0.2 copy.8
  83.7 25.2 %all_to_all.15 = bf16[256,3,128]{2,1,0:T(4,128)(2,1)S(1)} all-to-all(bf16[256,3,128]{2,1,0:T(4,128)(2,1)S(1)} %copy.8), channel_id=1, replica_groups=mesh['pole'=4,'node'=64] {'pole','node'}, dimensions={0} | all-to-all | bytes 393216 | tf_op jit(solution)/shard_map/force_exchange/all_to_all | solution.py:331
  108.9 0.9 convert_reduce_fusion
  (2 shorter events, 0.0 us)
Async XLA Ops:
  0.0 12.1 %copy-start.2 = (s32[4096]{0:T(1024)S(1)}, s32[4096]{0:T(1024)}, u32[]{:S(2)}) copy-start(s32[4096]{0:T(1024)} %param.6) | copy-start | bytes 49156
  0.0 12.1 %copy-start.3 = (s32[4096]{0:T(1024)S(1)}, s32[4096]{0:T(1024)}, u32[]{:S(2)}) copy-start(s32[4096]{0:T(1024)} %param.7) | copy-start | bytes 49156
  1.9 10.9 %collective-permute-start.3 = (bf16[82,1024]{1,0:T(8,128)(2,1)S(1)}, bf16[82,1024]{1,0:T(8,128)(2,1)S(1)}, u32[]{:S(2)}, u32[]{:S(2)}) collective-permute-start(bf16[82,1024]{1,0:T(8,128)(2,1)S(1)} %get-tuple-element.25), channel_id=1, source_target_pairs={{0,64},{64,128},{128,192},{192,0},{1,65},{65,129},{129,193},{193,1... | collective-permute-start | bytes 503816 | tf_op jit(solution)/shard_map/pole_exchange_first/ppermute | solution.py:214
  4.1 9.0 %collective-permute-start.4 = (bf16[82,1024]{1,0:T(8,128)(2,1)}, bf16[82,1024]{1,0:T(8,128)(2,1)S(1)}, u32[]{:S(2)}, u32[]{:S(2)}) collective-permute-start(bf16[82,1024]{1,0:T(8,128)(2,1)} %get-tuple-element.24), channel_id=1, source_target_pairs={{0,192},{64,0},{128,64},{192,128},{1,193},{65,1},{129,65},{193,129... | collective-permute-start | bytes 503816 | tf_op jit(solution)/shard_map/pole_exchange_first/ppermute | solution.py:214
  5.5 8.8 %collective-permute-start.5 = (bf16[82,1024]{1,0:T(8,128)(2,1)S(1)}, bf16[82,1024]{1,0:T(8,128)(2,1)S(1)}, u32[]{:S(2)}, u32[]{:S(2)}) collective-permute-start(bf16[82,1024]{1,0:T(8,128)(2,1)S(1)} %get-tuple-element.26), channel_id=1, source_target_pairs={{0,128},{64,192},{128,0},{192,64},{1,129},{65,193},{129,1},{193,65... | collective-permute-start | bytes 503816 | tf_op jit(solution)/shard_map/pole_exchange_first/ppermute | solution.py:214
  9.4 22.4 %collective-permute-start = (bf16[256,1024]{1,0:T(8,128)(2,1)}, bf16[256,1024]{1,0:T(8,128)(2,1)S(1)}, u32[]{:S(2)}, u32[]{:S(2)}) collective-permute-start(bf16[256,1024]{1,0:T(8,128)(2,1)} %get-tuple-element.29), channel_id=1, source_target_pairs={{0,64},{64,128},{128,192},{192,0},{1,65},{65,129},{129,193},{193,1... | collective-permute-start | bytes 1572872 | tf_op jit(solution)/shard_map/pole_exchange_second/ppermute | solution.py:214
  9.8 22.0 %collective-permute-start.1 = (bf16[256,1024]{1,0:T(8,128)(2,1)S(1)}, bf16[256,1024]{1,0:T(8,128)(2,1)S(1)}, u32[]{:S(2)}, u32[]{:S(2)}) collective-permute-start(bf16[256,1024]{1,0:T(8,128)(2,1)S(1)} %get-tuple-element.28), channel_id=1, source_target_pairs={{0,192},{64,0},{128,64},{192,128},{1,193},{65,1},{129,65},{193,129... | collective-permute-start | bytes 1572872 | tf_op jit(solution)/shard_map/pole_exchange_second/ppermute | solution.py:214
  12.9 23.9 %collective-permute-start.2 = (bf16[256,1024]{1,0:T(8,128)(2,1)S(1)}, bf16[256,1024]{1,0:T(8,128)(2,1)S(1)}, u32[]{:S(2)}, u32[]{:S(2)}) collective-permute-start(bf16[256,1024]{1,0:T(8,128)(2,1)S(1)} %get-tuple-element.27), channel_id=1, source_target_pairs={{0,128},{64,192},{128,0},{192,64},{1,129},{65,193},{129,1},{193,65... | collective-permute-start | bytes 1572872 | tf_op jit(solution)/shard_map/pole_exchange_second/ppermute | solution.py:214
  16.3 32.1 %all-to-all-start.1 = ((bf16[64,32,128]{2,1,0:T(8,128)(2,1)}), bf16[64,32,128]{2,1,0:T(8,128)(2,1)S(1)}, u32[]{:S(2)}, u32[]{:S(2)}) async-start(bf16[64,32,128]{2,1,0:T(8,128)(2,1)} %bitcast.21), calls=%async_computation.1 | async-start | bytes 1048576 | tf_op jit(solution)/shard_map/route_first/all_to_all | solution.py:260
  38.1 3.4 %collective-permute-start.6 = (bf16[1024,256]{1,0:T(8,128)(2,1)S(1)}, bf16[1024,256]{1,0:T(8,128)(2,1)S(1)}, u32[]{:S(2)}, u32[]{:S(2)}) collective-permute-start(bf16[1024,256]{1,0:T(8,128)(2,1)S(1)} %get-tuple-element.19), channel_id=1, source_target_pairs={{0,1},{1,0},{2,3},{3,2},{4,5},{5,4},{6,7},{7,6},{8,9},{9,8},{10,11... | collective-permute-start | bytes 1572872 | tf_op jit(solution)/shard_map/route_second/ppermute | solution.py:297
  48.4 31.5 %all-to-all-start = ((bf16[32,64,256]{2,1,0:T(8,128)(2,1)}), bf16[32,64,256]{2,1,0:T(8,128)(2,1)S(1)}, u32[]{:S(2)}, u32[]{:S(2)}) async-start(bf16[32,64,256]{2,1,0:T(8,128)(2,1)} %pad_maximum_fusion), calls=%async_computation | async-start | bytes 2097152 | tf_op jit(solution)/shard_map/route_second/all_to_all | solution.py:303
  53.7 8.4 %copy-start.1 = (s32[2,1024]{1,0:T(2,128)S(1)}, s32[2,1024]{1,0:T(2,128)}, u32[]{:S(2)}) copy-start(s32[2,1024]{1,0:T(2,128)} %atoms.1) | copy-start | bytes 24580
  62.1 1.1 %copy-start = (bf16[3,1024,128]{2,1,0:T(8,128)(2,1)S(1)}, bf16[3,1024,128]{2,1,0:T(8,128)(2,1)}, u32[]{:S(2)}) copy-start(bf16[3,1024,128]{2,1,0:T(8,128)(2,1)} %get-tuple-element.22.deriv) | copy-start | bytes 2359300

commit v5 on v4

--- a/solution.py
+++ b/solution.py
@@ -36,8 +36,8 @@
     return lax.dot_general(a, b, (((1,), (1,)), ((), ())), preferred_element_type=F32)
 
 
-def plan_kernel(capacity, nodes, pole, node, slot, pick, where, slot_row):
-    slots, blocks = pick.shape
+def plan_kernel(capacity, nodes, pole, node, slot, where, slot_row):
+    blocks = node.shape[1]
     here = pole[0]
     slot_row[...] = slot[pl.ds(here, 1), :]
     row = node[pl.ds(here, 1), :]
@@ -51,9 +51,6 @@
         rank = jnp.sum(same * before, axis=0, keepdims=True).astype(jnp.int32)
         where[:, start : start + tile] = part * capacity + rank
         seen = seen + jnp.sum(same, axis=1, keepdims=True)
-    place = where[...]
-    for start in range(0, slots, tile):
-        pick[start : start + tile, :] = one_hot(place, start, tile)
 
 
 def deriv_kernel(half, deriv, out_second, out_first):
@@ -77,7 +74,7 @@
     return total
 
 
-def pack_first_kernel(pick, slot_row, *refs):
+def pack_first_kernel(where, slot_row, *refs):
     *parts, out, dens, rows, sem = refs
     columns = parts[0].shape[0]
     wide = dens.shape[0]
@@ -89,9 +86,11 @@
     total = dens[...].astype(BF16)
     tile = min(512, rows.shape[0])
     copies = []
+    place = where[...]
     for start in range(0, rows.shape[0], tile):
         part = pl.ds(start, tile)
-        rows[part, :] = rows_times(pick[part, :], total).astype(BF16)
+        picked = one_hot(place, start, tile)
+        rows[part, :] = rows_times(picked, total).astype(BF16)
         copies.append(
             pltpu.make_async_copy(rows.at[part, :], out.at[part, :], sem.at[start // tile])
         )
@@ -203,32 +202,31 @@
     owners = poles * nodes
     partials = dens_part[0].T
 
-    def exchange(first_column, columns):
+    def exchange(first_column, columns, steps):
         def share(which):
             start = lax.rem(pole + which, poles) * blocks
             return lax.dynamic_slice(partials, (first_column, start), (columns, blocks))
 
         parts = []
-        for step in (1, 3, 2):
+        for step in steps:
             pairs = [(k, (k + step) % poles) for k in range(poles)]
             parts.append(lax.ppermute(share(step), "pole", pairs))
         return parts
 
     with jax.named_scope("pole_exchange_first"):
-        parts_first = exchange(split, last)
+        parts_first = exchange(split, last, (2, 1, 3))
         parts_first.append(
             lax.dynamic_slice(partials, (split, pole * blocks), (last, blocks))
         )
     with jax.named_scope("pole_exchange_second"):
-        parts_second = exchange(0, split)
+        parts_second = exchange(0, split, (1, 3, 2))
 
     whole = pl.BlockSpec(memory_space=pltpu.VMEM)
     scalar = pl.BlockSpec(memory_space=pltpu.SMEM)
-    pick_out, place, slot_row = pl.pallas_call(
+    place, slot_row = pl.pallas_call(
         functools.partial(plan_kernel, capacity, nodes),
         in_specs=[scalar, whole, whole],
         out_shape=[
-            jax.ShapeDtypeStruct((slots, blocks), BF16),
             jax.ShapeDtypeStruct((1, blocks), jnp.int32),
             jax.ShapeDtypeStruct((1, blocks), jnp.int32),
         ],
@@ -274,7 +272,7 @@
         compiler_params=params(),
         cost_estimate=cost(16 * slots * blocks * wide, 16 * slots * blocks),
         name="pack_first",
-    )(pick_out, slot_row, *parts_first)
+    )(place, slot_row, *parts_first)
     with jax.named_scope("pole_exchange_second"):
         later, packed_first = lax.optimization_barrier((partials, packed_first))
         parts_second.append(

time: 110 us -> 111 us (level)
  blocking collectives: 25.2 us -> 26.4 us
    all_to_all x1, blocking collectives: 25.2 us -> 26.4 us  [body(): lax.all_to_all(jnp.transpose(partial_forces, (1, 0, 2)), ('pole', 'node')...]
    all_to_all x1, starting transfers between devices: 14.4 us -> 13.2 us  [route(): lax.all_to_all(packed.reshape(nodes, capacity, columns), 'node', 0, 0, ti...]
  transfers between devices with their start and end apart: 9 -> 9, of which waited for: 5 -> 5; matrix products, arithmetic and copies ran while one was open for 8% -> 8% of each run, Pallas kernels for 10% -> 9%
where the time goes in v5:
time: 111 us; the launch traced here: 110 us
  starting transfers between devices  30.1 us (27%)
  waiting for transfers between devices  27.2 us (25%)
  blocking collectives  26.4 us (24%)
  Pallas kernels  13.6 us (12%)
  local copies, waits for them, and re-layouts  10.6 us (10%)
  other arithmetic  1.91 us (2%)
    all_to_all x1, blocking collectives, body(): lax.all_to_all(jnp.transpose(partial_forces, (1, 0, 2)), ('pole', 'node')...  26.4 us
    all_to_all x1, waiting for transfers between devices, body(): lax.all_to_all(both, 'node', 0, 0, axis_index_groups=groups, tiled=True)  14.6 us
    all_to_all x1, starting transfers between devices, route(): lax.all_to_all(packed.reshape(nodes, capacity, columns), 'node', 0, 0, ti...  13.2 us
    ppermute x6, starting transfers between devices, exchange(): parts.append(lax.ppermute(share(step), 'pole', pairs))  9.19 us
    ppermute x6, waiting for transfers between devices, exchange(): parts.append(lax.ppermute(share(step), 'pole', pairs))  5.76 us
    all_to_all x1, waiting for transfers between devices, route(): lax.all_to_all(packed.reshape(nodes, capacity, columns), 'node', 0, 0, ti...  5.36 us
    unnamed x9, local copies, waits for them, and re-layouts  5.11 us
    all_to_all x1, starting transfers between devices, body(): lax.all_to_all(both, 'node', 0, 0, axis_index_groups=groups, tiled=True)  5.01 us
  transfers between devices with their start and end apart: 9, of which 5 were waited for; matrix products, arithmetic and copies ran while one was open for 8% of the time, Pallas kernels for 9%

profile of v5, /device:TPU:1, one launch (start us, length us, event | category | flops | bytes accessed | tf_op | source)
XLA Modules:
  0.0 110.0 jit_solution(7539820778957307096)
XLA Ops:
  0.0 0.0 copy-start.2
  0.0 0.0 copy-start.3
  0.0 1.9 %dynamic-slice_bitcast_fusion.3 = (bf16[82,1024]{1,0:T(8,128)(2,1)S(1)}, bf16[82,1024]{1,0:T(8,128)(2,1)}, bf16[82,1024]{1,0:T(8,128)(2,1)S(1)}, bf16[82,1024]{1,0:T(8,128)(2,1)S(1)}) fusion(bf16[1,4096,338]{1,2,0:T(8,128)(2,1)} %param.5, s32[]{:T(128)S(6)} %select_n.19, s32[]{:T(128)S(6)} %select_n.16, s32[]{:T(128)S(6)} %select_n.18, s32[]{:T(128)S(6)} %select_n.17), kind=kLoop, calls=%fused_computation.5 | loop fusion | bytes 1343504 | tf_op jit(solution)/shard_map/pole_exchange_first/dynamic_slice | solution.py:219
  1.9 3.7 %collective-permute-start.3 = (bf16[82,1024]{1,0:T(8,128)(2,1)S(1)}, bf16[82,1024]{1,0:T(8,128)(2,1)S(1)}, u32[]{:S(2)}, u32[]{:S(2)}) collective-permute-start(bf16[82,1024]{1,0:T(8,128)(2,1)S(1)} %get-tuple-element.23), channel_id=1, source_target_pairs={{0,128},{64,192},{128,0},{192,64},{1,129},{65,193},{129,1},{193,65... | collective-permute-start | bytes 503816 | tf_op jit(solution)/shard_map/pole_exchange_first/ppermute | solution.py:213
  5.7 0.4 collective-permute-start.4
  6.1 2.3 %collective-permute-start.5 = (bf16[82,1024]{1,0:T(8,128)(2,1)S(1)}, bf16[82,1024]{1,0:T(8,128)(2,1)S(1)}, u32[]{:S(2)}, u32[]{:S(2)}) collective-permute-start(bf16[82,1024]{1,0:T(8,128)(2,1)S(1)} %get-tuple-element.24), channel_id=1, source_target_pairs={{0,192},{64,0},{128,64},{192,128},{1,193},{65,1},{129,65},{193,129... | collective-permute-start | bytes 503816 | tf_op jit(solution)/shard_map/pole_exchange_first/ppermute | solution.py:213
  8.4 2.3 %dynamic-slice_bitcast_fusion = (bf16[256,1024]{1,0:T(8,128)(2,1)S(1)}, bf16[256,1024]{1,0:T(8,128)(2,1)S(1)}, bf16[256,1024]{1,0:T(8,128)(2,1)}) fusion(bf16[1,4096,338]{1,2,0:T(8,128)(2,1)} %param.5, s32[]{:T(128)S(6)} %select_n.18, s32[]{:T(128)S(6)} %select_n.17, s32[]{:T(128)S(6)} %select_n.16), kind=kLoop, calls=%fused_computation.2 | loop fusion | bytes 3145740 | tf_op jit(solution)/shard_map/pole_exchange_second/dynamic_slice | solution.py:208
  10.6 0.0 collective-permute-start
  10.6 2.7 %collective-permute-start.1 = (bf16[256,1024]{1,0:T(8,128)(2,1)S(1)}, bf16[256,1024]{1,0:T(8,128)(2,1)S(1)}, u32[]{:S(2)}, u32[]{:S(2)}) collective-permute-start(bf16[256,1024]{1,0:T(8,128)(2,1)S(1)} %get-tuple-element.26), channel_id=1, source_target_pairs={{0,192},{64,0},{128,64},{192,128},{1,193},{65,1},{129,65},{193,129... | collective-permute-start | bytes 1572872 | tf_op jit(solution)/shard_map/pole_exchange_second/ppermute | solution.py:213
  13.3 0.0 copy-done.2
  13.3 0.0 copy-done.3
  13.3 0.2 placement.1
  13.6 0.0 collective-permute-done.3.refs_0_
  13.6 0.1 collective-permute-start.2
  13.7 1.1 %collective-permute-done.4.refs_1_ = bf16[82,1024]{1,0:T(8,128)(2,1)S(1)} collective-permute-done((bf16[82,1024]{1,0:T(8,128)(2,1)}, bf16[82,1024]{1,0:T(8,128)(2,1)S(1)}, u32[]{:S(2)}, u32[]{:S(2)}) %collective-permute-start.4) | collective-permute-done | bytes 167968 | tf_op jit(solution)/shard_map/pole_exchange_first/ppermute | solution.py:213
  14.8 0.0 collective-permute-done.5.refs_2_
  14.8 2.0 %pack_first.1 = bf16[2048,128]{1,0:T(8,128)(2,1)} custom-call(s32[1,1024]{1,0:T(1,128)S(1)} %get-tuple-element.13.where, s32[1,1024]{1,0:T(1,128)S(1)} %get-tuple-element.14.slot_row, bf16[82,1024]{1,0:T(8,128)(2,1)S(1)} %collective-permute-done.3.refs_0_, bf16[82,1024]{1,0:T(8,128)(2,1)S(1)} %collective-permute-done.4.refs_1_, ...), custom_call_target="tpu_custom_call" | custom-call | flops 4294967296 | bytes 33554432 | tf_op jit(solution)/shard_map/pack_first/pallas_call | solution.py:263
  16.9 13.2 %all-to-all-start.1 = ((bf16[64,32,128]{2,1,0:T(8,128)(2,1)}), bf16[64,32,128]{2,1,0:T(8,128)(2,1)S(1)}, u32[]{:S(2)}, u32[]{:S(2)}) async-start(bf16[64,32,128]{2,1,0:T(8,128)(2,1)} %bitcast.21), calls=%async_computation.1 | async-start | bytes 1048576 | tf_op jit(solution)/shard_map/route_first/all_to_all | solution.py:258
  30.1 1.1 constant_dynamic-slice_fusion.refs_3_
  31.2 0.0 collective-permute-done.refs_0_
  31.2 0.0 collective-permute-done.1.refs_1_
  31.2 4.6 %collective-permute-done.2.refs_2_ = bf16[256,1024]{1,0:T(8,128)(2,1)S(1)} collective-permute-done((bf16[256,1024]{1,0:T(8,128)(2,1)S(1)}, bf16[256,1024]{1,0:T(8,128)(2,1)S(1)}, u32[]{:S(2)}, u32[]{:S(2)}) %collective-permute-start.2) | collective-permute-done | bytes 524320 | tf_op jit(solution)/shard_map/pole_exchange_second/ppermute | solution.py:213
  35.8 1.3 %pack_second.1 = (bf16[1024,256]{1,0:T(8,128)(2,1)S(1)}, bf16[1024,256]{1,0:T(8,128)(2,1)S(1)}) custom-call(s32[1]{0:T(128)} %bitcast.core, s32[1,1024]{1,0:T(1,128)S(1)} %get-tuple-element.13.where, bf16[256,1024]{1,0:T(8,128)(2,1)S(1)} %collective-permute-done.refs_0_, bf16[256,1024]{1,0:T(8,128)(2,1)S(1)} %collective-permute-done.1.refs_1_, ...), custom_call_target="tpu_custom_call" | custom-call | flops 107374182400 | bytes 419430400 | tf_op jit(solution)/shard_map/pack_second/pallas_call | solution.py:286
  37.2 2.7 %collective-permute-start.6 = (bf16[1024,256]{1,0:T(8,128)(2,1)S(1)}, bf16[1024,256]{1,0:T(8,128)(2,1)S(1)}, u32[]{:S(2)}, u32[]{:S(2)}) collective-permute-start(bf16[1024,256]{1,0:T(8,128)(2,1)S(1)} %get-tuple-element.17), channel_id=1, source_target_pairs={{0,1},{1,0},{2,3},{3,2},{4,5},{5,4},{6,7},{7,6},{8,9},{9,8},{10,11... | collective-permute-start | bytes 1572872 | tf_op jit(solution)/shard_map/route_second/ppermute | solution.py:295
  39.9 1.5 %collective-permute-done.6 = bf16[1024,256]{1,0:T(8,128)(2,1)S(1)} collective-permute-done((bf16[1024,256]{1,0:T(8,128)(2,1)S(1)}, bf16[1024,256]{1,0:T(8,128)(2,1)S(1)}, u32[]{:S(2)}, u32[]{:S(2)}) %collective-permute-start.6) | collective-permute-done | bytes 524320 | tf_op jit(solution)/shard_map/route_second/ppermute | solution.py:295
  41.4 1.1 pad_maximum_fusion
  42.5 5.4 %all-to-all-done.1 = bf16[64,32,128]{2,1,0:T(8,128)(2,1)S(1)} async-done(((bf16[64,32,128]{2,1,0:T(8,128)(2,1)}), bf16[64,32,128]{2,1,0:T(8,128)(2,1)S(1)}, u32[]{:S(2)}, u32[]{:S(2)}) %all-to-all-start.1) | async-done | bytes 524320 | tf_op jit(solution)/shard_map/route_first/all_to_all | solution.py:258
  47.8 5.0 %all-to-all-start = ((bf16[32,64,256]{2,1,0:T(8,128)(2,1)}), bf16[32,64,256]{2,1,0:T(8,128)(2,1)S(1)}, u32[]{:S(2)}, u32[]{:S(2)}) async-start(bf16[32,64,256]{2,1,0:T(8,128)(2,1)} %pad_maximum_fusion), calls=%async_computation | async-start | bytes 2097152 | tf_op jit(solution)/shard_map/route_second/all_to_all | solution.py:301
  52.9 0.0 copy-start.1
  52.9 4.0 %copy.7.deriv = bf16[1024,1014]{1,0:T(8,128)(2,1)} copy(bf16[1024,1014]{0,1:T(8,128)(2,1)} %param.8) | data formatting | bytes 4153344 | tf_op args[3]
  56.8 4.4 %align_derivatives.1 = (bf16[3,1024,256]{2,1,0:T(8,128)(2,1)}, bf16[3,1024,128]{2,1,0:T(8,128)(2,1)}) custom-call(bf16[1024,1014]{1,0:T(8,128)(2,1)} %copy.7.deriv), custom_call_target="tpu_custom_call" | custom-call | flops 2076672 | bytes 4153344 | tf_op jit(solution)/shard_map/align_derivatives/pallas_call | solution.py:239
  61.2 0.0 copy-done.1
  61.2 0.0 copy-start
  61.2 1.1 %copy-done = bf16[3,1024,128]{2,1,0:T(8,128)(2,1)S(1)} copy-done((bf16[3,1024,128]{2,1,0:T(8,128)(2,1)S(1)}, bf16[3,1024,128]{2,1,0:T(8,128)(2,1)}, u32[]{:S(2)}) %copy-start) | copy-done | bytes 786456
  62.3 2.0 %contract_first.1.info = f32[8,2048]{1,0:T(8,128)S(1)} custom-call(s32[1]{0:T(128)} %bitcast.core, bf16[2048,128]{1,0:T(8,128)(2,1)S(1)} %bitcast.40, bf16[3,1024,128]{2,1,0:T(8,128)(2,1)S(1)} %copy-done, s32[2,1024]{1,0:T(2,128)S(1)} %copy-done.1), custom_call_target="tpu_custom_call" | custom-call | flops 536870912 | bytes 4194304 | tf_op jit(solution)/shard_map/contract_first/pallas_call | solution.py:305
  64.4 14.6 %all-to-all-done = bf16[32,64,256]{2,1,0:T(8,128)(2,1)S(1)} async-done(((bf16[32,64,256]{2,1,0:T(8,128)(2,1)}), bf16[32,64,256]{2,1,0:T(8,128)(2,1)S(1)}, u32[]{:S(2)}, u32[]{:S(2)}) %all-to-all-start) | async-done | bytes 1048608 | tf_op jit(solution)/shard_map/route_second/all_to_all | solution.py:301
  78.9 3.6 %contract_and_scatter.1 = bf16[3,256,128]{2,1,0:T(8,128)(2,1)S(1)} custom-call(bf16[2048,256]{1,0:T(8,128)(2,1)S(1)} %bitcast.39, bf16[3,1024,256]{2,1,0:T(8,128)(2,1)} %get-tuple-element.18.source, f32[8,2048]{1,0:T(8,128)S(1)} %contract_first.1.info), custom_call_target="tpu_custom_call" | custom-call | flops 1073741824 | bytes 4194304 | tf_op jit(solution)/shard_map/contract_and_scatter/pallas_call | solution.py:314
  82.6 0.2 copy.8
  82.7 26.4 %all_to_all.15 = bf16[256,3,128]{2,1,0:T(4,128)(2,1)S(1)} all-to-all(bf16[256,3,128]{2,1,0:T(4,128)(2,1)S(1)} %copy.8), channel_id=1, replica_groups=mesh['pole'=4,'node'=64] {'pole','node'}, dimensions={0} | all-to-all | bytes 393216 | tf_op jit(solution)/shard_map/force_exchange/all_to_all | solution.py:329
  109.2 0.9 convert_reduce_fusion
  (2 shorter events, 0.0 us)
Async XLA Ops:
  0.0 13.3 %copy-start.2 = (s32[4096]{0:T(1024)S(1)}, s32[4096]{0:T(1024)}, u32[]{:S(2)}) copy-start(s32[4096]{0:T(1024)} %param.6) | copy-start | bytes 49156
  0.0 13.3 %copy-start.3 = (s32[4096]{0:T(1024)S(1)}, s32[4096]{0:T(1024)}, u32[]{:S(2)}) copy-start(s32[4096]{0:T(1024)} %param.7) | copy-start | bytes 49156
  1.9 11.7 %collective-permute-start.3 = (bf16[82,1024]{1,0:T(8,128)(2,1)S(1)}, bf16[82,1024]{1,0:T(8,128)(2,1)S(1)}, u32[]{:S(2)}, u32[]{:S(2)}) collective-permute-start(bf16[82,1024]{1,0:T(8,128)(2,1)S(1)} %get-tuple-element.23), channel_id=1, source_target_pairs={{0,128},{64,192},{128,0},{192,64},{1,129},{65,193},{129,1},{193,65... | collective-permute-start | bytes 503816 | tf_op jit(solution)/shard_map/pole_exchange_first/ppermute | solution.py:213
  5.7 9.2 %collective-permute-start.4 = (bf16[82,1024]{1,0:T(8,128)(2,1)}, bf16[82,1024]{1,0:T(8,128)(2,1)S(1)}, u32[]{:S(2)}, u32[]{:S(2)}) collective-permute-start(bf16[82,1024]{1,0:T(8,128)(2,1)} %get-tuple-element.22), channel_id=1, source_target_pairs={{0,64},{64,128},{128,192},{192,0},{1,65},{65,129},{129,193},{193,1... | collective-permute-start | bytes 503816 | tf_op jit(solution)/shard_map/pole_exchange_first/ppermute | solution.py:213
  6.1 8.8 %collective-permute-start.5 = (bf16[82,1024]{1,0:T(8,128)(2,1)S(1)}, bf16[82,1024]{1,0:T(8,128)(2,1)S(1)}, u32[]{:S(2)}, u32[]{:S(2)}) collective-permute-start(bf16[82,1024]{1,0:T(8,128)(2,1)S(1)} %get-tuple-element.24), channel_id=1, source_target_pairs={{0,192},{64,0},{128,64},{192,128},{1,193},{65,1},{129,65},{193,129... | collective-permute-start | bytes 503816 | tf_op jit(solution)/shard_map/pole_exchange_first/ppermute | solution.py:213
  10.6 20.6 %collective-permute-start = (bf16[256,1024]{1,0:T(8,128)(2,1)}, bf16[256,1024]{1,0:T(8,128)(2,1)S(1)}, u32[]{:S(2)}, u32[]{:S(2)}) collective-permute-start(bf16[256,1024]{1,0:T(8,128)(2,1)} %get-tuple-element.27), channel_id=1, source_target_pairs={{0,64},{64,128},{128,192},{192,0},{1,65},{65,129},{129,193},{193,1... | collective-permute-start | bytes 1572872 | tf_op jit(solution)/shard_map/pole_exchange_second/ppermute | solution.py:213
  10.6 20.6 %collective-permute-start.1 = (bf16[256,1024]{1,0:T(8,128)(2,1)S(1)}, bf16[256,1024]{1,0:T(8,128)(2,1)S(1)}, u32[]{:S(2)}, u32[]{:S(2)}) collective-permute-start(bf16[256,1024]{1,0:T(8,128)(2,1)S(1)} %get-tuple-element.26), channel_id=1, source_target_pairs={{0,192},{64,0},{128,64},{192,128},{1,193},{65,1},{129,65},{193,129... | collective-permute-start | bytes 1572872 | tf_op jit(solution)/shard_map/pole_exchange_second/ppermute | solution.py:213
  13.6 22.2 %collective-permute-start.2 = (bf16[256,1024]{1,0:T(8,128)(2,1)S(1)}, bf16[256,1024]{1,0:T(8,128)(2,1)S(1)}, u32[]{:S(2)}, u32[]{:S(2)}) collective-permute-start(bf16[256,1024]{1,0:T(8,128)(2,1)S(1)} %get-tuple-element.25), channel_id=1, source_target_pairs={{0,128},{64,192},{128,0},{192,64},{1,129},{65,193},{129,1},{193,65... | collective-permute-start | bytes 1572872 | tf_op jit(solution)/shard_map/pole_exchange_second/ppermute | solution.py:213
  16.9 31.0 %all-to-all-start.1 = ((bf16[64,32,128]{2,1,0:T(8,128)(2,1)}), bf16[64,32,128]{2,1,0:T(8,128)(2,1)S(1)}, u32[]{:S(2)}, u32[]{:S(2)}) async-start(bf16[64,32,128]{2,1,0:T(8,128)(2,1)} %bitcast.21), calls=%async_computation.1 | async-start | bytes 1048576 | tf_op jit(solution)/shard_map/route_first/all_to_all | solution.py:258
  37.2 4.3 %collective-permute-start.6 = (bf16[1024,256]{1,0:T(8,128)(2,1)S(1)}, bf16[1024,256]{1,0:T(8,128)(2,1)S(1)}, u32[]{:S(2)}, u32[]{:S(2)}) collective-permute-start(bf16[1024,256]{1,0:T(8,128)(2,1)S(1)} %get-tuple-element.17), channel_id=1, source_target_pairs={{0,1},{1,0},{2,3},{3,2},{4,5},{5,4},{6,7},{7,6},{8,9},{9,8},{10,11... | collective-permute-start | bytes 1572872 | tf_op jit(solution)/shard_map/route_second/ppermute | solution.py:295
  47.8 31.1 %all-to-all-start = ((bf16[32,64,256]{2,1,0:T(8,128)(2,1)}), bf16[32,64,256]{2,1,0:T(8,128)(2,1)S(1)}, u32[]{:S(2)}, u32[]{:S(2)}) async-start(bf16[32,64,256]{2,1,0:T(8,128)(2,1)} %pad_maximum_fusion), calls=%async_computation | async-start | bytes 2097152 | tf_op jit(solution)/shard_map/route_second/all_to_all | solution.py:301
  52.9 8.4 %copy-start.1 = (s32[2,1024]{1,0:T(2,128)S(1)}, s32[2,1024]{1,0:T(2,128)}, u32[]{:S(2)}) copy-start(s32[2,1024]{1,0:T(2,128)} %atoms.1) | copy-start | bytes 24580
  61.2 1.1 %copy-start = (bf16[3,1024,128]{2,1,0:T(8,128)(2,1)S(1)}, bf16[3,1024,128]{2,1,0:T(8,128)(2,1)}, u32[]{:S(2)}) copy-start(bf16[3,1024,128]{2,1,0:T(8,128)(2,1)} %get-tuple-element.20.deriv) | copy-start | bytes 2359300

commit v6 on v4

--- a/solution.py
+++ b/solution.py
@@ -87,7 +87,7 @@
     dens[columns : columns + 1, :] = (slot // BASE + 1).astype(F32)
     dens[columns + 1 : columns + 2, :] = (slot % BASE).astype(F32)
     total = dens[...].astype(BF16)
-    tile = min(512, rows.shape[0])
+    tile = min(256, rows.shape[0])
     copies = []
     for start in range(0, rows.shape[0], tile):
         part = pl.ds(start, tile)
@@ -269,7 +269,7 @@
         scratch_shapes=[
             pltpu.VMEM((wide, blocks), F32),
             pltpu.VMEM((slots, wide), BF16),
-            pltpu.SemaphoreType.DMA((max(1, slots // 512),)),
+            pltpu.SemaphoreType.DMA((max(1, slots // 256),)),
         ],
         compiler_params=params(),
         cost_estimate=cost(16 * slots * blocks * wide, 16 * slots * blocks),

time: 110 us -> 110 us (level)
  no operation moved by 1% of the time
where the time goes in v6:
time: 110 us
  starting transfers between devices  29.7 us (27%)
  waiting for transfers between devices  28.2 us (26%)
  blocking collectives  25.2 us (23%)
  Pallas kernels  14.1 us (13%)
  local copies, waits for them, and re-layouts  10.6 us (10%)
  other arithmetic  1.91 us (2%)
    all_to_all x1, blocking collectives, body(): lax.all_to_all(jnp.transpose(partial_forces, (1, 0, 2)), ('pole', 'node')...  25.2 us
    all_to_all x1, waiting for transfers between devices, body(): lax.all_to_all(both, 'node', 0, 0, axis_index_groups=groups, tiled=True)  14.7 us
    all_to_all x1, starting transfers between devices, route(): lax.all_to_all(packed.reshape(nodes, capacity, columns), 'node', 0, 0, ti...  14.4 us
    ppermute x6, starting transfers between devices, exchange(): parts.append(lax.ppermute(share(step), 'pole', pairs))  8.09 us
    ppermute x6, waiting for transfers between devices, exchange(): parts.append(lax.ppermute(share(step), 'pole', pairs))  6.15 us
    all_to_all x1, waiting for transfers between devices, route(): lax.all_to_all(packed.reshape(nodes, capacity, columns), 'node', 0, 0, ti...  5.9 us
    all_to_all x1, starting transfers between devices, body(): lax.all_to_all(both, 'node', 0, 0, axis_index_groups=groups, tiled=True)  5.31 us
    unnamed x9, local copies, waits for them, and re-layouts  5.11 us
  transfers between devices with their start and end apart: 9, of which 5 were waited for; matrix products, arithmetic and copies ran while one was open for 8% of the time, Pallas kernels for 10%

profile of v6, /device:TPU:1, one launch (start us, length us, event | category | flops | bytes accessed | tf_op | source)
XLA Modules:
  0.0 109.7 jit_solution(6721197440183278941)
XLA Ops:
  0.0 0.0 copy-start.2
  0.0 0.0 copy-start.3
  0.0 1.9 %dynamic-slice_bitcast_fusion.3 = (bf16[82,1024]{1,0:T(8,128)(2,1)S(1)}, bf16[82,1024]{1,0:T(8,128)(2,1)}, bf16[82,1024]{1,0:T(8,128)(2,1)S(1)}, bf16[82,1024]{1,0:T(8,128)(2,1)S(1)}) fusion(bf16[1,4096,338]{1,2,0:T(8,128)(2,1)} %param.5, s32[]{:T(128)S(6)} %select_n.19, s32[]{:T(128)S(6)} %select_n.17, s32[]{:T(128)S(6)} %select_n.16, s32[]{:T(128)S(6)} %select_n.18), kind=kLoop, calls=%fused_computation.5 | loop fusion | bytes 1343504 | tf_op jit(solution)/shard_map/pole_exchange_first/dynamic_slice | solution.py:220
  1.9 2.1 %collective-permute-start.3 = (bf16[82,1024]{1,0:T(8,128)(2,1)S(1)}, bf16[82,1024]{1,0:T(8,128)(2,1)S(1)}, u32[]{:S(2)}, u32[]{:S(2)}) collective-permute-start(bf16[82,1024]{1,0:T(8,128)(2,1)S(1)} %get-tuple-element.25), channel_id=1, source_target_pairs={{0,64},{64,128},{128,192},{192,0},{1,65},{65,129},{129,193},{193,1... | collective-permute-start | bytes 503816 | tf_op jit(solution)/shard_map/pole_exchange_first/ppermute | solution.py:214
  4.1 1.4 %collective-permute-start.4 = (bf16[82,1024]{1,0:T(8,128)(2,1)}, bf16[82,1024]{1,0:T(8,128)(2,1)S(1)}, u32[]{:S(2)}, u32[]{:S(2)}) collective-permute-start(bf16[82,1024]{1,0:T(8,128)(2,1)} %get-tuple-element.24), channel_id=1, source_target_pairs={{0,192},{64,0},{128,64},{192,128},{1,193},{65,1},{129,65},{193,129... | collective-permute-start | bytes 503816 | tf_op jit(solution)/shard_map/pole_exchange_first/ppermute | solution.py:214
  5.5 1.6 %collective-permute-start.5 = (bf16[82,1024]{1,0:T(8,128)(2,1)S(1)}, bf16[82,1024]{1,0:T(8,128)(2,1)S(1)}, u32[]{:S(2)}, u32[]{:S(2)}) collective-permute-start(bf16[82,1024]{1,0:T(8,128)(2,1)S(1)} %get-tuple-element.26), channel_id=1, source_target_pairs={{0,128},{64,192},{128,0},{192,64},{1,129},{65,193},{129,1},{193,65... | collective-permute-start | bytes 503816 | tf_op jit(solution)/shard_map/pole_exchange_first/ppermute | solution.py:214
  7.1 2.3 %dynamic-slice_bitcast_fusion = (bf16[256,1024]{1,0:T(8,128)(2,1)S(1)}, bf16[256,1024]{1,0:T(8,128)(2,1)S(1)}, bf16[256,1024]{1,0:T(8,128)(2,1)}) fusion(bf16[1,4096,338]{1,2,0:T(8,128)(2,1)} %param.5, s32[]{:T(128)S(6)} %select_n.18, s32[]{:T(128)S(6)} %select_n.17, s32[]{:T(128)S(6)} %select_n.16), kind=kLoop, calls=%fused_computation.2 | loop fusion | bytes 3145740 | tf_op jit(solution)/shard_map/pole_exchange_second/dynamic_slice | solution.py:209
  9.4 0.4 collective-permute-start
  9.8 2.3 %collective-permute-start.1 = (bf16[256,1024]{1,0:T(8,128)(2,1)S(1)}, bf16[256,1024]{1,0:T(8,128)(2,1)S(1)}, u32[]{:S(2)}, u32[]{:S(2)}) collective-permute-start(bf16[256,1024]{1,0:T(8,128)(2,1)S(1)} %get-tuple-element.28), channel_id=1, source_target_pairs={{0,192},{64,0},{128,64},{192,128},{1,193},{65,1},{129,65},{193,129... | collective-permute-start | bytes 1572872 | tf_op jit(solution)/shard_map/pole_exchange_second/ppermute | solution.py:214
  12.1 0.0 copy-done.2
  12.1 0.0 copy-done.3
  12.1 0.7 placement.1
  12.9 0.0 collective-permute-done.3.refs_0_
  12.9 0.2 collective-permute-start.2
  13.1 0.0 collective-permute-done.4.refs_1_
  13.1 1.2 %collective-permute-done.5.refs_2_ = bf16[82,1024]{1,0:T(8,128)(2,1)S(1)} collective-permute-done((bf16[82,1024]{1,0:T(8,128)(2,1)S(1)}, bf16[82,1024]{1,0:T(8,128)(2,1)S(1)}, u32[]{:S(2)}, u32[]{:S(2)}) %collective-permute-start.5) | collective-permute-done | bytes 167968 | tf_op jit(solution)/shard_map/pole_exchange_first/ppermute | solution.py:214
  14.3 2.0 %pack_first.1 = bf16[2048,128]{1,0:T(8,128)(2,1)} custom-call(bf16[2048,1024]{1,0:T(8,128)(2,1)S(1)} %get-tuple-element.15.pick, s32[1,1024]{1,0:T(1,128)S(1)} %get-tuple-element.16.slot_row, bf16[82,1024]{1,0:T(8,128)(2,1)S(1)} %collective-permute-done.3.refs_0_, bf16[82,1024]{1,0:T(8,128)(2,1)S(1)} %collective-permute-done.4.refs_1_, ...), custom_call_target="tpu_custom_call" | custom-call | flops 4294967296 | bytes 33554432 | tf_op jit(solution)/shard_map/pack_first/pallas_call | solution.py:265
  16.3 14.4 %all-to-all-start.1 = ((bf16[64,32,128]{2,1,0:T(8,128)(2,1)}), bf16[64,32,128]{2,1,0:T(8,128)(2,1)S(1)}, u32[]{:S(2)}, u32[]{:S(2)}) async-start(bf16[64,32,128]{2,1,0:T(8,128)(2,1)} %bitcast.21), calls=%async_computation.1 | async-start | bytes 1048576 | tf_op jit(solution)/shard_map/route_first/all_to_all | solution.py:260
  30.7 1.1 constant_dynamic-slice_fusion.refs_3_
  31.8 0.0 collective-permute-done.refs_0_
  31.8 0.0 collective-permute-done.1.refs_1_
  31.8 4.9 %collective-permute-done.2.refs_2_ = bf16[256,1024]{1,0:T(8,128)(2,1)S(1)} collective-permute-done((bf16[256,1024]{1,0:T(8,128)(2,1)S(1)}, bf16[256,1024]{1,0:T(8,128)(2,1)S(1)}, u32[]{:S(2)}, u32[]{:S(2)}) %collective-permute-start.2) | collective-permute-done | bytes 524320 | tf_op jit(solution)/shard_map/pole_exchange_second/ppermute | solution.py:214
  36.8 1.3 %pack_second.1 = (bf16[1024,256]{1,0:T(8,128)(2,1)S(1)}, bf16[1024,256]{1,0:T(8,128)(2,1)S(1)}) custom-call(s32[1]{0:T(128)} %bitcast.core, s32[1,1024]{1,0:T(1,128)S(1)} %get-tuple-element.14.where, bf16[256,1024]{1,0:T(8,128)(2,1)S(1)} %collective-permute-done.refs_0_, bf16[256,1024]{1,0:T(8,128)(2,1)S(1)} %collective-permute-done.1.refs_1_, ...), custom_call_target="tpu_custom_call" | custom-call | flops 107374182400 | bytes 419430400 | tf_op jit(solution)/shard_map/pack_second/pallas_call | solution.py:288
  38.1 1.9 %collective-permute-start.6 = (bf16[1024,256]{1,0:T(8,128)(2,1)S(1)}, bf16[1024,256]{1,0:T(8,128)(2,1)S(1)}, u32[]{:S(2)}, u32[]{:S(2)}) collective-permute-start(bf16[1024,256]{1,0:T(8,128)(2,1)S(1)} %get-tuple-element.19), channel_id=1, source_target_pairs={{0,1},{1,0},{2,3},{3,2},{4,5},{5,4},{6,7},{7,6},{8,9},{9,8},{10,11... | collective-permute-start | bytes 1572872 | tf_op jit(solution)/shard_map/route_second/ppermute | solution.py:297
  39.9 1.5 %collective-permute-done.6 = bf16[1024,256]{1,0:T(8,128)(2,1)S(1)} collective-permute-done((bf16[1024,256]{1,0:T(8,128)(2,1)S(1)}, bf16[1024,256]{1,0:T(8,128)(2,1)S(1)}, u32[]{:S(2)}, u32[]{:S(2)}) %collective-permute-start.6) | collective-permute-done | bytes 524320 | tf_op jit(solution)/shard_map/route_second/ppermute | solution.py:297
  41.5 1.1 pad_maximum_fusion
  42.5 5.9 %all-to-all-done.1 = bf16[64,32,128]{2,1,0:T(8,128)(2,1)S(1)} async-done(((bf16[64,32,128]{2,1,0:T(8,128)(2,1)}), bf16[64,32,128]{2,1,0:T(8,128)(2,1)S(1)}, u32[]{:S(2)}, u32[]{:S(2)}) %all-to-all-start.1) | async-done | bytes 524320 | tf_op jit(solution)/shard_map/route_first/all_to_all | solution.py:260
  48.4 5.3 %all-to-all-start = ((bf16[32,64,256]{2,1,0:T(8,128)(2,1)}), bf16[32,64,256]{2,1,0:T(8,128)(2,1)S(1)}, u32[]{:S(2)}, u32[]{:S(2)}) async-start(bf16[32,64,256]{2,1,0:T(8,128)(2,1)} %pad_maximum_fusion), calls=%async_computation | async-start | bytes 2097152 | tf_op jit(solution)/shard_map/route_second/all_to_all | solution.py:303
  53.7 0.0 copy-start.1
  53.7 4.0 %copy.7.deriv = bf16[1024,1014]{1,0:T(8,128)(2,1)} copy(bf16[1024,1014]{0,1:T(8,128)(2,1)} %param.8) | data formatting | bytes 4153344 | tf_op args[3]
  57.7 4.4 %align_derivatives.1 = (bf16[3,1024,256]{2,1,0:T(8,128)(2,1)}, bf16[3,1024,128]{2,1,0:T(8,128)(2,1)}) custom-call(bf16[1024,1014]{1,0:T(8,128)(2,1)} %copy.7.deriv), custom_call_target="tpu_custom_call" | custom-call | flops 2076672 | bytes 4153344 | tf_op jit(solution)/shard_map/align_derivatives/pallas_call | solution.py:241
  62.1 0.0 copy-done.1
  62.1 0.0 copy-start
  62.1 1.1 %copy-done = bf16[3,1024,128]{2,1,0:T(8,128)(2,1)S(1)} copy-done((bf16[3,1024,128]{2,1,0:T(8,128)(2,1)S(1)}, bf16[3,1024,128]{2,1,0:T(8,128)(2,1)}, u32[]{:S(2)}) %copy-start) | copy-done | bytes 786456
  63.2 2.0 %contract_first.1.info = f32[8,2048]{1,0:T(8,128)S(1)} custom-call(s32[1]{0:T(128)} %bitcast.core, bf16[2048,128]{1,0:T(8,128)(2,1)S(1)} %bitcast.40, bf16[3,1024,128]{2,1,0:T(8,128)(2,1)S(1)} %copy-done, s32[2,1024]{1,0:T(2,128)S(1)} %copy-done.1), custom_call_target="tpu_custom_call" | custom-call | flops 536870912 | bytes 4194304 | tf_op jit(solution)/shard_map/contract_first/pallas_call | solution.py:307
  65.3 14.7 %all-to-all-done = bf16[32,64,256]{2,1,0:T(8,128)(2,1)S(1)} async-done(((bf16[32,64,256]{2,1,0:T(8,128)(2,1)}), bf16[32,64,256]{2,1,0:T(8,128)(2,1)S(1)}, u32[]{:S(2)}, u32[]{:S(2)}) %all-to-all-start) | async-done | bytes 1048608 | tf_op jit(solution)/shard_map/route_second/all_to_all | solution.py:303
  79.9 3.6 %contract_and_scatter.1 = bf16[3,256,128]{2,1,0:T(8,128)(2,1)S(1)} custom-call(bf16[2048,256]{1,0:T(8,128)(2,1)S(1)} %bitcast.39, bf16[3,1024,256]{2,1,0:T(8,128)(2,1)} %get-tuple-element.20.source, f32[8,2048]{1,0:T(8,128)S(1)} %contract_first.1.info), custom_call_target="tpu_custom_call" | custom-call | flops 1073741824 | bytes 4194304 | tf_op jit(solution)/shard_map/contract_and_scatter/pallas_call | solution.py:316
  83.5 0.2 copy.8
  83.7 25.2 %all_to_all.15 = bf16[256,3,128]{2,1,0:T(4,128)(2,1)S(1)} all-to-all(bf16[256,3,128]{2,1,0:T(4,128)(2,1)S(1)} %copy.8), channel_id=1, replica_groups=mesh['pole'=4,'node'=64] {'pole','node'}, dimensions={0} | all-to-all | bytes 393216 | tf_op jit(solution)/shard_map/force_exchange/all_to_all | solution.py:331
  108.9 0.9 convert_reduce_fusion
  (2 shorter events, 0.0 us)
Async XLA Ops:
  0.0 12.1 %copy-start.2 = (s32[4096]{0:T(1024)S(1)}, s32[4096]{0:T(1024)}, u32[]{:S(2)}) copy-start(s32[4096]{0:T(1024)} %param.6) | copy-start | bytes 49156
  0.0 12.1 %copy-start.3 = (s32[4096]{0:T(1024)S(1)}, s32[4096]{0:T(1024)}, u32[]{:S(2)}) copy-start(s32[4096]{0:T(1024)} %param.7) | copy-start | bytes 49156
  1.9 10.9 %collective-permute-start.3 = (bf16[82,1024]{1,0:T(8,128)(2,1)S(1)}, bf16[82,1024]{1,0:T(8,128)(2,1)S(1)}, u32[]{:S(2)}, u32[]{:S(2)}) collective-permute-start(bf16[82,1024]{1,0:T(8,128)(2,1)S(1)} %get-tuple-element.25), channel_id=1, source_target_pairs={{0,64},{64,128},{128,192},{192,0},{1,65},{65,129},{129,193},{193,1... | collective-permute-start | bytes 503816 | tf_op jit(solution)/shard_map/pole_exchange_first/ppermute | solution.py:214
  4.1 9.0 %collective-permute-start.4 = (bf16[82,1024]{1,0:T(8,128)(2,1)}, bf16[82,1024]{1,0:T(8,128)(2,1)S(1)}, u32[]{:S(2)}, u32[]{:S(2)}) collective-permute-start(bf16[82,1024]{1,0:T(8,128)(2,1)} %get-tuple-element.24), channel_id=1, source_target_pairs={{0,192},{64,0},{128,64},{192,128},{1,193},{65,1},{129,65},{193,129... | collective-permute-start | bytes 503816 | tf_op jit(solution)/shard_map/pole_exchange_first/ppermute | solution.py:214
  5.5 8.8 %collective-permute-start.5 = (bf16[82,1024]{1,0:T(8,128)(2,1)S(1)}, bf16[82,1024]{1,0:T(8,128)(2,1)S(1)}, u32[]{:S(2)}, u32[]{:S(2)}) collective-permute-start(bf16[82,1024]{1,0:T(8,128)(2,1)S(1)} %get-tuple-element.26), channel_id=1, source_target_pairs={{0,128},{64,192},{128,0},{192,64},{1,129},{65,193},{129,1},{193,65... | collective-permute-start | bytes 503816 | tf_op jit(solution)/shard_map/pole_exchange_first/ppermute | solution.py:214
  9.4 22.4 %collective-permute-start = (bf16[256,1024]{1,0:T(8,128)(2,1)}, bf16[256,1024]{1,0:T(8,128)(2,1)S(1)}, u32[]{:S(2)}, u32[]{:S(2)}) collective-permute-start(bf16[256,1024]{1,0:T(8,128)(2,1)} %get-tuple-element.29), channel_id=1, source_target_pairs={{0,64},{64,128},{128,192},{192,0},{1,65},{65,129},{129,193},{193,1... | collective-permute-start | bytes 1572872 | tf_op jit(solution)/shard_map/pole_exchange_second/ppermute | solution.py:214
  9.8 22.0 %collective-permute-start.1 = (bf16[256,1024]{1,0:T(8,128)(2,1)S(1)}, bf16[256,1024]{1,0:T(8,128)(2,1)S(1)}, u32[]{:S(2)}, u32[]{:S(2)}) collective-permute-start(bf16[256,1024]{1,0:T(8,128)(2,1)S(1)} %get-tuple-element.28), channel_id=1, source_target_pairs={{0,192},{64,0},{128,64},{192,128},{1,193},{65,1},{129,65},{193,129... | collective-permute-start | bytes 1572872 | tf_op jit(solution)/shard_map/pole_exchange_second/ppermute | solution.py:214
  12.9 23.9 %collective-permute-start.2 = (bf16[256,1024]{1,0:T(8,128)(2,1)S(1)}, bf16[256,1024]{1,0:T(8,128)(2,1)S(1)}, u32[]{:S(2)}, u32[]{:S(2)}) collective-permute-start(bf16[256,1024]{1,0:T(8,128)(2,1)S(1)} %get-tuple-element.27), channel_id=1, source_target_pairs={{0,128},{64,192},{128,0},{192,64},{1,129},{65,193},{129,1},{193,65... | collective-permute-start | bytes 1572872 | tf_op jit(solution)/shard_map/pole_exchange_second/ppermute | solution.py:214
  16.3 32.1 %all-to-all-start.1 = ((bf16[64,32,128]{2,1,0:T(8,128)(2,1)}), bf16[64,32,128]{2,1,0:T(8,128)(2,1)S(1)}, u32[]{:S(2)}, u32[]{:S(2)}) async-start(bf16[64,32,128]{2,1,0:T(8,128)(2,1)} %bitcast.21), calls=%async_computation.1 | async-start | bytes 1048576 | tf_op jit(solution)/shard_map/route_first/all_to_all | solution.py:260
  38.1 3.4 %collective-permute-start.6 = (bf16[1024,256]{1,0:T(8,128)(2,1)S(1)}, bf16[1024,256]{1,0:T(8,128)(2,1)S(1)}, u32[]{:S(2)}, u32[]{:S(2)}) collective-permute-start(bf16[1024,256]{1,0:T(8,128)(2,1)S(1)} %get-tuple-element.19), channel_id=1, source_target_pairs={{0,1},{1,0},{2,3},{3,2},{4,5},{5,4},{6,7},{7,6},{8,9},{9,8},{10,11... | collective-permute-start | bytes 1572872 | tf_op jit(solution)/shard_map/route_second/ppermute | solution.py:297
  48.4 31.5 %all-to-all-start = ((bf16[32,64,256]{2,1,0:T(8,128)(2,1)}), bf16[32,64,256]{2,1,0:T(8,128)(2,1)S(1)}, u32[]{:S(2)}, u32[]{:S(2)}) async-start(bf16[32,64,256]{2,1,0:T(8,128)(2,1)} %pad_maximum_fusion), calls=%async_computation | async-start | bytes 2097152 | tf_op jit(solution)/shard_map/route_second/all_to_all | solution.py:303
  53.7 8.4 %copy-start.1 = (s32[2,1024]{1,0:T(2,128)S(1)}, s32[2,1024]{1,0:T(2,128)}, u32[]{:S(2)}) copy-start(s32[2,1024]{1,0:T(2,128)} %atoms.1) | copy-start | bytes 24580
  62.1 1.1 %copy-start = (bf16[3,1024,128]{2,1,0:T(8,128)(2,1)S(1)}, bf16[3,1024,128]{2,1,0:T(8,128)(2,1)}, u32[]{:S(2)}) copy-start(bf16[3,1024,128]{2,1,0:T(8,128)(2,1)} %get-tuple-element.22.deriv) | copy-start | bytes 2359300

commit v7 on v5

--- a/solution.py
+++ b/solution.py
@@ -84,7 +84,7 @@
     dens[columns : columns + 1, :] = (slot // BASE + 1).astype(F32)
     dens[columns + 1 : columns + 2, :] = (slot % BASE).astype(F32)
     total = dens[...].astype(BF16)
-    tile = min(512, rows.shape[0])
+    tile = min(256, rows.shape[0])
     copies = []
     place = where[...]
     for start in range(0, rows.shape[0], tile):
@@ -267,7 +267,7 @@
         scratch_shapes=[
             pltpu.VMEM((wide, blocks), F32),
             pltpu.VMEM((slots, wide), BF16),
-            pltpu.SemaphoreType.DMA((max(1, slots // 512),)),
+            pltpu.SemaphoreType.DMA((max(1, slots // 256),)),
         ],
         compiler_params=params(),
         cost_estimate=cost(16 * slots * blocks * wide, 16 * slots * blocks),

time: 111 us -> 111 us (level)
  no operation moved by 1% of the time
where the time goes in v7:
time: 111 us; the launch traced here: 110 us
  starting transfers between devices  30.2 us (27%)
  waiting for transfers between devices  27.2 us (25%)
  blocking collectives  26.4 us (24%)
  Pallas kernels  13.6 us (12%)
  local copies, waits for them, and re-layouts  10.6 us (10%)
  other arithmetic  1.91 us (2%)
    all_to_all x1, blocking collectives, body(): lax.all_to_all(jnp.transpose(partial_forces, (1, 0, 2)), ('pole', 'node')...  26.4 us
    all_to_all x1, waiting for transfers between devices, body(): lax.all_to_all(both, 'node', 0, 0, axis_index_groups=groups, tiled=True)  14.6 us
    all_to_all x1, starting transfers between devices, route(): lax.all_to_all(packed.reshape(nodes, capacity, columns), 'node', 0, 0, ti...  13.2 us
    ppermute x6, starting transfers between devices, exchange(): parts.append(lax.ppermute(share(step), 'pole', pairs))  9.19 us
    ppermute x6, waiting for transfers between devices, exchange(): parts.append(lax.ppermute(share(step), 'pole', pairs))  5.78 us
    all_to_all x1, waiting for transfers between devices, route(): lax.all_to_all(packed.reshape(nodes, capacity, columns), 'node', 0, 0, ti...  5.35 us
    unnamed x9, local copies, waits for them, and re-layouts  5.11 us
    all_to_all x1, starting transfers between devices, body(): lax.all_to_all(both, 'node', 0, 0, axis_index_groups=groups, tiled=True)  5.02 us
  transfers between devices with their start and end apart: 9, of which 5 were waited for; matrix products, arithmetic and copies ran while one was open for 8% of the time, Pallas kernels for 9%

profile of v7, /device:TPU:1, one launch (start us, length us, event | category | flops | bytes accessed | tf_op | source)
XLA Modules:
  0.0 110.0 jit_solution(12179744510975893630)
XLA Ops:
  0.0 0.0 copy-start.2
  0.0 0.0 copy-start.3
  0.0 1.9 %dynamic-slice_bitcast_fusion.3 = (bf16[82,1024]{1,0:T(8,128)(2,1)S(1)}, bf16[82,1024]{1,0:T(8,128)(2,1)}, bf16[82,1024]{1,0:T(8,128)(2,1)S(1)}, bf16[82,1024]{1,0:T(8,128)(2,1)S(1)}) fusion(bf16[1,4096,338]{1,2,0:T(8,128)(2,1)} %param.5, s32[]{:T(128)S(6)} %select_n.19, s32[]{:T(128)S(6)} %select_n.16, s32[]{:T(128)S(6)} %select_n.18, s32[]{:T(128)S(6)} %select_n.17), kind=kLoop, calls=%fused_computation.5 | loop fusion | bytes 1343504 | tf_op jit(solution)/shard_map/pole_exchange_first/dynamic_slice | solution.py:219
  1.9 3.7 %collective-permute-start.3 = (bf16[82,1024]{1,0:T(8,128)(2,1)S(1)}, bf16[82,1024]{1,0:T(8,128)(2,1)S(1)}, u32[]{:S(2)}, u32[]{:S(2)}) collective-permute-start(bf16[82,1024]{1,0:T(8,128)(2,1)S(1)} %get-tuple-element.23), channel_id=1, source_target_pairs={{0,128},{64,192},{128,0},{192,64},{1,129},{65,193},{129,1},{193,65... | collective-permute-start | bytes 503816 | tf_op jit(solution)/shard_map/pole_exchange_first/ppermute | solution.py:213
  5.7 0.4 collective-permute-start.4
  6.1 2.3 %collective-permute-start.5 = (bf16[82,1024]{1,0:T(8,128)(2,1)S(1)}, bf16[82,1024]{1,0:T(8,128)(2,1)S(1)}, u32[]{:S(2)}, u32[]{:S(2)}) collective-permute-start(bf16[82,1024]{1,0:T(8,128)(2,1)S(1)} %get-tuple-element.24), channel_id=1, source_target_pairs={{0,192},{64,0},{128,64},{192,128},{1,193},{65,1},{129,65},{193,129... | collective-permute-start | bytes 503816 | tf_op jit(solution)/shard_map/pole_exchange_first/ppermute | solution.py:213
  8.4 2.3 %dynamic-slice_bitcast_fusion = (bf16[256,1024]{1,0:T(8,128)(2,1)S(1)}, bf16[256,1024]{1,0:T(8,128)(2,1)S(1)}, bf16[256,1024]{1,0:T(8,128)(2,1)}) fusion(bf16[1,4096,338]{1,2,0:T(8,128)(2,1)} %param.5, s32[]{:T(128)S(6)} %select_n.18, s32[]{:T(128)S(6)} %select_n.17, s32[]{:T(128)S(6)} %select_n.16), kind=kLoop, calls=%fused_computation.2 | loop fusion | bytes 3145740 | tf_op jit(solution)/shard_map/pole_exchange_second/dynamic_slice | solution.py:208
  10.6 0.0 collective-permute-start
  10.6 2.7 %collective-permute-start.1 = (bf16[256,1024]{1,0:T(8,128)(2,1)S(1)}, bf16[256,1024]{1,0:T(8,128)(2,1)S(1)}, u32[]{:S(2)}, u32[]{:S(2)}) collective-permute-start(bf16[256,1024]{1,0:T(8,128)(2,1)S(1)} %get-tuple-element.26), channel_id=1, source_target_pairs={{0,192},{64,0},{128,64},{192,128},{1,193},{65,1},{129,65},{193,129... | collective-permute-start | bytes 1572872 | tf_op jit(solution)/shard_map/pole_exchange_second/ppermute | solution.py:213
  13.3 0.0 copy-done.2
  13.3 0.0 copy-done.3
  13.3 0.2 placement.1
  13.6 0.0 collective-permute-done.3.refs_0_
  13.6 0.1 collective-permute-start.2
  13.7 1.1 %collective-permute-done.4.refs_1_ = bf16[82,1024]{1,0:T(8,128)(2,1)S(1)} collective-permute-done((bf16[82,1024]{1,0:T(8,128)(2,1)}, bf16[82,1024]{1,0:T(8,128)(2,1)S(1)}, u32[]{:S(2)}, u32[]{:S(2)}) %collective-permute-start.4) | collective-permute-done | bytes 167968 | tf_op jit(solution)/shard_map/pole_exchange_first/ppermute | solution.py:213
  14.8 0.0 collective-permute-done.5.refs_2_
  14.8 2.0 %pack_first.1 = bf16[2048,128]{1,0:T(8,128)(2,1)} custom-call(s32[1,1024]{1,0:T(1,128)S(1)} %get-tuple-element.13.where, s32[1,1024]{1,0:T(1,128)S(1)} %get-tuple-element.14.slot_row, bf16[82,1024]{1,0:T(8,128)(2,1)S(1)} %collective-permute-done.3.refs_0_, bf16[82,1024]{1,0:T(8,128)(2,1)S(1)} %collective-permute-done.4.refs_1_, ...), custom_call_target="tpu_custom_call" | custom-call | flops 4294967296 | bytes 33554432 | tf_op jit(solution)/shard_map/pack_first/pallas_call | solution.py:263
  16.9 13.2 %all-to-all-start.1 = ((bf16[64,32,128]{2,1,0:T(8,128)(2,1)}), bf16[64,32,128]{2,1,0:T(8,128)(2,1)S(1)}, u32[]{:S(2)}, u32[]{:S(2)}) async-start(bf16[64,32,128]{2,1,0:T(8,128)(2,1)} %bitcast.21), calls=%async_computation.1 | async-start | bytes 1048576 | tf_op jit(solution)/shard_map/route_first/all_to_all | solution.py:258
  30.1 1.1 constant_dynamic-slice_fusion.refs_3_
  31.2 0.0 collective-permute-done.refs_0_
  31.2 0.0 collective-permute-done.1.refs_1_
  31.2 4.6 %collective-permute-done.2.refs_2_ = bf16[256,1024]{1,0:T(8,128)(2,1)S(1)} collective-permute-done((bf16[256,1024]{1,0:T(8,128)(2,1)S(1)}, bf16[256,1024]{1,0:T(8,128)(2,1)S(1)}, u32[]{:S(2)}, u32[]{:S(2)}) %collective-permute-start.2) | collective-permute-done | bytes 524320 | tf_op jit(solution)/shard_map/pole_exchange_second/ppermute | solution.py:213
  35.8 1.3 %pack_second.1 = (bf16[1024,256]{1,0:T(8,128)(2,1)S(1)}, bf16[1024,256]{1,0:T(8,128)(2,1)S(1)}) custom-call(s32[1]{0:T(128)} %bitcast.core, s32[1,1024]{1,0:T(1,128)S(1)} %get-tuple-element.13.where, bf16[256,1024]{1,0:T(8,128)(2,1)S(1)} %collective-permute-done.refs_0_, bf16[256,1024]{1,0:T(8,128)(2,1)S(1)} %collective-permute-done.1.refs_1_, ...), custom_call_target="tpu_custom_call" | custom-call | flops 107374182400 | bytes 419430400 | tf_op jit(solution)/shard_map/pack_second/pallas_call | solution.py:286
  37.2 2.7 %collective-permute-start.6 = (bf16[1024,256]{1,0:T(8,128)(2,1)S(1)}, bf16[1024,256]{1,0:T(8,128)(2,1)S(1)}, u32[]{:S(2)}, u32[]{:S(2)}) collective-permute-start(bf16[1024,256]{1,0:T(8,128)(2,1)S(1)} %get-tuple-element.17), channel_id=1, source_target_pairs={{0,1},{1,0},{2,3},{3,2},{4,5},{5,4},{6,7},{7,6},{8,9},{9,8},{10,11... | collective-permute-start | bytes 1572872 | tf_op jit(solution)/shard_map/route_second/ppermute | solution.py:295
  39.9 1.5 %collective-permute-done.6 = bf16[1024,256]{1,0:T(8,128)(2,1)S(1)} collective-permute-done((bf16[1024,256]{1,0:T(8,128)(2,1)S(1)}, bf16[1024,256]{1,0:T(8,128)(2,1)S(1)}, u32[]{:S(2)}, u32[]{:S(2)}) %collective-permute-start.6) | collective-permute-done | bytes 524320 | tf_op jit(solution)/shard_map/route_second/ppermute | solution.py:295
  41.4 1.1 pad_maximum_fusion
  42.5 5.4 %all-to-all-done.1 = bf16[64,32,128]{2,1,0:T(8,128)(2,1)S(1)} async-done(((bf16[64,32,128]{2,1,0:T(8,128)(2,1)}), bf16[64,32,128]{2,1,0:T(8,128)(2,1)S(1)}, u32[]{:S(2)}, u32[]{:S(2)}) %all-to-all-start.1) | async-done | bytes 524320 | tf_op jit(solution)/shard_map/route_first/all_to_all | solution.py:258
  47.8 5.0 %all-to-all-start = ((bf16[32,64,256]{2,1,0:T(8,128)(2,1)}), bf16[32,64,256]{2,1,0:T(8,128)(2,1)S(1)}, u32[]{:S(2)}, u32[]{:S(2)}) async-start(bf16[32,64,256]{2,1,0:T(8,128)(2,1)} %pad_maximum_fusion), calls=%async_computation | async-start | bytes 2097152 | tf_op jit(solution)/shard_map/route_second/all_to_all | solution.py:301
  52.9 0.0 copy-start.1
  52.9 4.0 %copy.7.deriv = bf16[1024,1014]{1,0:T(8,128)(2,1)} copy(bf16[1024,1014]{0,1:T(8,128)(2,1)} %param.8) | data formatting | bytes 4153344 | tf_op args[3]
  56.8 4.4 %align_derivatives.1 = (bf16[3,1024,256]{2,1,0:T(8,128)(2,1)}, bf16[3,1024,128]{2,1,0:T(8,128)(2,1)}) custom-call(bf16[1024,1014]{1,0:T(8,128)(2,1)} %copy.7.deriv), custom_call_target="tpu_custom_call" | custom-call | flops 2076672 | bytes 4153344 | tf_op jit(solution)/shard_map/align_derivatives/pallas_call | solution.py:239
  61.2 0.0 copy-done.1
  61.2 0.0 copy-start
  61.2 1.1 %copy-done = bf16[3,1024,128]{2,1,0:T(8,128)(2,1)S(1)} copy-done((bf16[3,1024,128]{2,1,0:T(8,128)(2,1)S(1)}, bf16[3,1024,128]{2,1,0:T(8,128)(2,1)}, u32[]{:S(2)}) %copy-start) | copy-done | bytes 786456
  62.3 2.0 %contract_first.1.info = f32[8,2048]{1,0:T(8,128)S(1)} custom-call(s32[1]{0:T(128)} %bitcast.core, bf16[2048,128]{1,0:T(8,128)(2,1)S(1)} %bitcast.40, bf16[3,1024,128]{2,1,0:T(8,128)(2,1)S(1)} %copy-done, s32[2,1024]{1,0:T(2,128)S(1)} %copy-done.1), custom_call_target="tpu_custom_call" | custom-call | flops 536870912 | bytes 4194304 | tf_op jit(solution)/shard_map/contract_first/pallas_call | solution.py:305
  64.4 14.6 %all-to-all-done = bf16[32,64,256]{2,1,0:T(8,128)(2,1)S(1)} async-done(((bf16[32,64,256]{2,1,0:T(8,128)(2,1)}), bf16[32,64,256]{2,1,0:T(8,128)(2,1)S(1)}, u32[]{:S(2)}, u32[]{:S(2)}) %all-to-all-start) | async-done | bytes 1048608 | tf_op jit(solution)/shard_map/route_second/all_to_all | solution.py:301
  79.0 3.6 %contract_and_scatter.1 = bf16[3,256,128]{2,1,0:T(8,128)(2,1)S(1)} custom-call(bf16[2048,256]{1,0:T(8,128)(2,1)S(1)} %bitcast.39, bf16[3,1024,256]{2,1,0:T(8,128)(2,1)} %get-tuple-element.18.source, f32[8,2048]{1,0:T(8,128)S(1)} %contract_first.1.info), custom_call_target="tpu_custom_call" | custom-call | flops 1073741824 | bytes 4194304 | tf_op jit(solution)/shard_map/contract_and_scatter/pallas_call | solution.py:314
  82.6 0.2 copy.8
  82.8 26.4 %all_to_all.15 = bf16[256,3,128]{2,1,0:T(4,128)(2,1)S(1)} all-to-all(bf16[256,3,128]{2,1,0:T(4,128)(2,1)S(1)} %copy.8), channel_id=1, replica_groups=mesh['pole'=4,'node'=64] {'pole','node'}, dimensions={0} | all-to-all | bytes 393216 | tf_op jit(solution)/shard_map/force_exchange/all_to_all | solution.py:329
  109.2 0.9 convert_reduce_fusion
  (2 shorter events, 0.0 us)
Async XLA Ops:
  0.0 13.3 %copy-start.2 = (s32[4096]{0:T(1024)S(1)}, s32[4096]{0:T(1024)}, u32[]{:S(2)}) copy-start(s32[4096]{0:T(1024)} %param.6) | copy-start | bytes 49156
  0.0 13.3 %copy-start.3 = (s32[4096]{0:T(1024)S(1)}, s32[4096]{0:T(1024)}, u32[]{:S(2)}) copy-start(s32[4096]{0:T(1024)} %param.7) | copy-start | bytes 49156
  1.9 11.7 %collective-permute-start.3 = (bf16[82,1024]{1,0:T(8,128)(2,1)S(1)}, bf16[82,1024]{1,0:T(8,128)(2,1)S(1)}, u32[]{:S(2)}, u32[]{:S(2)}) collective-permute-start(bf16[82,1024]{1,0:T(8,128)(2,1)S(1)} %get-tuple-element.23), channel_id=1, source_target_pairs={{0,128},{64,192},{128,0},{192,64},{1,129},{65,193},{129,1},{193,65... | collective-permute-start | bytes 503816 | tf_op jit(solution)/shard_map/pole_exchange_first/ppermute | solution.py:213
  5.7 9.2 %collective-permute-start.4 = (bf16[82,1024]{1,0:T(8,128)(2,1)}, bf16[82,1024]{1,0:T(8,128)(2,1)S(1)}, u32[]{:S(2)}, u32[]{:S(2)}) collective-permute-start(bf16[82,1024]{1,0:T(8,128)(2,1)} %get-tuple-element.22), channel_id=1, source_target_pairs={{0,64},{64,128},{128,192},{192,0},{1,65},{65,129},{129,193},{193,1... | collective-permute-start | bytes 503816 | tf_op jit(solution)/shard_map/pole_exchange_first/ppermute | solution.py:213
  6.1 8.8 %collective-permute-start.5 = (bf16[82,1024]{1,0:T(8,128)(2,1)S(1)}, bf16[82,1024]{1,0:T(8,128)(2,1)S(1)}, u32[]{:S(2)}, u32[]{:S(2)}) collective-permute-start(bf16[82,1024]{1,0:T(8,128)(2,1)S(1)} %get-tuple-element.24), channel_id=1, source_target_pairs={{0,192},{64,0},{128,64},{192,128},{1,193},{65,1},{129,65},{193,129... | collective-permute-start | bytes 503816 | tf_op jit(solution)/shard_map/pole_exchange_first/ppermute | solution.py:213
  10.6 20.6 %collective-permute-start = (bf16[256,1024]{1,0:T(8,128)(2,1)}, bf16[256,1024]{1,0:T(8,128)(2,1)S(1)}, u32[]{:S(2)}, u32[]{:S(2)}) collective-permute-start(bf16[256,1024]{1,0:T(8,128)(2,1)} %get-tuple-element.27), channel_id=1, source_target_pairs={{0,64},{64,128},{128,192},{192,0},{1,65},{65,129},{129,193},{193,1... | collective-permute-start | bytes 1572872 | tf_op jit(solution)/shard_map/pole_exchange_second/ppermute | solution.py:213
  10.6 20.6 %collective-permute-start.1 = (bf16[256,1024]{1,0:T(8,128)(2,1)S(1)}, bf16[256,1024]{1,0:T(8,128)(2,1)S(1)}, u32[]{:S(2)}, u32[]{:S(2)}) collective-permute-start(bf16[256,1024]{1,0:T(8,128)(2,1)S(1)} %get-tuple-element.26), channel_id=1, source_target_pairs={{0,192},{64,0},{128,64},{192,128},{1,193},{65,1},{129,65},{193,129... | collective-permute-start | bytes 1572872 | tf_op jit(solution)/shard_map/pole_exchange_second/ppermute | solution.py:213
  13.6 22.2 %collective-permute-start.2 = (bf16[256,1024]{1,0:T(8,128)(2,1)S(1)}, bf16[256,1024]{1,0:T(8,128)(2,1)S(1)}, u32[]{:S(2)}, u32[]{:S(2)}) collective-permute-start(bf16[256,1024]{1,0:T(8,128)(2,1)S(1)} %get-tuple-element.25), channel_id=1, source_target_pairs={{0,128},{64,192},{128,0},{192,64},{1,129},{65,193},{129,1},{193,65... | collective-permute-start | bytes 1572872 | tf_op jit(solution)/shard_map/pole_exchange_second/ppermute | solution.py:213
  16.9 31.0 %all-to-all-start.1 = ((bf16[64,32,128]{2,1,0:T(8,128)(2,1)}), bf16[64,32,128]{2,1,0:T(8,128)(2,1)S(1)}, u32[]{:S(2)}, u32[]{:S(2)}) async-start(bf16[64,32,128]{2,1,0:T(8,128)(2,1)} %bitcast.21), calls=%async_computation.1 | async-start | bytes 1048576 | tf_op jit(solution)/shard_map/route_first/all_to_all | solution.py:258
  37.2 4.3 %collective-permute-start.6 = (bf16[1024,256]{1,0:T(8,128)(2,1)S(1)}, bf16[1024,256]{1,0:T(8,128)(2,1)S(1)}, u32[]{:S(2)}, u32[]{:S(2)}) collective-permute-start(bf16[1024,256]{1,0:T(8,128)(2,1)S(1)} %get-tuple-element.17), channel_id=1, source_target_pairs={{0,1},{1,0},{2,3},{3,2},{4,5},{5,4},{6,7},{7,6},{8,9},{9,8},{10,11... | collective-permute-start | bytes 1572872 | tf_op jit(solution)/shard_map/route_second/ppermute | solution.py:295
  47.8 31.1 %all-to-all-start = ((bf16[32,64,256]{2,1,0:T(8,128)(2,1)}), bf16[32,64,256]{2,1,0:T(8,128)(2,1)S(1)}, u32[]{:S(2)}, u32[]{:S(2)}) async-start(bf16[32,64,256]{2,1,0:T(8,128)(2,1)} %pad_maximum_fusion), calls=%async_computation | async-start | bytes 2097152 | tf_op jit(solution)/shard_map/route_second/all_to_all | solution.py:301
  52.9 8.4 %copy-start.1 = (s32[2,1024]{1,0:T(2,128)S(1)}, s32[2,1024]{1,0:T(2,128)}, u32[]{:S(2)}) copy-start(s32[2,1024]{1,0:T(2,128)} %atoms.1) | copy-start | bytes 24580
  61.2 1.1 %copy-start = (bf16[3,1024,128]{2,1,0:T(8,128)(2,1)S(1)}, bf16[3,1024,128]{2,1,0:T(8,128)(2,1)}, u32[]{:S(2)}) copy-start(bf16[3,1024,128]{2,1,0:T(8,128)(2,1)} %get-tuple-element.20.deriv) | copy-start | bytes 2359300
